TPU v7x, 32 devices: a whole 2x2x4 slice. The times are simulated.
32 devices in a mesh: seq: 4 (over y, x), chan: 8 (over z, core).
Axes of the slice: x: 2, y: 2, z: 4, core: 2. Of those that a mesh axis runs over, the one named last changes fastest.
Arguments:
- hidden: bfloat16 [2, 8192, 2048], P(None, ('seq', 'chan')), may hold values from -6 to 6
- out_grad: bfloat16 [2, 8192, 2048], P(None, ('seq', 'chan')), may hold values from -6 to 6
- modality: int32 [2, 8192], P(None, 'seq'), may hold values from 0 to 2, as said below
- lengths: int32 [2, 4, 5], P(None, 'seq'), may hold values from 1 to 1024, as said below
- in_weight: bfloat16 [3, 2048, 2, 4096], P(None, 'seq', None, 'chan'), may hold values from -0.125 to 0.125
- x_weight: bfloat16 [3, 4096, 160], P(None, 'chan', 'seq'), may hold values from -0.09375 to 0.09375
- dt_weight: bfloat16 [3, 128, 4096], P(None, 'seq', 'chan'), may hold values from -0.5 to 0.5
- out_weight: bfloat16 [3, 4096, 2048], P(None, 'chan', 'seq'), may hold values from -0.375 to 0.375
- conv_weight: float32 [4, 4096], P(None, 'chan'), may hold values from -3 to 3
- conv_bias: float32 [4096], P('chan'), may hold values from -4 to 4
- a_log: float32 [16, 4096], P(None, 'chan'), may hold values from 0 to 2.7
- d_skip: float32 [4096], P('chan'), may hold values from 0.5 to 1.5
- dt_bias: float32 [4096], P('chan'), may hold values from -4.5 to -2
- norm_gain: float32 [2048], P('chan'), may hold values from 0.5 to 1.5
Outputs:
- out: bfloat16 [2, 8192, 2048], P(None, ('seq', 'chan'))
- hidden_grad: float32 [2, 8192, 2048], P(None, ('seq', 'chan'))
- in_weight_grad: float32 [3, 2048, 2, 4096], P(None, 'seq', None, 'chan')
- x_weight_grad: float32 [3, 4096, 160], P(None, 'chan', 'seq')
- dt_weight_grad: float32 [3, 128, 4096], P(None, 'seq', 'chan')
- out_weight_grad: float32 [3, 4096, 2048], P(None, 'chan', 'seq')
- conv_weight_grad: float32 [4, 4096], P(None, 'chan')
- conv_bias_grad: float32 [4096], P('chan')
- a_log_grad: float32 [16, 4096], P(None, 'chan')
- d_skip_grad: float32 [4096], P('chan')
- dt_bias_grad: float32 [4096], P('chan')
- norm_gain_grad: float32 [2048], P('chan')
Inputs may be any that keep to these rules, and one draw needn't show every extreme that they name: Each group's entries are 4 sequence lengths in token order and then the padding at the group's end; they sum to 2048; the longest sequence has exactly 1024 tokens and the padding at most 128. `modality`: constant over aligned runs of 1024 tokens.
All inputs are finite; a program needn't handle non-finite values.
Results may differ from a plain program's by a relative error of at most 0.011.
Values may be sent and summed in bfloat16 or wider, within the bound.
A program may use at most 1 GiB of HBM per device.

v0:
```python
import functools

import jax
import jax.numpy as jnp
from jax import lax
from jax.experimental import pallas as pl
from jax.experimental.pallas import tpu as pltpu
from jax.sharding import PartitionSpec as P

MODES = 3
MBLK = 1024
LOG2E = 1.4426950408889634
RESET = 1.0e4
CHUNKS = 8
UNROLL = 4

f32, bf16 = jnp.float32, jnp.bfloat16
HBM = pl.BlockSpec(memory_space=pl.ANY)
VMEM = pl.BlockSpec(memory_space=pltpu.VMEM)


def sds(shape, dtype):
    return jax.ShapeDtypeStruct(shape, dtype)


def cost(flops, nbytes, trans=0):
    return pl.CostEstimate(flops=int(flops), bytes_accessed=int(nbytes), transcendentals=int(trans))


def dsilu(value):
    sig = jax.nn.sigmoid(value)
    return sig * (1.0 + value * (1.0 - sig))


def gmm_kernel(trans, kinds, x, w, out):
    dims = (((1,), (1,)), ((), ())) if trans else (((1,), (0,)), ((), ()))
    out[...] = lax.dot_general(x[...], w[0], dims, preferred_element_type=f32).astype(out.dtype)


def gmm(kinds, x, w, trans, dtype, name, rb=512, cb=512):
    T, K = x.shape
    C = w.shape[1] if trans else w.shape[2]
    cb = min(cb, C)
    per = MBLK // rb
    wspec = (
        pl.BlockSpec((1, cb, K), lambda t, c, r, kinds: (kinds[t], c, 0))
        if trans
        else pl.BlockSpec((1, K, cb), lambda t, c, r, kinds: (kinds[t], 0, c))
    )
    return pl.pallas_call(
        functools.partial(gmm_kernel, trans),
        grid_spec=pltpu.PrefetchScalarGridSpec(
            num_scalar_prefetch=1,
            grid=(T // MBLK, C // cb, per),
            in_specs=[pl.BlockSpec((rb, K), lambda t, c, r, kinds: (t * per + r, 0)), wspec],
            out_specs=pl.BlockSpec((rb, cb), lambda t, c, r, kinds: (t * per + r, c)),
        ),
        out_shape=sds((T, C), dtype),
        compiler_params=pltpu.CompilerParams(vmem_limit_bytes=40 << 20),
        cost_estimate=cost(2 * T * K * C, 2 * T * K + 4 * K * C + 4 * T * C),
        name=name,
    )(kinds, x, w)


def wgrad_kernel(nm, plan, *refs):
    acc = refs[-1]
    out = refs[-2]
    step = pl.program_id(1)

    @pl.when(plan[2, step] == 0)
    def _():
        acc[...] = jnp.zeros_like(acc)

    for i in range(nm):

        @pl.when(plan[2, step] == i + 1)
        def _():
            acc[...] += lax.dot_general(
                refs[2 * i][...], refs[2 * i + 1][...], (((0,), (0,)), ((), ())), preferred_element_type=f32
            )

    out[0] = acc[...].astype(out.dtype)


def wgrad_plan(kinds):
    nm, nt = kinds.shape
    flat = kinds.reshape(-1)
    n = nm * nt
    ids = jnp.arange(n)
    modes = jnp.arange(MODES)
    first = jnp.min(jnp.where(flat[None, :] == modes[:, None], ids[None, :], n), axis=1)
    first = jnp.where(first == n, 0, first)
    key = jnp.concatenate([modes * (n + 1), flat * (n + 1) + 1 + ids])
    mode = jnp.concatenate([modes, flat])
    tile = jnp.concatenate([first, ids])
    live = jnp.concatenate([jnp.zeros((MODES,), jnp.int32), ids // nt + 1])
    rank = jnp.sum((key[None, :] < key[:, None]).astype(jnp.int32), axis=1)
    place = (rank[None, :] == jnp.arange(MODES + n)[:, None]).astype(jnp.int32)

    def order(v):
        return jnp.sum(place * v[None, :], axis=1)

    rows = [order(mode), order(tile), order(live)]
    for i in range(nm):
        rows.append(jnp.clip(order(tile) - i * nt, 0, nt - 1))
    return jnp.stack(rows).astype(jnp.int32)


def wgrad(plan, lefts, rights, name, db):
    nm = len(lefts)
    D, C = lefts[0].shape[1], rights[0].shape[1]
    specs, args = [], []
    for i in range(nm):
        specs.append(pl.BlockSpec((MBLK, db), lambda d, s, plan, i=i: (plan[3 + i, s], d)))
        specs.append(pl.BlockSpec((MBLK, C), lambda d, s, plan, i=i: (plan[3 + i, s], 0)))
        args += [lefts[i], rights[i]]
    T = nm * lefts[0].shape[0]
    return pl.pallas_call(
        functools.partial(wgrad_kernel, nm),
        grid_spec=pltpu.PrefetchScalarGridSpec(
            num_scalar_prefetch=1,
            grid=(D // db, plan.shape[1]),
            in_specs=specs,
            out_specs=pl.BlockSpec((1, db, C), lambda d, s, plan: (plan[0, s], d, 0)),
            scratch_shapes=[pltpu.VMEM((db, C), f32)],
        ),
        out_shape=sds((MODES, D, C), bf16),
        compiler_params=pltpu.CompilerParams(vmem_limit_bytes=48 << 20),
        cost_estimate=cost(2 * T * D * C, 2 * T * (D + C * (D // db)) + 2 * MODES * D * C),
        name=name,
    )(plan, *args)


def chain(ends, total, back):
    row = lax.broadcasted_iota(jnp.int32, ends.shape, 0)
    for k in (1, 2, 4):
        shift = CHUNKS - k if back else k
        ok = (row < CHUNKS - k) if back else (row >= k)
        ends = ends + total * jnp.where(ok, pltpu.roll(ends, shift, 0), 0.0)
        total = total * jnp.where(ok, pltpu.roll(total, shift, 0), 1.0)
    shift = CHUNKS - 1 if back else 1
    ok = (row < CHUNKS - 1) if back else (row >= 1)
    return jnp.where(ok, pltpu.roll(ends, shift, 0), 0.0)


def scan_kernel(
    S, NG, ddec_h, dx_h, ds_h, bc, rate2, rate, y_h, gb_h, fr_h, db, dc, drate,
    ddec, dx, ds, y, gb, fr, p_scr, bb, cb, q, sems
):
    NN, L = rate.shape
    KT = L // 128
    copies = []
    for a, (src, dst) in enumerate(((ddec_h, ddec), (dx_h, dx), (ds_h, ds))):
        for c in range(CHUNKS):
            copies.append(
                pltpu.make_async_copy(src.at[pl.ds(c * S, S), :], dst.at[:, c, :], sems.at[a, c])
            )
    for cp in copies:
        cp.start()
    db[...] = jnp.zeros_like(db)
    dc[...] = jnp.zeros_like(dc)
    y[...] = jnp.zeros_like(y)
    gb[...] = jnp.zeros_like(gb)
    fr[...] = jnp.zeros_like(fr)
    for cp in copies:
        cp.wait()

    def rows(s):
        return pl.ds(pl.multiple_of(s * 8, 8), 8)

    def wide(v):
        return jnp.concatenate([v] * KT, axis=1)

    def fold(v):
        return sum(v[:, 128 * i : 128 * i + 128] for i in range(KT))

    def loop(body, init):
        def outer(k, carry):
            for u in range(UNROLL):
                carry = body(k * UNROLL + u, carry)
            return carry

        return lax.fori_loop(0, S // UNROLL, outer, init)

    dsum = lax.fori_loop(0, S, lambda s, a: a + ddec[s], jnp.zeros((8, L), f32))

    def group(g, _):
        kk = lax.broadcasted_iota(jnp.int32, (2 * NN, NG * 128), 0)
        ln = lax.broadcasted_iota(jnp.int32, (2 * NN, NG * 128), 1) // 128
        Xb = jnp.where(kk == g * NG + ln, 1.0, 0.0).astype(bf16)
        Xc = jnp.where(kk == NN + g * NG + ln, 1.0, 0.0).astype(bf16)
        rr = lax.broadcasted_iota(jnp.int32, (NG * 128, 128), 0) // 128
        cc = lax.broadcasted_iota(jnp.int32, (NG * 128, 128), 1)
        R = jnp.where(cc == rr + g * NG, 1.0, 0.0).astype(bf16)

        def expand(i, _):
            at = pl.ds(pl.multiple_of(i * 256, 256), 256)
            v = bc[at, :]
            hi = v.astype(bf16)
            lo = (v - hi.astype(f32)).astype(bf16)
            for X, o in ((Xb, bb), (Xc, cb)):
                o[at, :] = jnp.dot(hi, X, preferred_element_type=f32) + jnp.dot(
                    lo, X, preferred_element_type=f32
                )
            return 0

        lax.fori_loop(0, S * 8 // 256, expand, 0)

        def reduce(out):
            def body(i, _):
                at = pl.ds(pl.multiple_of(i * 256, 256), 256)
                out[at, :] += jnp.dot(q[at, :].astype(bf16), R, preferred_element_type=f32)
                return 0

            lax.fori_loop(0, S * 8 // 256, body, 0)

        r2 = [jnp.broadcast_to(rate2[pl.ds(g * NG + n, 1), :], (8, L)) for n in range(NG)]
        rt = [jnp.broadcast_to(rate[pl.ds(g * NG + n, 1), :], (8, L)) for n in range(NG)]
        total = [jnp.exp2(dsum * r2[n]) for n in range(NG)]
        zero = tuple(jnp.zeros((8, L), f32) for _ in range(NG))
        cols = [slice(128 * n, 128 * n + 128) for n in range(NG)]

        def ahead(s, st):
            d, x, b = ddec[s], dx[s], bb[rows(s), :]
            return tuple(
                jnp.exp2(d * r2[n]) * st[n] + x * wide(b[:, cols[n]]) for n in range(NG)
            )

        st = loop(ahead, zero)
        st = tuple(chain(st[n], total[n], False) for n in range(NG))

        def forward(s, st):
            d, x, b, c, dst = ddec[s], dx[s], bb[rows(s), :], cb[rows(s), :], ds[s]
            acc, new = y[s], []
            for n in range(NG):
                p = jnp.exp2(d * r2[n]) * st[n]
                p_scr[s, n] = p
                h = p + x * wide(b[:, cols[n]])
                acc = acc + wide(c[:, cols[n]]) * h
                q[rows(s), cols[n]] = fold(dst * h)
                new.append(h)
            y[s] = acc
            return tuple(new)

        loop(forward, st)
        reduce(dc)

        def behind(k, A):
            s = S - 1 - k
            d, c, dst = ddec[s], cb[rows(s), :], ds[s]
            return tuple(
                jnp.exp2(d * r2[n]) * (dst * wide(c[:, cols[n]]) + A[n]) for n in range(NG)
            )

        A = loop(behind, zero)
        A = tuple(chain(A[n], total[n], True) for n in range(NG))

        def backward(k, carry):
            A, dr = carry
            s = S - 1 - k
            d, x, b, c, dst = ddec[s], dx[s], bb[rows(s), :], cb[rows(s), :], ds[s]
            ga, fa, nA, ndr = gb[s], fr[s], [], []
            for n in range(NG):
                G = dst * wide(c[:, cols[n]]) + A[n]
                nA.append(jnp.exp2(d * r2[n]) * G)
                flow = G * p_scr[s, n]
                ndr.append(dr[n] + flow * d)
                fa = fa + flow * rt[n]
                ga = ga + G * wide(b[:, cols[n]])
                q[rows(s), cols[n]] = fold(G * x)
            gb[s] = ga
            fr[s] = fa
            return tuple(nA), tuple(ndr)

        A, dr = loop(backward, (A, zero))
        reduce(db)
        for n in range(NG):
            drate[pl.ds(g * NG + n, 1), :] = jnp.sum(dr[n], axis=0, keepdims=True)
        return 0

    lax.fori_loop(0, NN // NG, group, 0)
    copies = []
    for a, (src, dst) in enumerate(((y, y_h), (gb, gb_h), (fr, fr_h))):
        for c in range(CHUNKS):
            copies.append(
                pltpu.make_async_copy(src.at[:, c, :], dst.at[pl.ds(c * S, S), :], sems.at[a, c])
            )
    for cp in copies:
        cp.start()
    for cp in copies:
        cp.wait()


def scan_both(ddec, dx, ds, bc, rate, NG=4):
    T, E = ddec.shape
    N = rate.shape[0]
    S = T // CHUNKS
    act = pltpu.VMEM((S, CHUNKS, E), f32)
    return pl.pallas_call(
        functools.partial(scan_kernel, S, NG),
        in_specs=[HBM] * 3 + [VMEM] * 3,
        out_specs=[HBM] * 3 + [VMEM] * 3,
        out_shape=[sds((T, E), f32)] * 3 + [sds((T, 128), f32)] * 2 + [sds((N, E), f32)],
        scratch_shapes=[act] * 6
        + [pltpu.VMEM((S, NG, CHUNKS, E), f32)]
        + [pltpu.VMEM((T, NG * 128), f32)] * 3
        + [pltpu.SemaphoreType.DMA((3, CHUNKS))],
        compiler_params=pltpu.CompilerParams(vmem_limit_bytes=60 << 20),
        cost_estimate=cost(60 * T * E * N, 24 * T * E, 4 * T * E * N),
        name="scan_both",
    )(ddec, dx, ds, bc, rate * LOG2E, rate)


def inter(v):
    return v.reshape((CHUNKS, v.shape[0] // CHUNKS) + v.shape[1:]).swapaxes(0, 1).reshape(v.shape)


def natural(v):
    return v.reshape((v.shape[0] // CHUNKS, CHUNKS) + v.shape[1:]).swapaxes(0, 1).reshape(v.shape)


def token_layout(lens, count):
    places = jnp.arange(count)
    begins = jnp.zeros_like(places)
    end = jnp.int32(0)
    for k in range(lens.shape[0]):
        start_of_padding = end
        end = end + lens[k]
        begins = begins + jnp.where(end <= places, lens[k], 0)
    return places - begins, (places < start_of_padding).astype(f32)


def lagged(values, lag):
    if lag == 0:
        return values
    return jnp.concatenate(
        [jnp.zeros((lag,) + values.shape[1:], values.dtype), values[: values.shape[0] - lag]], axis=0
    )


def leading(values, lag):
    if lag == 0:
        return values
    return jnp.concatenate(
        [values[lag:], jnp.zeros((lag,) + values.shape[1:], values.dtype)], axis=0
    )


def shards(
    hidden, out_grad, modality, lengths, in_weight, x_weight, dt_weight, out_weight,
    conv_weight, conv_bias, a_log, d_skip, dt_bias, norm_gain
):
    micro, rows, width = hidden.shape
    group = modality.shape[1]
    inner = conv_bias.shape[0]
    nstate = a_log.shape[0]
    taps = conv_weight.shape[0]
    kinds_all = modality[:, ::MBLK]
    plan = wgrad_plan(kinds_all)
    gain = lax.all_gather(norm_gain, "chan", axis=0, tiled=True)
    rate = -jnp.exp(a_log)
    x_small = jnp.swapaxes(x_weight, 1, 2)
    cols = x_small.shape[1]
    small = lax.all_gather(
        jnp.concatenate([x_small, dt_weight], axis=1), "seq", axis=0, tiled=False
    )
    small = jnp.swapaxes(small, 0, 1)
    x_full = small[:, :, :cols].reshape(MODES, -1, inner)
    dt_full = small[:, :, cols:].reshape(MODES, -1, inner)
    rank = dt_full.shape[1]
    scales, units, normed, gathered, ups = [], [], [], [], []
    for i in range(micro):
        source = hidden[i].astype(f32)
        scale = lax.rsqrt(jnp.mean(source * source, axis=1, keepdims=True) + 1e-05)
        unit = source * scale
        normed.append((unit * gain[None, :]).astype(bf16))
        scales.append(scale)
        units.append(unit)
    in_full = lax.all_gather(
        in_weight.reshape(MODES, -1, 2 * inner), "seq", axis=1, tiled=True
    )
    out_full = lax.all_gather(out_weight, "seq", axis=2, tiled=True)
    for i in range(micro):
        gathered.append(lax.all_gather(normed[i], "chan", axis=0, tiled=True))
        ups.append(lax.all_gather(out_grad[i], "chan", axis=0, tiled=True))
    outputs, input_grads, ys, d_mixes, xcs, d_projs, lows, d_pres = [], [], [], [], [], [], [], []
    sums = []
    g_gain = jnp.zeros((width,), f32)
    for i in range(micro):
        kinds = kinds_all[i]
        position, valid = token_layout(lengths[i, 0], group)
        keep = (position > 0)[:, None]
        valid = valid[:, None]
        reach = [(position >= lag).astype(f32)[:, None] for lag in range(taps)]
        mixed = gmm(kinds, gathered[i], in_full, False, f32, "in_proj")
        x_in, gate_in = mixed[:, :inner], mixed[:, inner:]
        conv = jnp.zeros_like(x_in) + conv_bias[None, :]
        for lag in range(taps):
            conv = conv + conv_weight[lag][None, :] * lagged(x_in, lag) * reach[lag]
        xc = jax.nn.silu(conv).astype(bf16)
        xc_f = xc.astype(f32)
        proj = lax.psum(gmm(kinds, xc, x_full, True, f32, "x_proj"), "chan")
        dt_low = proj[:, :rank].astype(bf16)
        bc = proj[:, rank:]
        dt_pre = gmm(kinds, dt_low, dt_full, False, f32, "dt_proj") + dt_bias[None, :]
        delta = jax.nn.softplus(dt_pre)
        d_y = gmm(kinds, ups[i], out_full, True, f32, "out_dgrad")
        gate = jax.nn.silu(gate_in)
        d_state = d_y * gate * valid
        dx = delta * xc_f
        ddec = jnp.where(keep, delta, RESET)
        s_y, s_gb, s_fr, s_b, s_c, s_rate = scan_both(ddec, dx, d_state, inter(bc), rate)
        scanned = s_y + d_skip[None, :] * xc_f
        y_out = (scanned * gate * valid).astype(bf16)
        branch = lax.psum_scatter(
            gmm(kinds, y_out, out_full, False, bf16, "out_proj"),
            "chan", scatter_dimension=0, tiled=True,
        )
        outputs.append((hidden[i].astype(f32) + branch.astype(f32)).astype(bf16))
        d_gate = (d_y * scanned * valid * dsilu(gate_in)).astype(bf16)
        d_delta = xc_f * s_gb + s_fr
        d_pre = (d_delta * jax.nn.sigmoid(dt_pre)).astype(bf16)
        d_low = gmm(kinds, d_pre, dt_full, True, f32, "dt_dgrad")
        d_bc = natural(jnp.concatenate([s_b[:, :nstate], s_c[:, :nstate]], axis=1))
        d_proj = lax.psum(jnp.concatenate([d_low, d_bc], axis=1), "chan").astype(bf16)
        d_xc = (
            d_state * d_skip[None, :]
            + delta * s_gb
            + gmm(kinds, d_proj, x_full, False, f32, "x_dgrad")
        )
        d_conv = d_xc * dsilu(conv)
        d_in = jnp.zeros_like(d_conv)
        conv_rows = []
        for lag in range(taps):
            masked = d_conv * reach[lag]
            conv_rows.append(jnp.sum(masked * lagged(x_in, lag), axis=0))
            d_in = d_in + conv_weight[lag][None, :] * leading(masked, lag)
        d_mixed = jnp.concatenate([d_in.astype(bf16), d_gate], axis=1)
        d_normed = lax.psum_scatter(
            gmm(kinds, d_mixed, in_full, True, bf16, "in_dgrad"),
            "chan", scatter_dimension=0, tiled=True,
        ).astype(f32)
        g_gain = g_gain + jnp.sum(d_normed * units[i], axis=0)
        d_unit = d_normed * gain[None, :]
        input_grads.append(
            scales[i] * (d_unit - units[i] * jnp.mean(d_unit * units[i], axis=1, keepdims=True))
            + out_grad[i].astype(f32)
        )
        ys.append(y_out)
        d_mixes.append(d_mixed)
        xcs.append(xc)
        d_projs.append(d_proj)
        lows.append(dt_low)
        d_pres.append(d_pre)
        sums.append(
            (
                jnp.stack(conv_rows, axis=0),
                jnp.sum(d_conv, axis=0),
                s_rate * rate,
                jnp.sum(d_state * xc_f, axis=0),
                jnp.sum(d_pre.astype(f32), axis=0),
            )
        )
    g_out = wgrad(plan, ys, ups, "out_wgrad", 256)
    g_dt = wgrad(plan, lows, d_pres, "dt_wgrad", 128)
    g_x = wgrad(plan, d_projs, xcs, "x_wgrad", d_projs[0].shape[1])
    g_in = wgrad(plan, gathered, d_mixes, "in_wgrad", 256)
    g_out = lax.psum_scatter(g_out, "seq", scatter_dimension=2, tiled=True)
    g_x = lax.psum_scatter(g_x, "seq", scatter_dimension=1, tiled=True)
    g_dt = lax.psum_scatter(g_dt, "seq", scatter_dimension=1, tiled=True)
    g_in = lax.psum_scatter(g_in, "seq", scatter_dimension=1, tiled=True)
    gain_part = lax.psum_scatter(g_gain, "chan", scatter_dimension=0, tiled=True)
    total = [sum(s[j] for s in sums) for j in range(5)]
    conv_total, bias_total, rate_total, skip_total, dtb_total, gain_total = lax.psum(
        (*total, gain_part), "seq"
    )
    return (
        jnp.stack(outputs, axis=0),
        jnp.stack(input_grads, axis=0),
        g_in.astype(f32).reshape(in_weight.shape),
        jnp.swapaxes(g_x.astype(f32), 1, 2),
        g_dt.astype(f32),
        g_out.astype(f32),
        conv_total,
        bias_total,
        rate_total,
        skip_total,
        dtb_total,
        gain_total,
    )


def solution(mesh):
    act = P(None, ("seq", "chan"), None)
    weights = (P(None, "seq", None, "chan"), P(None, "chan", "seq"), P(None, "seq", "chan"), P(None, "chan", "seq"))
    vectors = (P(None, "chan"), P("chan"), P(None, "chan"), P("chan"), P("chan"), P("chan"))
    return jax.shard_map(
        shards,
        mesh=mesh,
        in_specs=(act, act, P(None, "seq"), P(None, "seq", None), *weights, *vectors),
        out_specs=(act, act, *weights, *vectors),
        check_vma=False,
    )
```

profile of v0, /device:TPU:0, one launch (start us, length us, event | category | flops | bytes accessed | tf_op | source)
XLA Modules:
  0.0 1731.7 jit_solution(4772951378980994873)
XLA Ops:
  11.9 13.4 all-gather.3
  28.0 6.1 reshape.232
  34.8 15.6 all-gather
  71.0 14.7 all-gather.15.cloned.1.call-done.w
  85.6 83.7 %all-gather.21.cloned.1.call-done = bf16[1,2048,2048]{2,1,0:T(8,128)(2,1)} async-done(((bf16[1,256,2048]{2,1,0:T(8,128)(2,1)}), bf16[1,2048,2048]{2,1,0:T(8,128)(2,1)}) %all-gather.21.cloned.1.call-update) | async-done | bytes 8388624 | tf_op jit(solution)/shard_map/all_gather | solution.py:385
  172.1 8.0 out_dgrad.3
  182.2 70.0 %all-gather.19.cloned.1.call-done = bf16[1,2048,2048]{2,1,0:T(8,128)(2,1)} async-done(((bf16[1,256,2048]{2,1,0:T(8,128)(2,1)}), bf16[1,2048,2048]{2,1,0:T(8,128)(2,1)}) %all-gather.19.cloned.1.call-update) | async-done | bytes 8388624 | tf_op jit(solution)/shard_map/all_gather | solution.py:385
  255.0 8.0 out_dgrad.2
  265.0 69.8 %all-gather.17.cloned.1.call-done.x.refs_2_ = bf16[2048,2048]{1,0:T(8,128)(2,1)} async-done(((bf16[256,2048]{1,0:T(8,128)(2,1)}), bf16[2048,2048]{1,0:T(8,128)(2,1)}) %all-gather.17.cloned.1.call-update) | async-done | bytes 8388624 | tf_op jit(solution)/shard_map/all_gather | solution.py:384
  334.8 123.3 %all-gather.13.cloned.1.call-done.w = bf16[3,2048,1024]{2,1,0:T(8,128)(2,1)} async-done(((bf16[3,512,1024]{2,1,0:T(8,128)(2,1)}), bf16[3,2048,1024]{2,1,0:T(8,128)(2,1)}) %all-gather.13.cloned.1.call-update) | async-done | bytes 12582928 | tf_op jit(solution)/shard_map/all_gather | solution.py:379
  458.2 16.6 in_proj.3
  483.3 59.0 %all-gather.11.cloned.1.call-done.x.refs_0_ = bf16[2048,2048]{1,0:T(8,128)(2,1)} async-done(((bf16[256,2048]{1,0:T(8,128)(2,1)}), bf16[2048,2048]{1,0:T(8,128)(2,1)}) %all-gather.11.cloned.1.call-update) | async-done | bytes 8388624 | tf_op jit(solution)/shard_map/all_gather | solution.py:384
  542.3 16.1 in_proj.2
  571.5 10.8 fusion.9
  585.6 11.2 fusion.4
  601.9 3.6 broadcast_compare_fusion
  605.5 3.6 broadcast_compare_fusion.1
  609.8 87.1 %all-reduce.24.cloned.1.call-done = (f32[2048,160]{1,0:T(8,128)}, f32[2048,160]{1,0:T(8,128)}) async-done(((f32[2048,160]{1,0:T(8,128)}, f32[2048,160]{1,0:T(8,128)}), (f32[2048,160]{1,0:T(8,128)}, f32[2048,160]{1,0:T(8,128)})) %all-reduce.24.cloned.1.call-update) | async-done | bytes 2621456 | tf_op jit(solution)/shard_map/psum | solution.py:402
  705.5 4.7 convert_multiply_fusion.7
  710.2 120.8 %scan_both.2 = (f32[2048,512]{1,0:T(8,128)}, f32[2048,512]{1,0:T(8,128)}, f32[2048,512]{1,0:T(8,128)}, f32[2048,128]{1,0:T(8,128)}, f32[2048,128]{1,0:T(8,128)}, /*index=5*/f32[16,512]{1,0:T(8,128)}) custom-call(f32[2048,512]{1,0:T(8,128)} %get-tuple-element.98.ddec_h, f32[2048,512]{1,0:T(8,128)} %get-tuple-element.97.dx_h, ...), custom_call_target="tpu_custom_call" | custom-call | flops 1006632960 | bytes 25165824 | tf_op jit(solution)/shard_map/scan_both/pallas_call | solution.py:299
  835.8 9.7 convert_reduce_fusion.1
  850.4 121.0 %scan_both.3 = (f32[2048,512]{1,0:T(8,128)}, f32[2048,512]{1,0:T(8,128)}, f32[2048,512]{1,0:T(8,128)}, f32[2048,128]{1,0:T(8,128)}, f32[2048,128]{1,0:T(8,128)}, /*index=5*/f32[16,512]{1,0:T(8,128)}) custom-call(f32[2048,512]{1,0:T(8,128)} %get-tuple-element.123.ddec_h, f32[2048,512]{1,0:T(8,128)} %get-tuple-element.124.dx_h, ...), custom_call_target="tpu_custom_call" | custom-call | flops 1006632960 | bytes 25165824 | tf_op jit(solution)/shard_map/scan_both/pallas_call | solution.py:299
  971.4 6.1 convert_reduce_fusion
  981.8 88.9 %all-reduce.25 = (bf16[2048,160]{1,0:T(8,128)(2,1)}, bf16[2048,160]{1,0:T(8,128)(2,1)}) all-reduce(f32[2048,160]{1,0:T(8,128)} %pad_maximum_fusion.5, f32[2048,160]{1,0:T(8,128)} %pad_maximum_fusion.4), channel_id=1, replica_groups=mesh['seq'=4,'chan'=8] {'chan'}, use_global_device_ids=true, to_apply=%region_9.10 | all-reduce | flops 655360 | bytes 3932160 | tf_op jit(solution)/shard_map/psum | solution.py:425
  1073.1 5.4 x_wgrad.1
  1088.2 4.1 dt_wgrad.1
  1092.4 20.0 %fusion.43 = (f32[512]{0:T(512)S(1)}, f32[512]{0:T(512)S(1)}, f32[2048,512]{1,0:T(8,128)}, bf16[2048,512]{1,0:T(8,128)(2,1)}, bf16[2048,512]{1,0:T(8,128)(2,1)}) fusion(f32[2048,1024]{1,0:T(8,128)} %copy-done.1, f32[2048]{0:T(1024)S(1)} %get-tuple-element.148, f32[2048,512]{1,0:T(8,128)} %get-tuple-element.68, f32[2048,512]{1,0:T(8,128)} %copy-done.27, ...), kind=kLoop, calls=%fused_computation.165 | loop fusion | flops 42990592 | bytes 48259072 | tf_op jit(solution)/shard_map/reduce_sum | solution.py:458
  1112.5 14.8 fusion.44
  1128.9 26.0 %out_wgrad.1 = bf16[3,512,2048]{2,1,0:T(8,128)(2,1)} custom-call(s32[5,7]{1,0:T(8,128)S(1)} %stack.71.plan, bf16[2048,512]{1,0:T(8,128)(2,1)S(1)} %copy-done.29, bf16[2048,2048]{1,0:T(8,128)(2,1)} %bitcast.119, bf16[2048,512]{1,0:T(8,128)(2,1)S(1)} %copy-done.28, bf16[2048,2048]{1,0:T(8,128)(2,1)} %bitcast.117), custom_call_target="tpu_custom_call" | custom-call | flops 8589934592 | bytes 44040192 | tf_op jit(solution)/shard_map/out_wgrad/pallas_call | solution.py:118
  1155.7 7.6 multiply_reduce_fusion.2
  1175.1 5.1 multiply_reduce_fusion.6
  1180.2 4.7 slice.266
  1193.7 11.1 add_convert_fusion.1
  1204.8 3.7 pad_maximum_fusion.1.x.refs_3_
  1208.5 17.6 %in_dgrad.3 = bf16[2048,2048]{1,0:T(8,128)(2,1)S(1)} custom-call(s32[2]{0:T(128)S(1)} %get-tuple-element.136.kinds, bf16[2048,1024]{1,0:T(8,128)(2,1)S(1)} %pad_maximum_fusion.1.x.refs_3_, bf16[3,2048,1024]{2,1,0:T(8,128)(2,1)} %all-gather.13.cloned.1.call-done.w), custom_call_target="tpu_custom_call" | custom-call | flops 8589934592 | bytes 29360128 | tf_op jit(solution)/shard_map/in_dgrad/pallas_call | solution.py:50
  1234.4 17.6 %in_dgrad.2 = bf16[2048,2048]{1,0:T(8,128)(2,1)S(1)} custom-call(s32[2]{0:T(128)S(1)} %get-tuple-element.135.kinds, bf16[2048,1024]{1,0:T(8,128)(2,1)S(1)} %pad_maximum_fusion.x.refs_1_, bf16[3,2048,1024]{2,1,0:T(8,128)(2,1)} %all-gather.13.cloned.1.call-done.w), custom_call_target="tpu_custom_call" | custom-call | flops 8589934592 | bytes 29360128 | tf_op jit(solution)/shard_map/in_dgrad/pallas_call | solution.py:50
  1260.2 11.6 out_proj.3
  1276.3 11.6 out_proj.2
  1290.2 58.1 %in_wgrad.1 = bf16[3,2048,1024]{2,1,0:T(8,128)(2,1)} custom-call(s32[5,7]{1,0:T(8,128)S(1)} %stack.71.plan, bf16[2048,2048]{1,0:T(8,128)(2,1)} %all-gather.11.cloned.1.call-done.x.refs_0_, bf16[2048,1024]{1,0:T(8,128)(2,1)S(1)} %copy-done.39, bf16[2048,2048]{1,0:T(8,128)(2,1)} %all-gather.17.cloned.1.call-done.x.refs_2_, bf16[2048,1024]{1,0:T(8,128)(2,1)} %copy-done.37), custom_call_target="tpu_custom_call" | custom-call | flops 17179869184 | bytes 96468992 | tf_op jit(solution)/shard_map/in_wgrad/pallas_call | solution.py:118
  1354.9 3.5 convert_element_type.216
  1358.4 54.2 %reduce-scatter.13.cloned.1.call-done = bf16[256,2048]{1,0:T(8,128)(2,1)} async-done(((bf16[2048,2048]{1,0:T(8,128)(2,1)}), bf16[256,2048]{1,0:T(8,128)(2,1)}) %reduce-scatter.13.cloned.1.call-update) | async-done | bytes 1048592 | tf_op jit(solution)/shard_map/reduce_scatter | solution.py:439
  1415.4 14.2 all-reduce.14
  1429.7 17.5 %all-reduce.17 = (f32[4,512]{1,0:T(4,128)}, f32[512]{0:T(512)}, f32[16,512]{1,0:T(8,128)}, f32[512]{0:T(512)}, f32[512]{0:T(512)}, /*index=5*/f32[256]{0:T(256)}) all-reduce(f32[4,512]{1,0:T(4,128)S(1)} %maximum_add_fusion, f32[512]{0:T(512)S(1)} %add.498, ...), channel_id=1, replica_groups=mesh['seq'=4,'chan'=8] {'seq'}, use_global_device_ids=true, to_apply=%region_29.30 | all-reduce | flops 12032 | bytes 96256 | tf_op jit(solution)/shard_map/psum | solution.py:474
  1447.2 56.0 %reduce-scatter.11.cloned.1.call-done = bf16[256,2048]{1,0:T(8,128)(2,1)} async-done(((bf16[2048,2048]{1,0:T(8,128)(2,1)}), bf16[256,2048]{1,0:T(8,128)(2,1)}) %reduce-scatter.11.cloned.1.call-update) | async-done | bytes 1048592 | tf_op jit(solution)/shard_map/reduce_scatter | solution.py:415
  1503.2 90.3 %reduce-scatter.9.cloned.1.call-done = bf16[256,2048]{1,0:T(8,128)(2,1)} async-done(((bf16[2048,2048]{1,0:T(8,128)(2,1)}), bf16[256,2048]{1,0:T(8,128)(2,1)}) %reduce-scatter.9.cloned.1.call-update) | async-done | bytes 1048592 | tf_op jit(solution)/shard_map/reduce_scatter | solution.py:415
  1593.5 3.8 fusion.27
  1601.1 114.8 %reduce-scatter.17.cloned.1.call-done = bf16[3,512,1024]{2,1,0:T(8,128)(2,1)} async-done(((bf16[3,2048,1024]{2,1,0:T(8,128)(2,1)}), bf16[3,512,1024]{2,1,0:T(8,128)(2,1)}) %reduce-scatter.17.cloned.1.call-update) | async-done | bytes 3145744 | tf_op jit(solution)/shard_map/reduce_scatter | solution.py:471
  1715.9 9.0 reshape.249
  (339 shorter events, 154.5 us)
Async XLA Ops:
  7.2 18.2 %copy-start.51 = (bf16[2,256,2048]{2,1,0:T(8,128)(2,1)S(1)}, bf16[2,256,2048]{2,1,0:T(8,128)(2,1)}, u32[]{:S(2)}) copy-start(bf16[2,256,2048]{2,1,0:T(8,128)(2,1)} %param.14) | copy-start | bytes 6291460
  7.2 78.4 %all-gather.15.cloned.1.call-start = ((), (), s32[]{:S(2)}) async-start(), calls=%async_computation.9 | async-start | bytes 7864320 | tf_op jit(solution)/shard_map/all_gather | solution.py:382
  7.9 161.4 %all-gather.21.cloned.1.call-start = ((), (), s32[]{:S(2)}) async-start(), calls=%async_computation.19 | async-start | bytes 9437184 | tf_op jit(solution)/shard_map/all_gather | solution.py:385
  11.2 241.0 %all-gather.19.cloned.1.call-start = ((), (), s32[]{:S(2)}) async-start(), calls=%async_computation.18 | async-start | bytes 9437184 | tf_op jit(solution)/shard_map/all_gather | solution.py:385
  11.9 322.9 %all-gather.17.cloned.1.call-start = ((), (), s32[]{:S(2)}) async-start(), calls=%async_computation.11 | async-start | bytes 9437184 | tf_op jit(solution)/shard_map/all_gather | solution.py:384
  27.9 430.3 %all-gather.13.cloned.1.call-start = ((), (), s32[]{:S(2)}) async-start(), calls=%async_computation.8 | async-start | bytes 15728640 | tf_op jit(solution)/shard_map/all_gather | solution.py:379
  34.1 17.4 %copy-start.89 = (s32[2,1,5]{2,1,0:T(1,128)S(1)}, s32[2,1,5]{2,1,0:T(1,128)}, u32[]{:S(2)}) copy-start(s32[2,1,5]{2,1,0:T(1,128)} %param.17) | copy-start | bytes 124
  34.1 36.8 %copy-start.102 = (f32[4,512]{1,0:T(4,128)S(1)}, f32[4,512]{1,0:T(4,128)}, u32[]{:S(2)}) copy-start(f32[4,512]{1,0:T(4,128)} %param.22) | copy-start | bytes 24580
  34.1 508.2 %all-gather.11.cloned.1.call-start = ((), (), s32[]{:S(2)}) async-start(), calls=%async_computation.7 | async-start | bytes 9437184 | tf_op jit(solution)/shard_map/all_gather | solution.py:384
  34.7 662.2 %all-reduce.24.cloned.1.call-start = ((), (), s32[]{:S(2)}) async-start(), calls=%async_computation.21 | async-start | bytes 8388608 | tf_op jit(solution)/shard_map/psum | solution.py:402
  61.6 505.5 %copy-start.72 = (f32[2048]{0:T(1024)}, f32[2048]{0:T(1024)S(1)}, u32[]{:S(2)}) copy-start(f32[2048]{0:T(1024)S(1)} %get-tuple-element.147) | copy-start | bytes 24580
  64.7 502.4 %copy-start.74 = (f32[2048]{0:T(1024)}, f32[2048]{0:T(1024)S(1)}, u32[]{:S(2)}) copy-start(f32[2048]{0:T(1024)S(1)} %get-tuple-element.145) | copy-start | bytes 24580
  64.7 502.4 %copy-start.76 = (f32[2048]{0:T(1024)}, f32[2048]{0:T(1024)S(1)}, u32[]{:S(2)}) copy-start(f32[2048]{0:T(1024)S(1)} %get-tuple-element.146) | copy-start | bytes 24580
  67.8 517.7 %copy-start.66 = (f32[2048]{0:T(1024)}, f32[2048]{0:T(1024)S(1)}, u32[]{:S(2)}) copy-start(f32[2048]{0:T(1024)S(1)} %get-tuple-element.143) | copy-start | bytes 24580
  70.8 514.6 %copy-start.68 = (f32[2048]{0:T(1024)}, f32[2048]{0:T(1024)S(1)}, u32[]{:S(2)}) copy-start(f32[2048]{0:T(1024)S(1)} %get-tuple-element.141) | copy-start | bytes 24580
  70.9 514.6 %copy-start.70 = (f32[2048]{0:T(1024)}, f32[2048]{0:T(1024)S(1)}, u32[]{:S(2)}) copy-start(f32[2048]{0:T(1024)S(1)} %get-tuple-element.142) | copy-start | bytes 24580
  70.9 514.5 %copy-start.79 = (f32[1,512]{1,0:T(1,128)}, f32[1,512]{1,0:T(1,128)S(1)}, u32[]{:S(2)}) copy-start(f32[1,512]{1,0:T(1,128)S(1)} %get-tuple-element.119) | copy-start | bytes 6148
  70.9 514.5 %copy-start.81 = (f32[1,512]{1,0:T(1,128)}, f32[1,512]{1,0:T(1,128)S(1)}, u32[]{:S(2)}) copy-start(f32[1,512]{1,0:T(1,128)S(1)} %get-tuple-element.120) | copy-start | bytes 6148
  70.9 514.5 %copy-start.83 = (f32[1,512]{1,0:T(1,128)}, f32[1,512]{1,0:T(1,128)S(1)}, u32[]{:S(2)}) copy-start(f32[1,512]{1,0:T(1,128)S(1)} %get-tuple-element.121) | copy-start | bytes 6148
  70.9 514.5 %copy-start.85 = (f32[1,512]{1,0:T(1,128)}, f32[1,512]{1,0:T(1,128)S(1)}, u32[]{:S(2)}) copy-start(f32[1,512]{1,0:T(1,128)S(1)} %get-tuple-element.122) | copy-start | bytes 6148
  558.4 27.1 %copy-start = (f32[2048,1024]{1,0:T(8,128)}, f32[2048,1024]{1,0:T(8,128)S(1)}, u32[]{:S(2)}) copy-start(f32[2048,1024]{1,0:T(8,128)S(1)} %in_proj.2) | copy-start | bytes 25165828
  582.3 389.1 %copy-start.6 = (bf16[2048,512]{1,0:T(8,128)(2,1)}, bf16[2048,512]{1,0:T(8,128)(2,1)S(1)}, u32[]{:S(2)}) copy-start(bf16[2048,512]{1,0:T(8,128)(2,1)S(1)} %get-tuple-element.67.x.refs_3_) | copy-start | bytes 6291460
  596.8 12.4 copy-start.62
  601.3 750.3 %all-reduce.22.cloned.1.call-start = ((), (), s32[]{:S(2)}) async-start(), calls=%async_computation.20 | async-start | bytes 983040
  700.9 132.3 %copy-start.35 = (bf16[2048,128]{1,0:T(8,128)(2,1)}, bf16[2048,128]{1,0:T(8,128)(2,1)S(1)}, u32[]{:S(2)}) copy-start(bf16[2048,128]{1,0:T(8,128)(2,1)S(1)} %slice.306.x.refs_2_) | copy-start | bytes 1572868
  834.9 10.6 copy-start.13
  980.3 90.3 %copy-start.11 = (bf16[2048,512]{1,0:T(8,128)(2,1)S(1)}, bf16[2048,512]{1,0:T(8,128)(2,1)}, u32[]{:S(2)}) copy-start(bf16[2048,512]{1,0:T(8,128)(2,1)} %copy-done.8) | copy-start | bytes 6291460
  1079.2 274.0 %reduce-scatter.19.cloned.1.call-start = ((), (), s32[]{:S(2)}) async-start(), calls=%async_computation.16 | async-start | bytes 491520 | tf_op jit(solution)/shard_map/reduce_scatter | solution.py:470
  1092.3 262.6 %reduce-scatter.21.cloned.1.call-start = ((), (), s32[]{:S(2)}) async-start(), calls=%async_computation.17 | async-start | bytes 7864320 | tf_op jit(solution)/shard_map/reduce_scatter | solution.py:468
  1092.4 20.1 %slice-start = ((s8[8388608]{0:T(1024)(128)(4,1)}), s8[4194304]{0:T(1024)(128)(4,1)S(1)}, s32[]{:S(2)}) async-start(s8[8388608]{0:T(1024)(128)(4,1)} %bitcast.104), calls=%async_computation.22 | async-start | bytes 8388608
  1092.4 20.1 %slice-start.1 = ((s8[8388608]{0:T(1024)(128)(4,1)}), s8[4194304]{0:T(1024)(128)(4,1)S(1)}, s32[]{:S(2)}) async-start(s8[8388608]{0:T(1024)(128)(4,1)} %bitcast.104), calls=%async_computation.23 | async-start | bytes 8388608
  1092.4 20.1 %copy-start.12 = (bf16[2048,512]{1,0:T(8,128)(2,1)S(1)}, bf16[2048,512]{1,0:T(8,128)(2,1)}, u32[]{:S(2)}) copy-start(bf16[2048,512]{1,0:T(8,128)(2,1)} %copy-done.8) | copy-start | bytes 6291460
  1092.4 20.1 %copy-start.16 = (f32[2048,512]{1,0:T(8,128)S(1)}, f32[2048,512]{1,0:T(8,128)}, u32[]{:S(2)}) copy-start(f32[2048,512]{1,0:T(8,128)} %copy-done.14) | copy-start | bytes 12582916
  1092.4 20.1 %copy-start.19 = (f32[2048,512]{1,0:T(8,128)S(1)}, f32[2048,512]{1,0:T(8,128)}, u32[]{:S(2)}) copy-start(f32[2048,512]{1,0:T(8,128)} %copy-done.17) | copy-start | bytes 12582916
  1112.5 14.8 copy-start.28
  1155.0 203.4 %reduce-scatter.15.cloned.1.call-start = ((), (), s32[]{:S(2)}) async-start(), calls=%async_computation.14 | async-start | bytes 9437184 | tf_op jit(solution)/shard_map/reduce_scatter | solution.py:439
  1163.4 8.0 copy-start.67
  1163.4 8.0 copy-start.69
  1163.4 8.0 copy-start.71
  1231.5 181.0 %reduce-scatter.13.cloned.1.call-start = ((), (), s32[]{:S(2)}) async-start(), calls=%async_computation.13 | async-start | bytes 9437184 | tf_op jit(solution)/shard_map/reduce_scatter | solution.py:439
  1257.3 245.9 %reduce-scatter.11.cloned.1.call-start = ((), (), s32[]{:S(2)}) async-start(), calls=%async_computation.12 | async-start | bytes 9437184 | tf_op jit(solution)/shard_map/reduce_scatter | solution.py:415
  1271.8 321.7 %reduce-scatter.9.cloned.1.call-start = ((), (), s32[]{:S(2)}) async-start(), calls=%async_computation.10 | async-start | bytes 9437184 | tf_op jit(solution)/shard_map/reduce_scatter | solution.py:415
  1287.9 428.0 %reduce-scatter.17.cloned.1.call-start = ((), (), s32[]{:S(2)}) async-start(), calls=%async_computation.15 | async-start | bytes 15728640 | tf_op jit(solution)/shard_map/reduce_scatter | solution.py:471
  1348.4 64.1 %copy-start.52 = (bf16[2,256,2048]{2,1,0:T(8,128)(2,1)S(1)}, bf16[2,256,2048]{2,1,0:T(8,128)(2,1)}, u32[]{:S(2)}) copy-start(bf16[2,256,2048]{2,1,0:T(8,128)(2,1)} %param.14) | copy-start | bytes 6291460
  1348.4 64.1 %copy-start.61 = (f32[8,1,256]{2,1,0:T(1,128)S(1)}, f32[8,1,256]{2,1,0:T(1,128)}, u32[]{:S(2)}) copy-start(f32[8,1,256]{2,1,0:T(1,128)} %copy-done.60) | copy-start | bytes 24580
  1348.5 64.1 %copy-start.91 = (f32[256]{0:T(256)S(1)}, f32[256]{0:T(256)}, u32[]{:S(2)}) copy-start(f32[256]{0:T(256)} %copy-done.90) | copy-start | bytes 3076
  1348.5 64.1 %copy-start.93 = (f32[256]{0:T(256)S(1)}, f32[256]{0:T(256)}, u32[]{:S(2)}) copy-start(f32[256]{0:T(256)} %copy-done.92) | copy-start | bytes 3076
  1358.4 235.2 %copy-start.56 = (bf16[256,2048]{1,0:T(8,128)(2,1)S(1)}, bf16[256,2048]{1,0:T(8,128)(2,1)}, u32[]{:S(2)}) copy-start(bf16[256,2048]{1,0:T(8,128)(2,1)} %reduce-scatter.15.cloned.1.call-done) | copy-start | bytes 3145732
  (77 other events, 270.1 us)
Sparse Core Ops, SparseCore 0:
  9.9 75.7 all-gather.14
  87.2 82.0 all-gather.20
  171.5 80.6 all-gather.18
  254.2 80.5 all-gather.16
  337.1 121.0 all-gather.12
  460.2 82.0 all-gather.10
  601.4 95.4 all-reduce.23
  1079.4 43.0 all-reduce.21
  1125.4 24.4 reduce-scatter.18
  1155.1 71.2 reduce-scatter.20
  1231.7 90.5 reduce-scatter.14
  1324.5 87.9 reduce-scatter.12
  1414.9 88.2 reduce-scatter.10
  1505.5 88.0 reduce-scatter.8
  1596.8 119.0 reduce-scatter.16
where the time goes:
time: 1740 us; the launch traced here: 1730 us
  waiting for transfers between devices  825 us (47%)
  Pallas kernels  457 us (26%)
  other arithmetic  153 us (9%)
  blocking collectives  150 us (9%)
  local copies, waits for them, and re-layouts  123 us (7%)
  between operations  22.8 us (1%)
    pallas_call x2, Pallas kernels, scan_both(): pl.pallas_call(functools.partial(scan_kernel, S, NG), in_specs=[HBM] * 3...  242 us
    all_gather x2, waiting for transfers between devices, shards(): ups.append(lax.all_gather(out_grad[i], 'chan', axis=0, tiled=True))  154 us
    reduce_scatter x2, waiting for transfers between devices, shards(): lax.psum_scatter(gmm(kinds, y_out, out_full, False, bf16, 'out_proj'), 'c...  146 us
    all_gather x2, waiting for transfers between devices, shards(): gathered.append(lax.all_gather(normed[i], 'chan', axis=0, tiled=True))  129 us
    all_gather x1, waiting for transfers between devices, shards(): lax.all_gather(in_weight.reshape(MODES, -1, 2 * inner), 'seq', axis=1, ti...  123 us
    pallas_call x16, Pallas kernels, gmm(): pl.pallas_call(functools.partial(gmm_kernel, trans), grid_spec=pltpu.Pref...  122 us
    reduce_scatter x1, waiting for transfers between devices, shards(): g_in = lax.psum_scatter(g_in, 'seq', scatter_dimension=1, tiled=True)  115 us
    pallas_call x4, Pallas kernels, wgrad(): pl.pallas_call(functools.partial(wgrad_kernel, nm), grid_spec=pltpu.Prefe...  93.6 us
  transfers between devices with their start and end apart: 15, of which 11 were waited for; matrix products, arithmetic and copies ran while one was open for 8% of the time, Pallas kernels for 11%

commit v1 on v0

v1 whole, which is shorter than its diff:
```python
import functools

import jax
import jax.numpy as jnp
from jax import lax
from jax.experimental import pallas as pl
from jax.experimental.pallas import tpu as pltpu
from jax.sharding import PartitionSpec as P

MODES = 3
MBLK = 1024
LOG2E = 1.4426950408889634
RESET = 1.0e4
CHUNKS = 8
UNROLL = 8
RB = 512

f32, bf16 = jnp.float32, jnp.bfloat16
HBM = pl.BlockSpec(memory_space=pl.ANY)
VMEM = pl.BlockSpec(memory_space=pltpu.VMEM)
MESH = pl.DeviceIdType.MESH


def sds(shape, dtype):
    return jax.ShapeDtypeStruct(shape, dtype)


def cost(flops, nbytes, trans=0):
    return pl.CostEstimate(flops=int(flops), bytes_accessed=int(nbytes), transcendentals=int(trans))


def busy(us, nbytes):
    return cost(us * 1.1e9, nbytes)


def dsilu(value):
    sig = jax.nn.sigmoid(value)
    return sig * (1.0 + value * (1.0 - sig))


def by_tile(lefts, rights, left_dim):
    out = []
    for left, right in zip(lefts, rights):
        for t in range(right.shape[0] // MBLK):
            a = lax.slice_in_dim(left, t * MBLK, t * MBLK + MBLK, axis=left_dim)
            b = lax.slice_in_dim(right, t * MBLK, t * MBLK + MBLK, axis=0)
            dims = (((left_dim,), (0,)), ((), ()))
            out.append(lax.dot_general(a, b, dims, preferred_element_type=f32).astype(bf16))
    return out


def by_modality(kinds, tiles):
    out = []
    for m in range(MODES):
        out.append(
            sum(jnp.where(kinds[t] == m, tile.astype(f32), 0.0) for t, tile in enumerate(tiles)).astype(bf16)
        )
    return jnp.stack(out)


def by_modality_blocks(kinds, tiles, dim, n):
    blocks = [jnp.split(tile, n, axis=dim) for tile in tiles]
    return [by_modality(kinds, [b[j] for b in blocks]) for j in range(n)]


def chain(ends, total, back):
    row = lax.broadcasted_iota(jnp.int32, ends.shape, 0)
    for k in (1, 2, 4):
        shift = CHUNKS - k if back else k
        ok = (row < CHUNKS - k) if back else (row >= k)
        ends = ends + total * jnp.where(ok, pltpu.roll(ends, shift, 0), 0.0)
        total = total * jnp.where(ok, pltpu.roll(total, shift, 0), 1.0)
    shift = CHUNKS - 1 if back else 1
    ok = (row < CHUNKS - 1) if back else (row >= 1)
    return jnp.where(ok, pltpu.roll(ends, shift, 0), 0.0)


def scan_kernel(
    S, NG, ddec_h, dx_h, ds_h, bc_h, rate2, rate, y_h, gb_h, fr_h, dbc_h, drate,
    ddec, dx, ds, bc, y, gb, fr, dbc, p_scr, bb, cb, q, sems
):
    NN, L = rate.shape
    KT = L // 128
    copies = []
    for a, (src, dst) in enumerate(((ddec_h, ddec), (dx_h, dx), (ds_h, ds), (bc_h, bc))):
        for c in range(CHUNKS):
            copies.append(
                pltpu.make_async_copy(src.at[pl.ds(c * S, S), :], dst.at[:, c, :], sems.at[a, c])
            )
    for cp in copies:
        cp.start()
    dbc[...] = jnp.zeros_like(dbc)
    y[...] = jnp.zeros_like(y)
    gb[...] = jnp.zeros_like(gb)
    fr[...] = jnp.zeros_like(fr)
    for cp in copies:
        cp.wait()

    def rows(s):
        return pl.ds(pl.multiple_of(s * 8, 8), 8)

    def wide(v):
        return jnp.concatenate([v] * KT, axis=1)

    def fold(v):
        return sum(v[:, 128 * i : 128 * i + 128] for i in range(KT))

    def loop(body, init):
        def outer(k, carry):
            for u in range(UNROLL):
                carry = body(k * UNROLL + u, carry)
            return carry

        return lax.fori_loop(0, S // UNROLL, outer, init)

    dsum = lax.fori_loop(0, S, lambda s, a: a + ddec[s], jnp.zeros((8, L), f32))

    def group(g, _):
        kk = lax.broadcasted_iota(jnp.int32, (2 * NN, NG * 128), 0)
        ln = lax.broadcasted_iota(jnp.int32, (2 * NN, NG * 128), 1) // 128
        Xb = jnp.where(kk == g * NG + ln, 1.0, 0.0).astype(bf16)
        Xc = jnp.where(kk == NN + g * NG + ln, 1.0, 0.0).astype(bf16)
        rr = lax.broadcasted_iota(jnp.int32, (NG * 128, 128), 0) // 128
        cc = lax.broadcasted_iota(jnp.int32, (NG * 128, 128), 1)
        Rb = jnp.where(cc == rr + g * NG, 1.0, 0.0).astype(bf16)
        Rc = jnp.where(cc == rr + NN + g * NG, 1.0, 0.0).astype(bf16)

        v = bc[...].reshape(S * CHUNKS, 128)[:, : 2 * NN]
        hi = v.astype(bf16)
        lo = (v - hi.astype(f32)).astype(bf16)
        bb[...] = dot(hi, Xb) + dot(lo, Xb)
        cb[...] = dot(hi, Xc) + dot(lo, Xc)

        def reduce(R):
            out = dot(q[...].astype(bf16), R)
            dbc[...] += out.reshape(S, CHUNKS, 128)

        r2 = [jnp.broadcast_to(rate2[pl.ds(g * NG + n, 1), :], (8, L)) for n in range(NG)]
        rt = [jnp.broadcast_to(rate[pl.ds(g * NG + n, 1), :], (8, L)) for n in range(NG)]
        total = [jnp.exp2(dsum * r2[n]) for n in range(NG)]
        zero = tuple(jnp.zeros((8, L), f32) for _ in range(NG))
        cols = [slice(128 * n, 128 * n + 128) for n in range(NG)]

        def ahead(s, st):
            d, x, b = ddec[s], dx[s], bb[rows(s), :]
            return tuple(
                jnp.exp2(d * r2[n]) * st[n] + x * wide(b[:, cols[n]]) for n in range(NG)
            )

        st = loop(ahead, zero)
        st = tuple(chain(st[n], total[n], False) for n in range(NG))

        def forward(s, st):
            d, x, b, c, dst = ddec[s], dx[s], bb[rows(s), :], cb[rows(s), :], ds[s]
            acc, new = y[s], []
            for n in range(NG):
                p = jnp.exp2(d * r2[n]) * st[n]
                p_scr[s, n] = p
                h = p + x * wide(b[:, cols[n]])
                acc = acc + wide(c[:, cols[n]]) * h
                q[rows(s), cols[n]] = fold(dst * h)
                new.append(h)
            y[s] = acc
            return tuple(new)

        loop(forward, st)
        reduce(Rc)

        def behind(k, A):
            s = S - 1 - k
            d, c, dst = ddec[s], cb[rows(s), :], ds[s]
            return tuple(
                jnp.exp2(d * r2[n]) * (dst * wide(c[:, cols[n]]) + A[n]) for n in range(NG)
            )

        A = loop(behind, zero)
        A = tuple(chain(A[n], total[n], True) for n in range(NG))

        def backward(k, carry):
            A, dr = carry
            s = S - 1 - k
            d, x, b, c, dst = ddec[s], dx[s], bb[rows(s), :], cb[rows(s), :], ds[s]
            ga, fa, nA, ndr = gb[s], fr[s], [], []
            for n in range(NG):
                G = dst * wide(c[:, cols[n]]) + A[n]
                nA.append(jnp.exp2(d * r2[n]) * G)
                flow = G * p_scr[s, n]
                ndr.append(dr[n] + flow * d)
                fa = fa + flow * rt[n]
                ga = ga + G * wide(b[:, cols[n]])
                q[rows(s), cols[n]] = fold(G * x)
            gb[s] = ga
            fr[s] = fa
            return tuple(nA), tuple(ndr)

        A, dr = loop(backward, (A, zero))
        reduce(Rb)
        for n in range(NG):
            drate[pl.ds(g * NG + n, 1), :] = jnp.sum(dr[n], axis=0, keepdims=True)
        return 0

    lax.fori_loop(0, NN // NG, group, 0)
    copies = []
    for a, (src, dst) in enumerate(((y, y_h), (gb, gb_h), (fr, fr_h), (dbc, dbc_h))):
        for c in range(CHUNKS):
            copies.append(
                pltpu.make_async_copy(src.at[:, c, :], dst.at[pl.ds(c * S, S), :], sems.at[a, c])
            )
    for cp in copies:
        cp.start()
    for cp in copies:
        cp.wait()


def scan_both(ddec, dx, ds, bc, rate, NG=4):
    T, E = ddec.shape
    N = rate.shape[0]
    S = T // CHUNKS
    act = pltpu.VMEM((S, CHUNKS, E), f32)
    thin = pltpu.VMEM((S, CHUNKS, 128), f32)
    return pl.pallas_call(
        functools.partial(scan_kernel, S, NG),
        in_specs=[HBM] * 4 + [VMEM] * 2,
        out_specs=[HBM] * 4 + [VMEM],
        out_shape=[sds((T, E), f32)] * 3 + [sds((T, 128), f32), sds((N, E), f32)],
        scratch_shapes=[act] * 3 + [thin] + [act] * 3 + [thin]
        + [pltpu.VMEM((S, NG, CHUNKS, E), f32)]
        + [pltpu.VMEM((T, NG * 128), f32)] * 3
        + [pltpu.SemaphoreType.DMA((4, CHUNKS))],
        compiler_params=pltpu.CompilerParams(vmem_limit_bytes=60 << 20),
        cost_estimate=busy(105.0 * T * E * N / (2048 * 512 * 16), 24 * T * E),
        name="scan_both",
    )(ddec, dx, ds, bc, rate * LOG2E, rate)


def sum_kernel(pairs, n, *refs):
    parts, outs, rest = refs[:n], refs[n : 2 * n], refs[2 * n :]
    half, near, mine, far = rest[:n], rest[n : 2 * n], rest[2 * n : 3 * n], rest[3 * n : 4 * n]
    sems_s, sems_r = rest[4 * n :]
    T = parts[0].shape[1]
    H = T // 2
    Q = H // pairs
    me = lax.axis_index("chan")
    core, z = lax.rem(me, 2), me // 2
    mate = me + 1 - 2 * core
    peers = [lax.rem(z + k, pairs) for k in range(1, pairs)]
    gate = pltpu.get_barrier_semaphore()
    for dev in [mate] + [2 * p + core for p in peers]:
        pl.semaphore_signal(gate, inc=1, device_id={"chan": dev}, device_id_type=MESH)
    pl.semaphore_wait(gate, pairs)

    def cols(i, n):
        return pl.ds(pl.multiple_of(i * n, n), n)

    def send(a, src, dst, k, dev):
        c = pltpu.make_async_remote_copy(
            src_ref=src, dst_ref=dst, send_sem=sems_s.at[a, k], recv_sem=sems_r.at[a, k],
            device_id={"chan": dev}, device_id_type=MESH,
        )
        c.start()
        return c

    first = [send(a, parts[a].at[:, cols(1 - core, H)], near[a], 0, mate) for a in range(n)]
    for a in range(n):
        first[a].wait()
        half[a][...] = (
            parts[a][:, cols(core, H)].astype(f32) + near[a][...].astype(f32)
        ).astype(half[a].dtype)
    sends = [
        [send(a, half[a].at[:, cols(p, Q)], far[a].at[k], 1 + k, 2 * p + core) for a in range(n)]
        for k, p in enumerate(peers)
    ]
    totals = [half[a][:, cols(z, Q)].astype(f32) for a in range(n)]
    for k in range(pairs - 1):
        for a in range(n):
            sends[k][a].wait()
            totals[a] = totals[a] + far[a][k].astype(f32)
    at = pl.ds(pl.multiple_of(core * H + z * Q, Q), Q)
    sends = []
    for a in range(n):
        mine[a][...] = totals[a].astype(mine[a].dtype)
        for k, p in enumerate(peers):
            sends.append(send(a, mine[a], outs[a].at[:, at], pairs + k, 2 * p + core))
        outs[a][:, at] = mine[a][...]
    for c in sends:
        c.wait()
    last = [
        send(a, outs[a].at[:, cols(core, H)], outs[a].at[:, cols(core, H)], 2 * pairs - 1, mate)
        for a in range(n)
    ]
    for c in last:
        c.wait()


def chan_sum(parts, number):
    n = len(parts)
    T = parts[0].shape[1]
    pairs = lax.axis_size("chan") // 2
    Q = T // 2 // pairs
    if Q % 128:
        return [lax.psum(p.astype(f32), "chan").astype(p.dtype) for p in parts]
    shapes = [(p.shape[0], p.dtype) for p in parts]
    return pl.pallas_call(
        functools.partial(sum_kernel, pairs, n),
        in_specs=[VMEM] * n,
        out_specs=[VMEM] * n,
        out_shape=[sds(p.shape, p.dtype) for p in parts],
        scratch_shapes=[pltpu.VMEM((c, T // 2), d) for c, d in shapes] * 2
        + [pltpu.VMEM((c, Q), d) for c, d in shapes]
        + [pltpu.VMEM((pairs - 1, c, Q), d) for c, d in shapes]
        + [pltpu.SemaphoreType.DMA((n, 2 * pairs))] * 2,
        compiler_params=pltpu.CompilerParams(
            collective_id=number, has_side_effects=True, vmem_limit_bytes=32 << 20
        ),
        cost_estimate=busy(26.0, 4 * T),
        name="chan_sum",
    )(*parts)


def places(lens, block):
    t = lax.broadcasted_iota(jnp.int32, (RB, 1), 0) + block * RB
    begins = jnp.zeros_like(t)
    end = jnp.int32(0)
    start_of_padding = end
    for k in range(lens.shape[0]):
        start_of_padding = end
        end = end + lens[k]
        begins = begins + jnp.where(end <= t, lens[k], 0)
    return t - begins, jnp.where(t < start_of_padding, 1.0, 0.0)


def silu(v):
    return v * jax.nn.sigmoid(v)


def dot(a, b):
    return jnp.dot(a, b, preferred_element_type=f32)


def dot_nt(a, b):
    return lax.dot_general(a, b, (((1,), (1,)), ((), ())), preferred_element_type=f32)


def dot_tn(a, b):
    return lax.dot_general(a, b, (((0,), (0,)), ((), ())), preferred_element_type=f32)


def conv_of(xe, cw, cb, position, taps):
    conv = jnp.zeros((RB, cw.shape[1]), f32) + cb[...]
    lags = []
    for k in range(taps):
        lag = xe[pl.ds(8 - k, RB), :]
        lags.append(lag)
        conv = conv + cw[k : k + 1, :] * lag * jnp.where(position >= k, 1.0, 0.0)
    return conv, lags


def in_kernel(taps, kinds, lens, g, xw, cw, cb, *rest):
    ws, (x_o, gate_o, xc_o, low_o, thin_o, xe) = rest[:-6], rest[-6:]
    blk = pl.program_id(0)
    P4 = ws[0].shape[1]
    inner = cw.shape[1]
    mixed = sum(dot(g[:, P4 * j : P4 * j + P4], w[0]) for j, w in enumerate(ws))
    x = mixed[:, :inner]
    x_o[...] = x
    gate_o[...] = mixed[:, inner:]

    @pl.when(blk == 0)
    def _():
        xe[pl.ds(0, 8), :] = jnp.zeros((8, inner), f32)

    @pl.when(blk > 0)
    def _():
        xe[pl.ds(0, 8), :] = xe[pl.ds(RB, 8), :]

    xe[pl.ds(8, RB), :] = x
    position, valid = places(lens, blk)
    conv, lags = conv_of(xe, cw, cb, position, taps)
    xc = silu(conv).astype(bf16)
    xc_o[...] = xc
    part = dot_nt(xw[0], xc)
    rank = low_o.shape[0]
    low_o[...] = part[:rank].astype(bf16)
    thin_o[...] = part[rank:]


def mid_kernel(kinds, lens, u, gate, xc, low, thin, dtw, dtb, *rest):
    ws, (ddec_o, delta_o, dx_o, ds_o, dy_o, bc_o) = rest[:-6], rest[-6:]
    blk = pl.program_id(0)
    P4 = ws[0].shape[2]
    dy = sum(dot_nt(u[:, P4 * j : P4 * j + P4], w[0]) for j, w in enumerate(ws))
    position, valid = places(lens, blk)
    pre = dot_tn(low[...], dtw[0]) + dtb[...]
    delta = jnp.maximum(pre, 0.0) + jnp.log1p(jnp.exp(-jnp.abs(pre)))
    ddec_o[...] = jnp.where(position > 0, delta, RESET)
    delta_o[...] = delta
    dx_o[...] = delta * xc[...].astype(f32)
    ds_o[...] = dy * silu(gate[...]) * valid
    dy_o[...] = dy
    bc_o[...] = jnp.concatenate([thin[...], jnp.zeros((128 - thin.shape[0], RB), f32)], axis=0).T


def post_kernel(nbc, kinds, lens, y, gb, fr, ds, dy, gate, xc, delta, dbc, skip, dtw, *rest):
    ws, (out_o, y_o, dgate_o, dpre_o, dxc_o, dpp_o, sum_o) = rest[:-7], rest[-7:]
    blk = pl.program_id(0)
    position, valid = places(lens, blk)
    x = xc[...].astype(f32)
    z = gate[...]
    scanned = y[...] + skip[...] * x
    yo = (scanned * silu(z) * valid).astype(bf16)
    y_o[...] = yo
    dgate_o[...] = (dy[...] * scanned * valid * dsilu(z)).astype(bf16)
    dl = delta[...]
    g = gb[...]
    dpre = ((x * g + fr[...]) * (1.0 - jnp.exp(-dl))).astype(bf16)
    dpre_o[...] = dpre
    dlow = dot_nt(dtw[0], dpre)
    dpp_o[...] = jnp.concatenate([dlow, dbc[...].T[:nbc, :]], axis=0).astype(bf16)
    d = ds[...]
    dxc_o[...] = d * skip[...] + dl * g
    P4 = ws[0].shape[2]
    for j, w in enumerate(ws):
        out_o[:, P4 * j : P4 * j + P4] = dot(yo, w[0]).astype(bf16)

    @pl.when(blk == 0)
    def _():
        sum_o[...] = jnp.zeros_like(sum_o)

    sum_o[0:1, :] += jnp.sum(d * x, axis=0, keepdims=True)
    sum_o[1:2, :] += jnp.sum(dpre.astype(f32), axis=0, keepdims=True)


def back_kernel(taps, nblk, kinds, lens, dproj, xw, dxc, x, xprev, cw, cb, dgate, g, *rest):
    ws, (din_o, dn_o, sum_o, gain_o, xe, mk) = rest[:-6], rest[-6:]
    step = pl.program_id(0)
    blk = nblk - 1 - step
    inner = cw.shape[1]
    position, valid = places(lens, blk)
    xe[pl.ds(0, 8), :] = jnp.where(blk > 0, xprev[...], 0.0)
    xe[pl.ds(8, RB), :] = x[...]
    conv, lags = conv_of(xe, cw, cb, position, taps)
    dconv = (dxc[...] + dot_tn(dproj[...], xw[0])) * dsilu(conv)

    @pl.when(step == 0)
    def _():
        sum_o[...] = jnp.zeros_like(sum_o)
        gain_o[...] = jnp.zeros_like(gain_o)
        mk[:, pl.ds(RB, 8), :] = jnp.zeros((taps, 8, inner), f32)

    @pl.when(step > 0)
    def _():
        mk[:, pl.ds(RB, 8), :] = mk[:, pl.ds(0, 8), :]

    din = jnp.zeros((RB, inner), f32)
    for k in range(taps):
        masked = dconv * jnp.where(position >= k, 1.0, 0.0)
        mk[k, pl.ds(0, RB), :] = masked
        sum_o[k : k + 1, :] += jnp.sum(masked * lags[k], axis=0, keepdims=True)
        din = din + cw[k : k + 1, :] * mk[k, pl.ds(k, RB), :]
    sum_o[taps : taps + 1, :] += jnp.sum(dconv, axis=0, keepdims=True)
    din_o[...] = din.astype(bf16)
    dmix = jnp.concatenate([din.astype(bf16), dgate[...]], axis=1)
    P4 = ws[0].shape[1]
    for j, w in enumerate(ws):
        part = dot_nt(dmix, w[0])
        at = slice(P4 * j, P4 * j + P4)
        dn_o[:, at] = part.astype(bf16)
        gain_o[0:1, at] += jnp.sum(part * g[:, at].astype(f32), axis=0, keepdims=True)


def stage(kernel, name, T, blocked, weights, whole, outs, sums, scratch, kinds, lens, us, reverse=False, prev=None, order=None, across={}, out_across=()):
    n = T // RB
    at = (lambda b: n - 1 - b) if reverse else (lambda b: b)
    per = MBLK // RB
    row = lambda b, kinds, lens: (at(b), 0)
    const = lambda b, kinds, lens: (0, 0)
    specs = {}
    args = {}
    col = lambda b, kinds, lens: (0, at(b))
    for key, a in blocked.items():
        specs[key], args[key] = pl.BlockSpec((RB, a.shape[1]), row), a
    for key, a in across.items():
        specs[key], args[key] = pl.BlockSpec((a.shape[0], RB), col), a
    for key, a in weights.items():
        specs[key] = pl.BlockSpec((1,) + a.shape[1:], lambda b, kinds, lens: (kinds[at(b) // per], 0, 0))
        args[key] = a
    for key, a in whole.items():
        specs[key], args[key] = pl.BlockSpec(a.shape, const), a
    if prev is not None:
        key, a = prev
        specs[key] = pl.BlockSpec((8, a.shape[1]), lambda b, kinds, lens: (jnp.maximum(at(b) * (RB // 8) - 1, 0), 0))
        args[key] = a
    out_specs = [pl.BlockSpec((RB, c), row) for c, _ in outs] + [pl.BlockSpec((c, RB), col) for c, _ in out_across] + [pl.BlockSpec(shape, const) for shape in sums]
    out_shape = [sds((T, c), dtype) for c, dtype in outs] + [sds((c, T), dtype) for c, dtype in out_across] + [sds(shape, f32) for shape in sums]
    nbytes = sum(a.size * a.dtype.itemsize for a in blocked.values()) + sum(T * c * 4 for c, _ in outs)
    return pl.pallas_call(
        kernel,
        grid_spec=pltpu.PrefetchScalarGridSpec(
            num_scalar_prefetch=2,
            grid=(n,),
            in_specs=[specs[k] for k in order],
            out_specs=out_specs,
            scratch_shapes=scratch,
        ),
        out_shape=out_shape,
        compiler_params=pltpu.CompilerParams(vmem_limit_bytes=56 << 20),
        cost_estimate=busy(us, nbytes),
        name=name,
    )(kinds, lens, *[args[k] for k in order])


def swap(v, bits, axis="seq"):
    n = lax.axis_size(axis)
    return lax.ppermute(v, axis, [(i, i ^ bits) for i in range(n)])


def square_gather_near(own):
    n = lax.axis_size("seq")
    return [own] + [swap(own, j) for j in range(1, 3 if n == 4 else n)]


def square_gather_far(blocks):
    if lax.axis_size("seq") != 4:
        return blocks
    own, by_x, by_y = blocks
    half = own.shape[1] // 2
    first = swap(by_x[:, :half], 2)
    second = swap(by_y[:, half:], 1)
    return [own, by_x, by_y, jnp.concatenate([first, second], axis=1)]


def scatter_far(parts):
    if len(parts) != 4:
        return []
    half = parts[3].shape[1] // 2
    return [swap(parts[3][:, :half], 1), swap(parts[3][:, half:], 2)]


def scatter_near(parts, far):
    if len(parts) != 4:
        return [parts[0]] + [swap(p, j) for j, p in enumerate(parts) if j]
    own, for_x, for_y, _ = parts
    a, b = far
    half = a.shape[1]
    for_y = jnp.concatenate(
        [(for_y[:, :half].astype(f32) + a.astype(f32)).astype(bf16), for_y[:, half:]], axis=1
    )
    for_x = jnp.concatenate(
        [for_x[:, :half], (for_x[:, half:].astype(f32) + b.astype(f32)).astype(bf16)], axis=1
    )
    return [own, swap(for_x, 1), swap(for_y, 2)]


def total_of(terms):
    return sum(t.astype(f32) for t in terms)


def seq_sum(v):
    return v + sum(swap(v, j) for j in range(1, lax.axis_size("seq")))


def chan_scatter(v):
    me = lax.axis_index("chan")
    bit = lax.axis_size("chan") // 2
    while bit:
        low, high = jnp.split(v, 2, axis=1)
        up = (me & bit) > 0
        v = jnp.where(up, high, low) + swap(jnp.where(up, low, high), bit, "chan")
        bit //= 2
    return v


def square_order(v, me):
    n = lax.axis_size("seq")
    parts = jnp.split(v, n, axis=-1)
    bit = 1
    while bit < n:
        on = (me & bit) > 0
        parts = [jnp.where(on, parts[i ^ bit], parts[i]) for i in range(n)]
        bit *= 2
    return jnp.concatenate(parts, axis=-1)


def shards(
    hidden, out_grad, modality, lengths, in_weight, x_weight, dt_weight, out_weight,
    conv_weight, conv_bias, a_log, d_skip, dt_bias, norm_gain
):
    micro, rows, width = hidden.shape
    T = modality.shape[1]
    inner = conv_bias.shape[0]
    nstate = a_log.shape[0]
    taps = conv_weight.shape[0]
    me = lax.axis_index("seq")
    nseq = lax.axis_size("seq")
    kinds_all = modality[:, ::MBLK]
    flat = kinds_all.reshape(-1)
    rate = -jnp.exp(a_log)
    P4 = in_weight.shape[1]
    w_own, norm_gain = lax.optimization_barrier(
        (in_weight.reshape(MODES, P4, 2 * inner), norm_gain)
    )
    w_in = square_gather_near(w_own)
    gain = lax.all_gather(norm_gain, "chan", axis=0, tiled=True)
    x_small = jnp.swapaxes(x_weight, 1, 2)
    ncols = x_small.shape[1]
    scales, units, normed, flipped = [], [], [], []
    for i in range(micro):
        source = hidden[i].astype(f32)
        scale = lax.rsqrt(jnp.mean(source * source, axis=1, keepdims=True) + 1e-05)
        unit = source * scale
        normed.append(square_order((unit * gain[None, :]).astype(bf16), me))
        flipped.append(square_order(out_grad[i], me))
        scales.append(scale)
        units.append(unit)
    w_in = square_gather_far(w_in)
    small = jnp.concatenate([x_small, dt_weight], axis=1)
    small = jnp.concatenate([small] + [swap(small, b) for b in range(1, nseq)], axis=2)
    small = square_order(small, me)
    x_full = jnp.concatenate(jnp.split(small[:, :ncols], nseq, axis=2), axis=1)
    dt_full = jnp.concatenate(jnp.split(small[:, ncols:], nseq, axis=2), axis=1)
    rank = dt_full.shape[1]
    later, w_in[-1] = lax.optimization_barrier((out_weight, w_in[-1]))
    w_out = square_gather_near(later)
    gathered = [lax.all_gather(normed[i], "chan", axis=0, tiled=True) for i in range(micro)]
    ups = [lax.all_gather(flipped[i], "chan", axis=0, tiled=True) for i in range(micro)]
    win = {f"w{j}": w for j, w in enumerate(w_in)}
    ws = list(win)
    vec = dict(cw=conv_weight, cb=conv_bias[None, :])
    skip, dtb = d_skip[None, :], dt_bias[None, :]
    branches, dn_parts, sums = [], [], []
    t_out, t_gate, t_x, t_dt, t_xw, d_ins = [], [], [], [], [], []

    def finish(c, d_proj):
        i = c["i"]
        d_in, dn_part, sum_b, sum_g = stage(
            functools.partial(back_kernel, taps, T // RB), "back_stage", T,
            dict(dxc=c["dxc"], x=c["x"], dgate=c["dgate"], g=gathered[i]), dict(**win, xw=x_full), vec,
            [(inner, bf16), (width, bf16)], [(8, inner), (8, width)],
            [pltpu.VMEM((RB + 8, inner), f32), pltpu.VMEM((taps, RB + 8, inner), f32)],
            kinds_all[i], lengths[i, 0], 26.0,
            reverse=True, prev=("xprev", c["x"]),
            order=["dproj", "xw", "dxc", "x", "xprev", "cw", "cb", "dgate", "g", *ws],
            across=dict(dproj=d_proj),
        )
        d_ins.append(d_in)
        t_xw.extend(by_tile([d_proj], [c["xc"]], 1))
        sums.append((c["sum_a"], sum_b, c["s_rate"] * rate, sum_g[:1]))
        return dn_part

    carried = None
    for i in range(micro):
        kinds, lens = kinds_all[i], lengths[i, 0]
        if carried is not None:
            gathered[i], d_part = lax.optimization_barrier((gathered[i], d_part))
        x_in, gate, xc, low_part, bc_part = stage(
            functools.partial(in_kernel, taps), "in_stage", T,
            dict(g=gathered[i]), dict(**win, xw=x_full), vec,
            [(inner, f32), (inner, f32), (inner, bf16)], [],
            [pltpu.VMEM((RB + 8, inner), f32)], kinds, lens, 21.0,
            order=["g", "xw", "cw", "cb", *ws],
            out_across=((rank, bf16), (2 * nstate, f32)),
        )
        if carried is None:
            *w_out, bc_part = lax.optimization_barrier((*w_out, bc_part))
            wout = {f"w{j}": w for j, w in enumerate(square_gather_far(w_out))}
            low, thin = chan_sum([low_part, bc_part], 0)
        else:
            low, thin, d_proj = chan_sum([low_part, bc_part, d_part], 1)
            dn_part = finish(carried, d_proj)
            thin, dn_part = lax.optimization_barrier((thin, dn_part))
            dn_parts.append(lax.psum_scatter(dn_part, "chan", scatter_dimension=0, tiled=True))
        ddec, delta, dx, ds, dy, bc = stage(
            mid_kernel, "mid_stage", T,
            dict(u=ups[i], gate=gate, xc=xc), dict(**wout, dtw=dt_full), dict(dtb=dtb),
            [(inner, f32)] * 5 + [(128, f32)], [], [], kinds, lens, 19.0,
            order=["u", "gate", "xc", "low", "thin", "dtw", "dtb", *ws], across=dict(low=low, thin=thin),
        )
        y, gb, fr, dbc, s_rate = scan_both(ddec, dx, ds, bc, rate)
        if dn_parts:
            dbc, branches, dn_parts = lax.optimization_barrier((dbc, branches, dn_parts))
        out_part, y_out, d_gate, d_pre, dxc, d_part, sum_a = stage(
            functools.partial(post_kernel, 2 * nstate), "post_stage", T,
            dict(y=y, gb=gb, fr=fr, ds=ds, dy=dy, gate=gate, xc=xc, delta=delta, dbc=dbc),
            dict(**wout, dtw=dt_full), dict(skip=skip),
            [(width, bf16), (inner, bf16), (inner, bf16), (inner, bf16), (inner, f32)],
            [(8, inner)], [], kinds, lens, 23.0,
            order=["y", "gb", "fr", "ds", "dy", "gate", "xc", "delta", "dbc", "skip", "dtw", *ws],
            out_across=((x_full.shape[1], bf16),),
        )
        branches.append(lax.psum_scatter(out_part, "chan", scatter_dimension=0, tiled=True))
        t_out += by_tile([y_out], [ups[i]], 0)
        t_gate += by_tile([gathered[i]], [d_gate], 0)
        t_dt += by_tile([low], [d_pre], 1)
        carried = dict(i=i, dxc=dxc, x=x_in, dgate=d_gate, xc=xc, sum_a=sum_a, s_rate=s_rate)
    g_out = by_modality_blocks(flat, t_out, 1, nseq)
    g_gate = by_modality_blocks(flat, t_gate, 0, nseq)
    far = scatter_far(g_out)
    d_part, far, g_gate[-1] = lax.optimization_barrier((d_part, far, g_gate[-1]))
    g_out = scatter_near(g_out, far)
    (d_proj,) = chan_sum([d_part], 2)
    far = scatter_far(g_gate)
    d_proj, far, g_out = lax.optimization_barrier((d_proj, far, g_out))
    g_gate = scatter_near(g_gate, far)
    dn_part = finish(carried, d_proj)
    dn_part, branches[-1] = lax.optimization_barrier((dn_part, branches[-1]))
    dn_parts.append(lax.psum_scatter(dn_part, "chan", scatter_dimension=0, tiled=True))
    g_dt = by_modality(flat, t_dt)
    g_xw = by_modality(flat, t_xw)
    ndt = dt_weight.shape[1]

    def seat_rows(bits):
        seat = me ^ bits
        a = lax.dynamic_slice_in_dim(g_xw, seat * ncols, ncols, 1)
        b = lax.dynamic_slice_in_dim(g_dt, seat * ndt, ndt, 1)
        return jnp.concatenate([a, b], axis=1)

    g_small = [seat_rows(0)] + [swap(seat_rows(b), b) for b in range(1, nseq)]
    totals = [sum(s[j] for s in sums) for j in range(4)]
    gain_rows = square_order(totals[3], me).reshape(-1, inner)
    vectors = seq_sum(jnp.concatenate([*totals[:3], gain_rows], axis=0))
    gain_total = chan_scatter(vectors[-gain_rows.shape[0] :].reshape(1, width))[0] / norm_gain
    last_in, g_gate, vectors, g_small = lax.optimization_barrier((d_ins[-1], g_gate, vectors, g_small))
    for i in range(micro):
        t_x += by_tile([gathered[i]], [last_in if i == micro - 1 else d_ins[i]], 0)
    g_x = by_modality_blocks(flat, t_x, 0, nseq)
    g_x = scatter_near(g_x, scatter_far(g_x))
    g_out, g_gate, g_x = total_of(g_out), total_of(g_gate), total_of(g_x)
    outputs, input_grads = [], []
    for i in range(micro):
        branch = square_order(branches[i].astype(f32), me)
        outputs.append((hidden[i].astype(f32) + branch).astype(bf16))
        d_unit = square_order(dn_parts[i].astype(f32), me) * gain[None, :]
        input_grads.append(
            scales[i] * (d_unit - units[i] * jnp.mean(d_unit * units[i], axis=1, keepdims=True))
            + out_grad[i].astype(f32)
        )
    g_small = total_of(g_small)
    return (
        jnp.stack(outputs, axis=0),
        jnp.stack(input_grads, axis=0),
        jnp.stack([g_x, g_gate], axis=2),
        jnp.swapaxes(g_small[:, :ncols], 1, 2),
        g_small[:, ncols:],
        g_out,
        vectors[8 : 8 + taps],
        vectors[8 + taps],
        vectors[16 : 16 + nstate],
        vectors[0],
        vectors[1],
        gain_total,
    )


def solution(mesh):
    act = P(None, ("seq", "chan"), None)
    weights = (P(None, "seq", None, "chan"), P(None, "chan", "seq"), P(None, "seq", "chan"), P(None, "chan", "seq"))
    vectors = (P(None, "chan"), P("chan"), P(None, "chan"), P("chan"), P("chan"), P("chan"))
    return jax.shard_map(
        shards,
        mesh=mesh,
        in_specs=(act, act, P(None, "seq"), P(None, "seq", None), *weights, *vectors),
        out_specs=(act, act, *weights, *vectors),
        check_vma=False,
    )
```

time: 1740 us -> 984 us (0.57)
  waiting for transfers between devices: 825 us -> 195 us
  blocking collectives: 150 us -> 13.4 us
  other arithmetic: 153 us -> 58.9 us
  Pallas kernels: 457 us -> 534 us
  local copies, waits for them, and re-layouts: 123 us -> 52.2 us
  matrix products: 0 us -> 51.5 us
  starting transfers between devices: 0.61 us -> 42.1 us
    all_gather x6 -> x4, waiting for transfers between devices: 421 us -> 0.04 us  [the longest x2 0.02 us: shards(): lax.all_gather(flipped[i], 'chan', axis=0, tiled=True)]
    reduce_scatter x7 -> x4, waiting for transfers between devices: 315 us -> 0.06 us  [the longest x2 0.04 us: shards(): lax.psum_scatter(out_part, 'chan', scatter_dimension=0, tiled=True)]
    ppermute x0 -> x32, waiting for transfers between devices: none -> 194 us  [swap(): return lax.ppermute(v, axis, [(i, i ^ bits) for i in range(n)])]
    psum x2 -> x0, blocking collectives: 106 us -> none  [the longest x1 88.9 us: shards(): lax.psum(jnp.concatenate([d_low, d_bc], axis=1), 'chan').astype(bf16)]
    reduce_sum x11 -> x1, other arithmetic: 88.5 us -> 1.03 us  [shards(): jnp.mean(d_unit * units[i], axis=1, keepdims=True)]
    psum x1 -> x0, waiting for transfers between devices: 87.1 us -> none  [shards(): proj = lax.psum(gmm(kinds, xc, x_full, True, f32, 'x_proj'), 'chan')]
    pallas_call x22 -> x13, Pallas kernels: 457 us -> 534 us  [the longest x2 227 us: scan_both(): pl.pallas_call(functools.partial(scan_kernel, S, NG), in_specs=[HBM] * 4...]
    dot_general x0 -> x20, matrix products: none -> 51.5 us  [by_tile(): lax.dot_general(a, b, dims, preferred_element_type=f32).astype(bf16)]
  transfers between devices with their start and end apart: 15 -> 40, of which waited for: 11 -> 14; matrix products, arithmetic and copies ran while one was open for 8% -> 12% of each run, Pallas kernels for 11% -> 53%
where the time goes in v1:
time: 984 us; the launch traced here: 971 us
  Pallas kernels  534 us (54%)
  waiting for transfers between devices  195 us (20%)
  other arithmetic  58.9 us (6%)
  local copies, waits for them, and re-layouts  52.2 us (5%)
  matrix products  51.5 us (5%)
  starting transfers between devices  42.1 us (4%)
  between operations  24.3 us (2%)
  blocking collectives  13.4 us (1%)
    pallas_call x2, Pallas kernels, scan_both(): pl.pallas_call(functools.partial(scan_kernel, S, NG), in_specs=[HBM] * 4...  227 us
    ppermute x32, waiting for transfers between devices, swap(): return lax.ppermute(v, axis, [(i, i ^ bits) for i in range(n)])  194 us
    pallas_call x8, Pallas kernels, stage(): pl.pallas_call(kernel, grid_spec=pltpu.PrefetchScalarGridSpec(num_scalar_...  168 us
    pallas_call x3, Pallas kernels, chan_sum(): pl.pallas_call(functools.partial(sum_kernel, pairs, n), in_specs=[VMEM] *...  139 us
    dot_general x20, matrix products, by_tile(): lax.dot_general(a, b, dims, preferred_element_type=f32).astype(bf16)  51.5 us
    ppermute x32, starting transfers between devices, swap(): return lax.ppermute(v, axis, [(i, i ^ bits) for i in range(n)])  41.6 us
    unnamed x212, local copies, waits for them, and re-layouts  35.7 us
  transfers between devices with their start and end apart: 40, of which 14 were waited for; matrix products, arithmetic and copies ran while one was open for 12% of the time, Pallas kernels for 53%

profile of v1, /device:TPU:0, one launch (start us, length us, event | category | flops | bytes accessed | tf_op | source)
XLA Modules:
  0.0 971.2 jit_solution(3966092777119004060)
XLA Ops:
  7.2 2.0 fusion.73
  9.3 6.2 reshape.289.rest_0_
  15.5 13.4 %all-gather = f32[8,1,256]{2,1,0:T(1,128)S(1)} all-gather(f32[1,1,256]{2,1,0:T(1,128)S(1)} %bitcast.199), channel_id=1, replica_groups=mesh['seq'=4,'chan'=8] {'chan'}, dimensions={0}, use_global_device_ids=true | all-gather | bytes 9216 | tf_op jit(solution)/shard_map/all_gather | solution.py:603
  40.5 2.4 collective-permute-start
  43.0 63.9 %collective-permute-done.4.rest_2_ = bf16[3,512,1024]{2,1,0:T(8,128)(2,1)S(1)} collective-permute-done((bf16[3,512,1024]{2,1,0:T(8,128)(2,1)}, bf16[3,512,1024]{2,1,0:T(8,128)(2,1)S(1)}, u32[]{:S(2)}, u32[]{:S(2)}) %collective-permute-start.4) | collective-permute-done | bytes 3145760 | tf_op jit(solution)/shard_map/ppermute | solution.py:514
  115.3 2.7 collective-permute-done
  121.3 29.6 %collective-permute-done.6 = bf16[3,256,1024]{2,1,0:T(8,128)(2,1)} collective-permute-done((bf16[3,256,1024]{2,1,0:T(8,128)(2,1)S(1)}, bf16[3,256,1024]{2,1,0:T(8,128)(2,1)}, u32[]{:S(2)}, u32[]{:S(2)}) %collective-permute-start.6) | collective-permute-done | bytes 1572896 | tf_op jit(solution)/shard_map/ppermute | solution.py:514
  150.9 3.9 pad_maximum_fusion.2.rest_3_
  156.8 19.6 %in_stage.2 = (f32[2048,512]{1,0:T(8,128)}, f32[2048,512]{1,0:T(8,128)}, bf16[2048,512]{1,0:T(8,128)(2,1)}, bf16[128,2048]{1,0:T(8,128)(2,1)}, f32[32,2048]{1,0:T(8,128)}) custom-call(s32[2]{0:T(128)} %get-tuple-element.341.kinds, s32[5]{0:T(128)} %get-tuple-element.339.lens, bf16[2048,2048]{1,0:T(8,128)(2,1)} %all-gather.12.cloned.1.call-done.g, ...), custom_call_target="tpu_custom_call" | custom-call | flops 23100000256 | bytes 20971520 | tf_op jit(solution)/shard_map/in_stage/pallas_call | solution.py:496
  176.4 14.1 %collective-permute-done.8.rest_2_ = bf16[3,512,512]{2,1,0:T(8,128)(2,1)S(1)} collective-permute-done((bf16[3,512,512]{2,1,0:T(8,128)(2,1)}, bf16[3,512,512]{2,1,0:T(8,128)(2,1)S(1)}, u32[]{:S(2)}, u32[]{:S(2)}) %collective-permute-start.8) | collective-permute-done | bytes 1572896 | tf_op jit(solution)/shard_map/ppermute | solution.py:514
  195.2 40.9 %chan_sum.3 = (bf16[128,2048]{1,0:T(8,128)(2,1)S(1)}, f32[32,2048]{1,0:T(8,128)S(1)}) custom-call(bf16[128,2048]{1,0:T(8,128)(2,1)S(1)} %copy-done.11, f32[32,2048]{1,0:T(8,128)S(1)} %copy-done.15), custom_call_target="tpu_custom_call" | custom-call | flops 28600000512 | bytes 8192 | tf_op jit(solution)/shard_map/chan_sum/pallas_call | solution.py:303
  238.9 16.6 %mid_stage.2 = (f32[2048,512]{1,0:T(8,128)}, f32[2048,512]{1,0:T(8,128)}, f32[2048,512]{1,0:T(8,128)}, f32[2048,512]{1,0:T(8,128)}, f32[2048,512]{1,0:T(8,128)}, /*index=5*/f32[2048,128]{1,0:T(8,128)}) custom-call(s32[2]{0:T(128)} %get-tuple-element.341.kinds, s32[5]{0:T(128)} %get-tuple-element.339.lens, ...), custom_call_target="tpu_custom_call" | custom-call | flops 20899999744 | bytes 36700160 | tf_op jit(solution)/shard_map/mid_stage/pallas_call | solution.py:496
  255.6 113.7 %scan_both.2 = (f32[2048,512]{1,0:T(8,128)}, f32[2048,512]{1,0:T(8,128)}, f32[2048,512]{1,0:T(8,128)}, f32[2048,128]{1,0:T(8,128)}, f32[16,512]{1,0:T(8,128)}) custom-call(f32[2048,512]{1,0:T(8,128)} %get-tuple-element.121.ddec_h, f32[2048,512]{1,0:T(8,128)} %get-tuple-element.122.dx_h, f32[2048,512]{1,0:T(8,128)} %get-tuple-element.123.ds_h.ds, ...), custom_call_target="tpu_custom_call" | custom-call | flops 115499999232 | bytes 25165824 | tf_op jit(solution)/shard_map/scan_both/pallas_call | solution.py:221
  369.3 20.7 %post_stage.2 = (bf16[2048,2048]{1,0:T(8,128)(2,1)}, bf16[2048,512]{1,0:T(8,128)(2,1)}, bf16[2048,512]{1,0:T(8,128)(2,1)}, bf16[2048,512]{1,0:T(8,128)(2,1)}, f3...) custom-call(s32[2]{0:T(128)} %get-tuple-element.341.kinds, s32[5]{0:T(128)} %get-tuple-element.339.lens, ...), custom_call_target="tpu_custom_call" | custom-call | flops 25300000768 | bytes 66060288 | tf_op jit(solution)/shard_map/post_stage/pallas_call | solution.py:496
  390.1 20.0 %in_stage.3 = (f32[2048,512]{1,0:T(8,128)}, f32[2048,512]{1,0:T(8,128)}, bf16[2048,512]{1,0:T(8,128)(2,1)}, bf16[128,2048]{1,0:T(8,128)(2,1)}, f32[32,2048]{1,0:T(8,128)}) custom-call(s32[2]{0:T(128)} %get-tuple-element.342.kinds, s32[5]{0:T(128)} %get-tuple-element.340.lens, bf16[2048,2048]{1,0:T(8,128)(2,1)} %all-gather.8.cloned.1.call-done.g, ...), custom_call_target="tpu_custom_call" | custom-call | flops 23100000256 | bytes 20971520 | tf_op jit(solution)/shard_map/in_stage/pallas_call | solution.py:496
  412.1 62.1 %chan_sum.4 = (bf16[128,2048]{1,0:T(8,128)(2,1)S(1)}, f32[32,2048]{1,0:T(8,128)S(1)}, bf16[160,2048]{1,0:T(8,128)(2,1)S(1)}) custom-call(bf16[128,2048]{1,0:T(8,128)(2,1)S(1)} %copy-done.12, f32[32,2048]{1,0:T(8,128)S(1)} %copy-done.16, bf16[160,2048]{1,0:T(8,128)(2,1)S(1)} %copy-done.10), custom_call_target="tpu_custom_call" | custom-call | flops 28600000512 | bytes 8192 | tf_op jit(solution)/shard_map/chan_sum/pallas_call | solution.py:303
  476.7 25.9 %back_stage.2 = (bf16[2048,512]{1,0:T(8,128)(2,1)}, bf16[2048,2048]{1,0:T(8,128)(2,1)}, f32[8,512]{1,0:T(8,128)}, f32[8,2048]{1,0:T(8,128)}) custom-call(s32[2]{0:T(128)} %get-tuple-element.341.kinds, s32[5]{0:T(128)} %get-tuple-element.339.lens, bf16[160,2048]{1,0:T(8,128)(2,1)} %copy-done.7, bf16[3,160,512]{2,1,0:T(8,128)(2,1)} %pad_maximum_fusion.25.xw, ...), custom_call_target="tpu_custom_call" | custom-call | flops 28600000512 | bytes 39845888 | tf_op jit(solution)/shard_map/back_stage/pallas_call | solution.py:496
  512.8 2.3 fusion.86
  516.2 18.0 %mid_stage.3 = (f32[2048,512]{1,0:T(8,128)}, f32[2048,512]{1,0:T(8,128)}, f32[2048,512]{1,0:T(8,128)}, f32[2048,512]{1,0:T(8,128)}, f32[2048,512]{1,0:T(8,128)}, /*index=5*/f32[2048,128]{1,0:T(8,128)}) custom-call(s32[2]{0:T(128)} %get-tuple-element.342.kinds, s32[5]{0:T(128)} %get-tuple-element.340.lens, bf16[2048,2048]{1,0:T(8,128)(2,1)} %all-gather.6.cloned.1.call-done.u, ...), custom_call_target="tpu_custom_call" | custom-call | flops 20899999744 | bytes 36700160 | tf_op jit(solution)/shard_map/mid_stage/pallas_call | solution.py:496
  534.2 113.6 %scan_both.3 = (f32[2048,512]{1,0:T(8,128)}, f32[2048,512]{1,0:T(8,128)}, f32[2048,512]{1,0:T(8,128)}, f32[2048,128]{1,0:T(8,128)}, f32[16,512]{1,0:T(8,128)}) custom-call(f32[2048,512]{1,0:T(8,128)} %get-tuple-element.146.ddec_h, f32[2048,512]{1,0:T(8,128)} %get-tuple-element.147.dx_h, f32[2048,512]{1,0:T(8,128)} %get-tuple-element.148.ds_h.ds, ...), custom_call_target="tpu_custom_call" | custom-call | flops 115499999232 | bytes 25165824 | tf_op jit(solution)/shard_map/scan_both/pallas_call | solution.py:221
  647.9 21.4 %post_stage.3 = (bf16[2048,2048]{1,0:T(8,128)(2,1)}, bf16[2048,512]{1,0:T(8,128)(2,1)}, bf16[2048,512]{1,0:T(8,128)(2,1)}, bf16[2048,512]{1,0:T(8,128)(2,1)}, f3...) custom-call(s32[2]{0:T(128)} %get-tuple-element.342.kinds, s32[5]{0:T(128)} %get-tuple-element.340.lens, ...), custom_call_target="tpu_custom_call" | custom-call | flops 25300000768 | bytes 66060288 | tf_op jit(solution)/shard_map/post_stage/pallas_call | solution.py:496
  672.1 5.0 fusion.51
  677.2 4.7 fusion.48
  682.1 2.4 fusion.42
  684.5 2.4 fusion.36
  686.9 3.7 fusion.45
  690.9 2.6 fusion.57
  693.5 2.4 fusion.54
  703.1 2.4 fusion.30
  705.5 2.8 fusion.24
  713.3 6.5 collective-permute-done.12
  722.4 1.8 collective-permute-start.15
  725.5 35.6 %chan_sum.5.dproj = bf16[160,2048]{1,0:T(8,128)(2,1)S(1)} custom-call(bf16[160,2048]{1,0:T(8,128)(2,1)S(1)} %copy-done.9), custom_call_target="tpu_custom_call" | custom-call | flops 28600000512 | bytes 8192 | tf_op jit(solution)/shard_map/chan_sum/pallas_call | solution.py:303
  762.0 12.1 %collective-permute-done.15 = bf16[3,512,512]{2,1,0:T(8,128)(2,1)S(1)} collective-permute-done((bf16[3,512,512]{2,1,0:T(8,128)(2,1)S(1)}, bf16[3,512,512]{2,1,0:T(8,128)(2,1)S(1)}, u32[]{:S(2)}, u32[]{:S(2)}) %collective-permute-start.15) | collective-permute-done | bytes 1572896 | tf_op jit(solution)/shard_map/ppermute | solution.py:514
  776.5 26.0 %back_stage.3 = (bf16[2048,512]{1,0:T(8,128)(2,1)}, bf16[2048,2048]{1,0:T(8,128)(2,1)}, f32[8,512]{1,0:T(8,128)}, f32[8,2048]{1,0:T(8,128)}) custom-call(s32[2]{0:T(128)} %get-tuple-element.342.kinds, s32[5]{0:T(128)} %get-tuple-element.340.lens, bf16[160,2048]{1,0:T(8,128)(2,1)} %copy-done.5, bf16[3,160,512]{2,1,0:T(8,128)(2,1)} %pad_maximum_fusion.25.xw, ...), custom_call_target="tpu_custom_call" | custom-call | flops 28600000512 | bytes 39845888 | tf_op jit(solution)/shard_map/back_stage/pallas_call | solution.py:496
  804.0 6.3 fusion.39
  836.7 2.3 convert_add_fusion.1
  842.2 3.1 collective-permute-start.29
  845.4 1.9 collective-permute-done.29
  847.3 6.0 collective-permute-start.30
  855.9 23.5 %collective-permute-done.24 = bf16[3,72,512]{2,1,0:T(8,128)(2,1)S(1)} collective-permute-done((bf16[3,72,512]{2,1,0:T(8,128)(2,1)S(1)}, bf16[3,72,512]{2,1,0:T(8,128)(2,1)S(1)}, u32[]{:S(2)}, u32[]{:S(2)}) %collective-permute-start.24) | collective-permute-done | bytes 221216 | tf_op jit(solution)/shard_map/ppermute | solution.py:514
  879.4 5.0 fusion.33
  884.4 2.5 fusion.27
  893.2 12.8 %collective-permute-done.27 = bf16[3,256,512]{2,1,0:T(8,128)(2,1)S(1)} collective-permute-done((bf16[3,256,512]{2,1,0:T(8,128)(2,1)S(1)}, bf16[3,256,512]{2,1,0:T(8,128)(2,1)S(1)}, u32[]{:S(2)}, u32[]{:S(2)}) %collective-permute-start.27) | collective-permute-done | bytes 786464 | tf_op jit(solution)/shard_map/ppermute | solution.py:514
  906.3 2.7 collective-permute-start.28
  915.1 24.5 %collective-permute-done.28 = bf16[3,512,512]{2,1,0:T(8,128)(2,1)S(1)} collective-permute-done((bf16[3,512,512]{2,1,0:T(8,128)(2,1)S(1)}, bf16[3,512,512]{2,1,0:T(8,128)(2,1)S(1)}, u32[]{:S(2)}, u32[]{:S(2)}) %collective-permute-start.28) | collective-permute-done | bytes 1572896 | tf_op jit(solution)/shard_map/ppermute | solution.py:514
  942.1 7.8 copy.27
  961.7 2.3 pad_maximum_fusion.1
  (427 shorter events, 122.7 us)
Async XLA Ops:
  7.2 149.6 %all-gather.12.cloned.1.call-start = ((), (), s32[]{:S(2)}) async-start(), calls=%async_computation.7 | async-start | bytes 9437184 | tf_op jit(solution)/shard_map/all_gather | solution.py:624
  9.3 19.7 %copy-start.17 = (bf16[2,256,2048]{2,1,0:T(8,128)(2,1)S(1)}, bf16[2,256,2048]{2,1,0:T(8,128)(2,1)}, u32[]{:S(2)}) copy-start(bf16[2,256,2048]{2,1,0:T(8,128)(2,1)} %param.14) | copy-start | bytes 6291460
  31.6 206.2 %all-gather.10.cloned.1.call-start = ((), (), s32[]{:S(2)}) async-start(), calls=%async_computation.6 | async-start | bytes 9437184 | tf_op jit(solution)/shard_map/all_gather | solution.py:625
  33.8 356.3 %all-gather.8.cloned.1.call-start = ((), (), s32[]{:S(2)}) async-start(), calls=%async_computation.5 | async-start | bytes 9437184 | tf_op jit(solution)/shard_map/all_gather | solution.py:624
  35.7 480.5 %all-gather.6.cloned.1.call-start = ((), (), s32[]{:S(2)}) async-start(), calls=%async_computation.4 | async-start | bytes 9437184 | tf_op jit(solution)/shard_map/all_gather | solution.py:625
  35.7 71.2 %collective-permute-start.4 = (bf16[3,512,1024]{2,1,0:T(8,128)(2,1)}, bf16[3,512,1024]{2,1,0:T(8,128)(2,1)S(1)}, u32[]{:S(2)}, u32[]{:S(2)}) collective-permute-start(bf16[3,512,1024]{2,1,0:T(8,128)(2,1)} %reshape.289.rest_0_), channel_id=1, source_target_pairs={{0,16},{8,24},{16,0},{24,8},{1,17},{9,25},{17,1},{25,9},{2,18},{10... | collective-permute-start | bytes 9437192 | tf_op jit(solution)/shard_map/ppermute | solution.py:514
  37.3 71.3 %collective-permute-start.3 = (bf16[3,512,1024]{2,1,0:T(8,128)(2,1)}, bf16[3,512,1024]{2,1,0:T(8,128)(2,1)S(1)}, u32[]{:S(2)}, u32[]{:S(2)}) collective-permute-start(bf16[3,512,1024]{2,1,0:T(8,128)(2,1)} %reshape.289.rest_0_), channel_id=1, source_target_pairs={{0,8},{8,0},{16,24},{24,16},{1,9},{9,1},{17,25},{25,17},{2,10},{10... | collective-permute-start | bytes 9437192 | tf_op jit(solution)/shard_map/ppermute | solution.py:514
  39.5 75.8 %collective-permute-start.2 = (bf16[3,72,512]{2,1,0:T(8,128)(2,1)}, bf16[3,72,512]{2,1,0:T(8,128)(2,1)}, u32[]{:S(2)}, u32[]{:S(2)}) collective-permute-start(bf16[3,72,512]{2,1,0:T(8,128)(2,1)} %pad_maximum_fusion.29), channel_id=1, source_target_pairs={{0,8},{8,0},{16,24},{24,16},{1,9},{9,1},{17,25},{25,17},{2,10},{10... | collective-permute-start | bytes 663560 | tf_op jit(solution)/shard_map/ppermute | solution.py:514
  40.0 75.3 %collective-permute-start.1 = (bf16[3,72,512]{2,1,0:T(8,128)(2,1)}, bf16[3,72,512]{2,1,0:T(8,128)(2,1)}, u32[]{:S(2)}, u32[]{:S(2)}) collective-permute-start(bf16[3,72,512]{2,1,0:T(8,128)(2,1)} %pad_maximum_fusion.29), channel_id=1, source_target_pairs={{0,16},{8,24},{16,0},{24,8},{1,17},{9,25},{17,1},{25,9},{2,18},{10... | collective-permute-start | bytes 663560 | tf_op jit(solution)/shard_map/ppermute | solution.py:514
  40.5 77.5 %collective-permute-start = (bf16[3,72,512]{2,1,0:T(8,128)(2,1)}, bf16[3,72,512]{2,1,0:T(8,128)(2,1)}, u32[]{:S(2)}, u32[]{:S(2)}) collective-permute-start(bf16[3,72,512]{2,1,0:T(8,128)(2,1)} %pad_maximum_fusion.29), channel_id=1, source_target_pairs={{0,24},{8,16},{16,8},{24,0},{1,25},{9,17},{17,9},{25,1},{2,26},{10... | collective-permute-start | bytes 663560 | tf_op jit(solution)/shard_map/ppermute | solution.py:514
  107.0 43.9 %collective-permute-start.6 = (bf16[3,256,1024]{2,1,0:T(8,128)(2,1)S(1)}, bf16[3,256,1024]{2,1,0:T(8,128)(2,1)}, u32[]{:S(2)}, u32[]{:S(2)}) collective-permute-start(bf16[3,256,1024]{2,1,0:T(8,128)(2,1)S(1)} %slice.519), channel_id=1, source_target_pairs={{0,8},{8,0},{16,24},{24,16},{1,9},{9,1},{17,25},{25,17},{2,10},{10... | collective-permute-start | bytes 4718600 | tf_op jit(solution)/shard_map/ppermute | solution.py:514
  109.9 41.0 %collective-permute-start.5 = (bf16[3,256,1024]{2,1,0:T(8,128)(2,1)}, bf16[3,256,1024]{2,1,0:T(8,128)(2,1)}, u32[]{:S(2)}, u32[]{:S(2)}) collective-permute-start(bf16[3,256,1024]{2,1,0:T(8,128)(2,1)} %slice.518), channel_id=1, source_target_pairs={{0,16},{8,24},{16,0},{24,8},{1,17},{9,25},{17,1},{25,9},{2,18},{10... | collective-permute-start | bytes 4718600 | tf_op jit(solution)/shard_map/ppermute | solution.py:514
  112.8 535.1 %reduce-scatter.5.cloned.1.call-start = ((), (), s32[]{:S(2)}) async-start(), calls=%async_computation.8 | async-start | bytes 9437184 | tf_op jit(solution)/shard_map/reduce_scatter | solution.py:690
  154.8 35.7 %collective-permute-start.8 = (bf16[3,512,512]{2,1,0:T(8,128)(2,1)}, bf16[3,512,512]{2,1,0:T(8,128)(2,1)S(1)}, u32[]{:S(2)}, u32[]{:S(2)}) collective-permute-start(bf16[3,512,512]{2,1,0:T(8,128)(2,1)} %rest_0_.3), channel_id=1, source_target_pairs={{0,16},{8,24},{16,0},{24,8},{1,17},{9,25},{17,1},{25,9},{2,18},{10... | collective-permute-start | bytes 4718600 | tf_op jit(solution)/shard_map/ppermute | solution.py:514
  155.4 35.5 %collective-permute-start.7 = (bf16[3,512,512]{2,1,0:T(8,128)(2,1)}, bf16[3,512,512]{2,1,0:T(8,128)(2,1)}, u32[]{:S(2)}, u32[]{:S(2)}) collective-permute-start(bf16[3,512,512]{2,1,0:T(8,128)(2,1)} %rest_0_.3), channel_id=1, source_target_pairs={{0,8},{8,0},{16,24},{24,16},{1,9},{9,1},{17,25},{25,17},{2,10},{10... | collective-permute-start | bytes 4718600 | tf_op jit(solution)/shard_map/ppermute | solution.py:514
  176.4 18.8 %copy-start.11 = (bf16[128,2048]{1,0:T(8,128)(2,1)S(1)}, bf16[128,2048]{1,0:T(8,128)(2,1)}, u32[]{:S(2)}) copy-start(bf16[128,2048]{1,0:T(8,128)(2,1)} %get-tuple-element.112.refs_0_) | copy-start | bytes 1572868
  176.4 18.8 %copy-start.15 = (f32[32,2048]{1,0:T(8,128)S(1)}, f32[32,2048]{1,0:T(8,128)}, u32[]{:S(2)}) copy-start(f32[32,2048]{1,0:T(8,128)} %get-tuple-element.115.refs_1_) | copy-start | bytes 786436
  190.5 45.6 %copy-start.61 = (bf16[3,512,512]{2,1,0:T(8,128)(2,1)}, bf16[3,512,512]{2,1,0:T(8,128)(2,1)S(1)}, u32[]{:S(2)}) copy-start(bf16[3,512,512]{2,1,0:T(8,128)(2,1)S(1)} %collective-permute-done.8.rest_2_) | copy-start | bytes 4718596
  192.3 45.4 %collective-permute-start.10 = (bf16[3,256,512]{2,1,0:T(8,128)(2,1)S(1)}, bf16[3,256,512]{2,1,0:T(8,128)(2,1)S(1)}, u32[]{:S(2)}, u32[]{:S(2)}) collective-permute-start(bf16[3,256,512]{2,1,0:T(8,128)(2,1)S(1)} %slice.190), channel_id=1, source_target_pairs={{0,8},{8,0},{16,24},{24,16},{1,9},{9,1},{17,25},{25,17},{2,10},{10... | collective-permute-start | bytes 2359304 | tf_op jit(solution)/shard_map/ppermute | solution.py:514
  193.9 43.8 %collective-permute-start.9 = (bf16[3,256,512]{2,1,0:T(8,128)(2,1)S(1)}, bf16[3,256,512]{2,1,0:T(8,128)(2,1)S(1)}, u32[]{:S(2)}, u32[]{:S(2)}) collective-permute-start(bf16[3,256,512]{2,1,0:T(8,128)(2,1)S(1)} %slice.189), channel_id=1, source_target_pairs={{0,16},{8,24},{16,0},{24,8},{1,17},{9,25},{17,1},{25,9},{2,18},{10... | collective-permute-start | bytes 2359304 | tf_op jit(solution)/shard_map/ppermute | solution.py:514
  390.0 257.9 %reduce-scatter.7.cloned.1.call-start = ((), (), s32[]{:S(2)}) async-start(), calls=%async_computation.9 | async-start | bytes 9437184 | tf_op jit(solution)/shard_map/reduce_scatter | solution.py:671
  390.1 20.0 %copy-start.10 = (bf16[160,2048]{1,0:T(8,128)(2,1)S(1)}, bf16[160,2048]{1,0:T(8,128)(2,1)}, u32[]{:S(2)}) copy-start(bf16[160,2048]{1,0:T(8,128)(2,1)} %get-tuple-element.137.refs_2_) | copy-start | bytes 1966084
  502.6 299.9 %reduce-scatter.9.cloned.1.call-start = ((), (), s32[]{:S(2)}) async-start(), calls=%async_computation.10 | async-start | bytes 9437184 | tf_op jit(solution)/shard_map/reduce_scatter | solution.py:690
  669.3 286.3 %reduce-scatter.11.cloned.1.call-start = ((), (), s32[]{:S(2)}) async-start(), calls=%async_computation.11 | async-start | bytes 9437184 | tf_op jit(solution)/shard_map/reduce_scatter | solution.py:706
  686.9 25.4 %copy-start.19 = (bf16[2048,512]{1,0:T(8,128)(2,1)}, bf16[2048,512]{1,0:T(8,128)(2,1)S(1)}, u32[]{:S(2)}) copy-start(bf16[2048,512]{1,0:T(8,128)(2,1)S(1)} %fusion.36) | copy-start | bytes 6291460
  699.9 19.9 %collective-permute-start.12 = (bf16[3,256,512]{2,1,0:T(8,128)(2,1)S(1)}, bf16[3,256,512]{2,1,0:T(8,128)(2,1)S(1)}, u32[]{:S(2)}, u32[]{:S(2)}) collective-permute-start(bf16[3,256,512]{2,1,0:T(8,128)(2,1)S(1)} %get-tuple-element.294), channel_id=1, source_target_pairs={{0,16},{8,24},{16,0},{24,8},{1,17},{9,25},{17,1},{25,9},{2,18},{10... | collective-permute-start | bytes 2359304 | tf_op jit(solution)/shard_map/ppermute | solution.py:514
  700.0 19.9 %collective-permute-start.11 = (bf16[3,256,512]{2,1,0:T(8,128)(2,1)S(1)}, bf16[3,256,512]{2,1,0:T(8,128)(2,1)S(1)}, u32[]{:S(2)}, u32[]{:S(2)}) collective-permute-start(bf16[3,256,512]{2,1,0:T(8,128)(2,1)S(1)} %get-tuple-element.295), channel_id=1, source_target_pairs={{0,8},{8,0},{16,24},{24,16},{1,9},{9,1},{17,25},{25,17},{2,10},{10... | collective-permute-start | bytes 2359304 | tf_op jit(solution)/shard_map/ppermute | solution.py:514
  720.1 41.9 %collective-permute-start.14 = (bf16[3,256,512]{2,1,0:T(8,128)(2,1)S(1)}, bf16[3,256,512]{2,1,0:T(8,128)(2,1)S(1)}, u32[]{:S(2)}, u32[]{:S(2)}) collective-permute-start(bf16[3,256,512]{2,1,0:T(8,128)(2,1)S(1)} %get-tuple-element.292), channel_id=1, source_target_pairs={{0,16},{8,24},{16,0},{24,8},{1,17},{9,25},{17,1},{25,9},{2,18},{10... | collective-permute-start | bytes 2359304 | tf_op jit(solution)/shard_map/ppermute | solution.py:514
  721.8 40.2 %collective-permute-start.13 = (bf16[3,256,512]{2,1,0:T(8,128)(2,1)S(1)}, bf16[3,256,512]{2,1,0:T(8,128)(2,1)S(1)}, u32[]{:S(2)}, u32[]{:S(2)}) collective-permute-start(bf16[3,256,512]{2,1,0:T(8,128)(2,1)S(1)} %get-tuple-element.293), channel_id=1, source_target_pairs={{0,8},{8,0},{16,24},{24,16},{1,9},{9,1},{17,25},{25,17},{2,10},{10... | collective-permute-start | bytes 2359304 | tf_op jit(solution)/shard_map/ppermute | solution.py:514
  722.4 51.7 %collective-permute-start.15 = (bf16[3,512,512]{2,1,0:T(8,128)(2,1)S(1)}, bf16[3,512,512]{2,1,0:T(8,128)(2,1)S(1)}, u32[]{:S(2)}, u32[]{:S(2)}) collective-permute-start(bf16[3,512,512]{2,1,0:T(8,128)(2,1)S(1)} %pad_maximum_fusion.8), channel_id=1, source_target_pairs={{0,8},{8,0},{16,24},{24,16},{1,9},{9,1},{17,25},{25,17},{2,10},{10... | collective-permute-start | bytes 4718600 | tf_op jit(solution)/shard_map/ppermute | solution.py:514
  724.6 49.6 %collective-permute-start.16 = (bf16[3,512,512]{2,1,0:T(8,128)(2,1)S(1)}, bf16[3,512,512]{2,1,0:T(8,128)(2,1)S(1)}, u32[]{:S(2)}, u32[]{:S(2)}) collective-permute-start(bf16[3,512,512]{2,1,0:T(8,128)(2,1)S(1)} %pad_maximum_fusion.10), channel_id=1, source_target_pairs={{0,16},{8,24},{16,0},{24,8},{1,17},{9,25},{17,1},{25,9},{2,18},{10... | collective-permute-start | bytes 4718600 | tf_op jit(solution)/shard_map/ppermute | solution.py:514
  825.2 13.9 %collective-permute-start.21 = (f32[36,512]{1,0:T(8,128)S(1)}, f32[36,512]{1,0:T(8,128)S(1)}, u32[]{:S(2)}, u32[]{:S(2)}) collective-permute-start(f32[36,512]{1,0:T(8,128)S(1)} %pad_maximum_fusion.34), channel_id=1, source_target_pairs={{0,24},{8,16},{16,8},{24,0},{1,25},{9,17},{17,9},{25,1},{2,26},{10... | collective-permute-start | bytes 221192 | tf_op jit(solution)/shard_map/ppermute | solution.py:514
  825.7 15.0 %collective-permute-start.20 = (f32[36,512]{1,0:T(8,128)S(1)}, f32[36,512]{1,0:T(8,128)S(1)}, u32[]{:S(2)}, u32[]{:S(2)}) collective-permute-start(f32[36,512]{1,0:T(8,128)S(1)} %pad_maximum_fusion.34), channel_id=1, source_target_pairs={{0,16},{8,24},{16,0},{24,8},{1,17},{9,25},{17,1},{25,9},{2,18},{10... | collective-permute-start | bytes 221192 | tf_op jit(solution)/shard_map/ppermute | solution.py:514
  827.2 15.0 %collective-permute-start.19 = (f32[36,512]{1,0:T(8,128)S(1)}, f32[36,512]{1,0:T(8,128)S(1)}, u32[]{:S(2)}, u32[]{:S(2)}) collective-permute-start(f32[36,512]{1,0:T(8,128)S(1)} %pad_maximum_fusion.34), channel_id=1, source_target_pairs={{0,8},{8,0},{16,24},{24,16},{1,9},{9,1},{17,25},{25,17},{2,10},{10... | collective-permute-start | bytes 221192 | tf_op jit(solution)/shard_map/ppermute | solution.py:514
  832.2 23.6 %collective-permute-start.22 = (bf16[3,72,512]{2,1,0:T(8,128)(2,1)S(1)}, bf16[3,72,512]{2,1,0:T(8,128)(2,1)S(1)}, u32[]{:S(2)}, u32[]{:S(2)}) collective-permute-start(bf16[3,72,512]{2,1,0:T(8,128)(2,1)S(1)} %pad_maximum_fusion.31), channel_id=1, source_target_pairs={{0,8},{8,0},{16,24},{24,16},{1,9},{9,1},{17,25},{25,17},{2,10},{10... | collective-permute-start | bytes 663560 | tf_op jit(solution)/shard_map/ppermute | solution.py:514
  832.9 23.0 %collective-permute-start.23 = (bf16[3,72,512]{2,1,0:T(8,128)(2,1)S(1)}, bf16[3,72,512]{2,1,0:T(8,128)(2,1)S(1)}, u32[]{:S(2)}, u32[]{:S(2)}) collective-permute-start(bf16[3,72,512]{2,1,0:T(8,128)(2,1)S(1)} %pad_maximum_fusion.32), channel_id=1, source_target_pairs={{0,16},{8,24},{16,0},{24,8},{1,17},{9,25},{17,1},{25,9},{2,18},{10... | collective-permute-start | bytes 663560 | tf_op jit(solution)/shard_map/ppermute | solution.py:514
  836.6 47.7 %slice-start.3 = ((s8[8388608]{0:T(1024)(128)(4,1)}), s8[4194304]{0:T(1024)(128)(4,1)S(1)}, s32[]{:S(2)}) async-start(s8[8388608]{0:T(1024)(128)(4,1)} %bitcast.206), calls=%async_computation.15 | async-start | bytes 8388608
  839.0 40.4 %copy-start.93 = (bf16[2048,512]{1,0:T(8,128)(2,1)S(1)}, bf16[2048,512]{1,0:T(8,128)(2,1)}, u32[]{:S(2)}) copy-start(bf16[2048,512]{1,0:T(8,128)(2,1)} %get-tuple-element.190) | copy-start | bytes 6291460
  839.1 40.2 %collective-permute-start.18 = (bf16[3,512,512]{2,1,0:T(8,128)(2,1)S(1)}, bf16[3,512,512]{2,1,0:T(8,128)(2,1)S(1)}, u32[]{:S(2)}, u32[]{:S(2)}) collective-permute-start(bf16[3,512,512]{2,1,0:T(8,128)(2,1)S(1)} %pad_maximum_fusion.15), channel_id=1, source_target_pairs={{0,16},{8,24},{16,0},{24,8},{1,17},{9,25},{17,1},{25,9},{2,18},{10... | collective-permute-start | bytes 4718600 | tf_op jit(solution)/shard_map/ppermute | solution.py:514
  840.7 38.6 %collective-permute-start.17 = (bf16[3,512,512]{2,1,0:T(8,128)(2,1)S(1)}, bf16[3,512,512]{2,1,0:T(8,128)(2,1)S(1)}, u32[]{:S(2)}, u32[]{:S(2)}) collective-permute-start(bf16[3,512,512]{2,1,0:T(8,128)(2,1)S(1)} %pad_maximum_fusion.13), channel_id=1, source_target_pairs={{0,8},{8,0},{16,24},{24,16},{1,9},{9,1},{17,25},{25,17},{2,10},{10... | collective-permute-start | bytes 4718600 | tf_op jit(solution)/shard_map/ppermute | solution.py:514
  842.2 5.0 collective-permute-start.29
  847.3 7.8 collective-permute-start.30
  855.0 24.3 %collective-permute-start.24 = (bf16[3,72,512]{2,1,0:T(8,128)(2,1)S(1)}, bf16[3,72,512]{2,1,0:T(8,128)(2,1)S(1)}, u32[]{:S(2)}, u32[]{:S(2)}) collective-permute-start(bf16[3,72,512]{2,1,0:T(8,128)(2,1)S(1)} %pad_maximum_fusion.33), channel_id=1, source_target_pairs={{0,24},{8,16},{16,8},{24,0},{1,25},{9,17},{17,9},{25,1},{2,26},{10... | collective-permute-start | bytes 663560 | tf_op jit(solution)/shard_map/ppermute | solution.py:514
  855.8 54.1 %collective-permute-start.31 = (f32[1,256]{1,0:T(1,128)S(1)}, f32[1,256]{1,0:T(1,128)S(1)}, u32[]{:S(2)}, u32[]{:S(2)}) collective-permute-start(f32[1,256]{1,0:T(1,128)S(1)} %broadcast_select_fusion.60), channel_id=1, source_target_pairs={{0,1},{1,0},{2,3},{3,2},{4,5},{5,4},{6,7},{7,6},{8,9},{9,8},{10,11... | collective-permute-start | bytes 3080 | tf_op jit(solution)/shard_map/ppermute | solution.py:514
  889.6 19.4 %collective-permute-start.25 = (bf16[3,256,512]{2,1,0:T(8,128)(2,1)S(1)}, bf16[3,256,512]{2,1,0:T(8,128)(2,1)S(1)}, u32[]{:S(2)}, u32[]{:S(2)}) collective-permute-start(bf16[3,256,512]{2,1,0:T(8,128)(2,1)S(1)} %get-tuple-element.290), channel_id=1, source_target_pairs={{0,16},{8,24},{16,0},{24,8},{1,17},{9,25},{17,1},{25,9},{2,18},{10... | collective-permute-start | bytes 2359304 | tf_op jit(solution)/shard_map/ppermute | solution.py:514
  890.5 15.5 %collective-permute-start.27 = (bf16[3,256,512]{2,1,0:T(8,128)(2,1)S(1)}, bf16[3,256,512]{2,1,0:T(8,128)(2,1)S(1)}, u32[]{:S(2)}, u32[]{:S(2)}) collective-permute-start(bf16[3,256,512]{2,1,0:T(8,128)(2,1)S(1)} %get-tuple-element.291), channel_id=1, source_target_pairs={{0,8},{8,0},{16,24},{24,16},{1,9},{9,1},{17,25},{25,17},{2,10},{10... | collective-permute-start | bytes 2359304 | tf_op jit(solution)/shard_map/ppermute | solution.py:514
  906.3 33.3 %collective-permute-start.28 = (bf16[3,512,512]{2,1,0:T(8,128)(2,1)S(1)}, bf16[3,512,512]{2,1,0:T(8,128)(2,1)S(1)}, u32[]{:S(2)}, u32[]{:S(2)}) collective-permute-start(bf16[3,512,512]{2,1,0:T(8,128)(2,1)S(1)} %pad_maximum_fusion.20), channel_id=1, source_target_pairs={{0,16},{8,24},{16,0},{24,8},{1,17},{9,25},{17,1},{25,9},{2,18},{10... | collective-permute-start | bytes 4718600 | tf_op jit(solution)/shard_map/ppermute | solution.py:514
  909.3 30.7 %collective-permute-start.26 = (bf16[3,512,512]{2,1,0:T(8,128)(2,1)S(1)}, bf16[3,512,512]{2,1,0:T(8,128)(2,1)S(1)}, u32[]{:S(2)}, u32[]{:S(2)}) collective-permute-start(bf16[3,512,512]{2,1,0:T(8,128)(2,1)S(1)} %pad_maximum_fusion.18), channel_id=1, source_target_pairs={{0,8},{8,0},{16,24},{24,16},{1,9},{9,1},{17,25},{25,17},{2,10},{10... | collective-permute-start | bytes 4718600 | tf_op jit(solution)/shard_map/ppermute | solution.py:514
  (97 other events, 300.3 us)
Sparse Core Ops, SparseCore 0:
  31.7 80.2 all-gather.11
  113.6 80.5 all-gather.9
  195.8 90.9 all-gather.7
  288.3 79.5 all-gather.5
  390.2 113.9 reduce-scatter.4
  506.3 94.7 reduce-scatter.6
  669.5 104.6 reduce-scatter.8
  802.7 94.0 reduce-scatter.10

commit v2 on v1

--- a/solution.py
+++ b/solution.py
@@ -13,6 +13,7 @@
 RESET = 1.0e4
 CHUNKS = 8
 UNROLL = 8
+EARLY = 0.2
 RB = 512
 
 f32, bf16 = jnp.float32, jnp.bfloat16
@@ -30,7 +31,7 @@
 
 
 def busy(us, nbytes):
-    return cost(us * 1.1e9, nbytes)
+    return cost(us * EARLY * 1.1e9, nbytes * EARLY)
 
 
 def dsilu(value):
@@ -38,14 +39,14 @@
     return sig * (1.0 + value * (1.0 - sig))
 
 
-def by_tile(lefts, rights, left_dim):
+def by_tile(lefts, rights, left_dim, dtype=bf16):
     out = []
     for left, right in zip(lefts, rights):
         for t in range(right.shape[0] // MBLK):
             a = lax.slice_in_dim(left, t * MBLK, t * MBLK + MBLK, axis=left_dim)
             b = lax.slice_in_dim(right, t * MBLK, t * MBLK + MBLK, axis=0)
             dims = (((left_dim,), (0,)), ((), ()))
-            out.append(lax.dot_general(a, b, dims, preferred_element_type=f32).astype(bf16))
+            out.append(lax.dot_general(a, b, dims, preferred_element_type=f32).astype(dtype))
     return out
 
 
@@ -75,25 +76,46 @@
     return jnp.where(ok, pltpu.roll(ends, shift, 0), 0.0)
 
 
-def scan_kernel(
-    S, NG, ddec_h, dx_h, ds_h, bc_h, rate2, rate, y_h, gb_h, fr_h, dbc_h, drate,
-    ddec, dx, ds, bc, y, gb, fr, dbc, p_scr, bb, cb, q, sems
-):
+def scan_kernel(S, NG, mode, *refs):
+    ahead_too, back_too = mode != 2, mode != 1
+    ins, refs = refs[:4], refs[4:]
+    rate2, rate, refs = refs[0], refs[1], refs[2:]
+    kept_h = None
+    if mode == 2:
+        kept_h, refs = refs[0], refs[1:]
+    y_h = gb_h = fr_h = drate = y = gb = fr = None
+    if ahead_too:
+        y_h, refs = refs[0], refs[1:]
+    if back_too:
+        gb_h, fr_h, drate, refs = refs[0], refs[1], refs[2], refs[3:]
+    dbc_h, refs = refs[0], refs[1:]
+    if mode == 1:
+        kept_h, refs = refs[0], refs[1:]
+    ddec, dx, ds, bc, dbc, p_scr, bb, cb, q, sems, kept_sem = refs[:11]
+    refs = refs[11:]
+    if ahead_too:
+        y, refs = refs[0], refs[1:]
+    if back_too:
+        gb, fr = refs
     NN, L = rate.shape
     KT = L // 128
+    groups = NN // NG
     copies = []
-    for a, (src, dst) in enumerate(((ddec_h, ddec), (dx_h, dx), (ds_h, ds), (bc_h, bc))):
+    for a, (src, dst) in enumerate(zip(ins, (ddec, dx, ds, bc))):
         for c in range(CHUNKS):
             copies.append(
                 pltpu.make_async_copy(src.at[pl.ds(c * S, S), :], dst.at[:, c, :], sems.at[a, c])
             )
     for cp in copies:
         cp.start()
-    dbc[...] = jnp.zeros_like(dbc)
-    y[...] = jnp.zeros_like(y)
-    gb[...] = jnp.zeros_like(gb)
-    fr[...] = jnp.zeros_like(fr)
-    for cp in copies:
+    if mode == 2:
+        pltpu.make_async_copy(kept_h.at[0], p_scr, kept_sem).start()
+    for acc in (dbc, y, gb, fr):
+        if acc is not None:
+            acc[...] = jnp.zeros_like(acc)
+    at = CHUNKS if mode == 2 else 2 * CHUNKS
+    late = copies[at : at + CHUNKS]
+    for cp in copies[:at] + copies[at + CHUNKS :]:
         cp.wait()
 
     def rows(s):
@@ -124,7 +146,6 @@
         cc = lax.broadcasted_iota(jnp.int32, (NG * 128, 128), 1)
         Rb = jnp.where(cc == rr + g * NG, 1.0, 0.0).astype(bf16)
         Rc = jnp.where(cc == rr + NN + g * NG, 1.0, 0.0).astype(bf16)
-
         v = bc[...].reshape(S * CHUNKS, 128)[:, : 2 * NN]
         hi = v.astype(bf16)
         lo = (v - hi.astype(f32)).astype(bf16)
@@ -146,9 +167,6 @@
             return tuple(
                 jnp.exp2(d * r2[n]) * st[n] + x * wide(b[:, cols[n]]) for n in range(NG)
             )
-
-        st = loop(ahead, zero)
-        st = tuple(chain(st[n], total[n], False) for n in range(NG))
 
         def forward(s, st):
             d, x, b, c, dst = ddec[s], dx[s], bb[rows(s), :], cb[rows(s), :], ds[s]
@@ -163,18 +181,12 @@
             y[s] = acc
             return tuple(new)
 
-        loop(forward, st)
-        reduce(Rc)
-
         def behind(k, A):
             s = S - 1 - k
             d, c, dst = ddec[s], cb[rows(s), :], ds[s]
             return tuple(
                 jnp.exp2(d * r2[n]) * (dst * wide(c[:, cols[n]]) + A[n]) for n in range(NG)
             )
-
-        A = loop(behind, zero)
-        A = tuple(chain(A[n], total[n], True) for n in range(NG))
 
         def backward(k, carry):
             A, dr = carry
@@ -193,44 +205,93 @@
             fr[s] = fa
             return tuple(nA), tuple(ndr)
 
-        A, dr = loop(backward, (A, zero))
-        reduce(Rb)
-        for n in range(NG):
-            drate[pl.ds(g * NG + n, 1), :] = jnp.sum(dr[n], axis=0, keepdims=True)
+        if ahead_too:
+            st = loop(ahead, zero)
+            st = tuple(chain(st[n], total[n], False) for n in range(NG))
+            if mode == 1:
+
+                @pl.when(g > 0)
+                def _():
+                    pltpu.make_async_copy(p_scr, kept_h.at[g - 1], kept_sem).wait()
+
+            @pl.when(g == 0)
+            def _():
+                for cp in late:
+                    cp.wait()
+
+            loop(forward, st)
+            if mode == 1:
+                pltpu.make_async_copy(p_scr, kept_h.at[g], kept_sem).start()
+            reduce(Rc)
+        if back_too:
+            A = loop(behind, zero)
+            A = tuple(chain(A[n], total[n], True) for n in range(NG))
+            if mode == 2:
+                pltpu.make_async_copy(kept_h.at[g], p_scr, kept_sem).wait()
+
+                @pl.when(g == 0)
+                def _():
+                    for cp in late:
+                        cp.wait()
+
+            A, dr = loop(backward, (A, zero))
+            if mode == 2:
+
+                @pl.when(g + 1 < groups)
+                def _():
+                    pltpu.make_async_copy(kept_h.at[g + 1], p_scr, kept_sem).start()
+
+            reduce(Rb)
+            for n in range(NG):
+                drate[pl.ds(g * NG + n, 1), :] = jnp.sum(dr[n], axis=0, keepdims=True)
         return 0
 
-    lax.fori_loop(0, NN // NG, group, 0)
+    lax.fori_loop(0, groups, group, 0)
     copies = []
     for a, (src, dst) in enumerate(((y, y_h), (gb, gb_h), (fr, fr_h), (dbc, dbc_h))):
+        if src is None:
+            continue
         for c in range(CHUNKS):
             copies.append(
                 pltpu.make_async_copy(src.at[:, c, :], dst.at[pl.ds(c * S, S), :], sems.at[a, c])
             )
     for cp in copies:
         cp.start()
+    if mode == 1:
+        pltpu.make_async_copy(p_scr, kept_h.at[groups - 1], kept_sem).wait()
     for cp in copies:
         cp.wait()
 
 
-def scan_both(ddec, dx, ds, bc, rate, NG=4):
+def scan(mode, ddec, dx, ds, bc, rate, kept=None, NG=4):
     T, E = ddec.shape
     N = rate.shape[0]
     S = T // CHUNKS
     act = pltpu.VMEM((S, CHUNKS, E), f32)
     thin = pltpu.VMEM((S, CHUNKS, 128), f32)
+    row, states = sds((T, E), f32), sds((N // NG, S, NG, CHUNKS, E), f32)
+    outs, specs = [], []
+    if mode != 2:
+        outs, specs = outs + [row], specs + [HBM]
+    if mode != 1:
+        outs, specs = outs + [row, row, sds((N, E), f32)], specs + [HBM, HBM, VMEM]
+    outs, specs = outs + [sds((T, 128), f32)], specs + [HBM]
+    if mode == 1:
+        outs, specs = outs + [states], specs + [HBM]
     return pl.pallas_call(
-        functools.partial(scan_kernel, S, NG),
-        in_specs=[HBM] * 4 + [VMEM] * 2,
-        out_specs=[HBM] * 4 + [VMEM],
-        out_shape=[sds((T, E), f32)] * 3 + [sds((T, 128), f32), sds((N, E), f32)],
-        scratch_shapes=[act] * 3 + [thin] + [act] * 3 + [thin]
+        functools.partial(scan_kernel, S, NG, mode),
+        in_specs=[HBM] * 4 + [VMEM] * 2 + ([HBM] if mode == 2 else []),
+        out_specs=specs,
+        out_shape=outs,
+        scratch_shapes=[act] * 3 + [thin] * 2
         + [pltpu.VMEM((S, NG, CHUNKS, E), f32)]
         + [pltpu.VMEM((T, NG * 128), f32)] * 3
-        + [pltpu.SemaphoreType.DMA((4, CHUNKS))],
+        + [pltpu.SemaphoreType.DMA((4, CHUNKS)), pltpu.SemaphoreType.DMA]
+        + [act] * ((mode != 2) + 2 * (mode != 1)),
         compiler_params=pltpu.CompilerParams(vmem_limit_bytes=60 << 20),
-        cost_estimate=busy(105.0 * T * E * N / (2048 * 512 * 16), 24 * T * E),
-        name="scan_both",
-    )(ddec, dx, ds, bc, rate * LOG2E, rate)
+        cost_estimate=busy((114.0, 62.0, 68.0)[mode] * T * E * N / (2048 * 512 * 16), 24 * T * E),
+        name=("scan_both", "scan_ahead", "scan_back")[mode],
+    )(ddec, dx, ds, bc, rate * LOG2E, rate, *([kept] if mode == 2 else []))
 
 
 def sum_kernel(pairs, n, *refs):
@@ -341,6 +402,13 @@
     return lax.dot_general(a, b, (((1,), (1,)), ((), ())), preferred_element_type=f32)
 
 
+def cut(ws, dim):
+    at = 0
+    for w in ws:
+        yield slice(at, at + w.shape[dim]), w
+        at += w.shape[dim]
+
+
 def dot_tn(a, b):
     return lax.dot_general(a, b, (((0,), (0,)), ((), ())), preferred_element_type=f32)
 
@@ -358,9 +426,8 @@
 def in_kernel(taps, kinds, lens, g, xw, cw, cb, *rest):
     ws, (x_o, gate_o, xc_o, low_o, thin_o, xe) = rest[:-6], rest[-6:]
     blk = pl.program_id(0)
-    P4 = ws[0].shape[1]
     inner = cw.shape[1]
-    mixed = sum(dot(g[:, P4 * j : P4 * j + P4], w[0]) for j, w in enumerate(ws))
+    mixed = sum(dot(g[:, at], w[0]) for at, w in cut(ws, 1))
     x = mixed[:, :inner]
     x_o[...] = x
     gate_o[...] = mixed[:, inner:]
@@ -387,8 +454,7 @@
 def mid_kernel(kinds, lens, u, gate, xc, low, thin, dtw, dtb, *rest):
     ws, (ddec_o, delta_o, dx_o, ds_o, dy_o, bc_o) = rest[:-6], rest[-6:]
     blk = pl.program_id(0)
-    P4 = ws[0].shape[2]
-    dy = sum(dot_nt(u[:, P4 * j : P4 * j + P4], w[0]) for j, w in enumerate(ws))
+    dy = sum(dot_nt(u[:, at], w[0]) for at, w in cut(ws, 2))
     position, valid = places(lens, blk)
     pre = dot_tn(low[...], dtw[0]) + dtb[...]
     delta = jnp.maximum(pre, 0.0) + jnp.log1p(jnp.exp(-jnp.abs(pre)))
@@ -400,29 +466,31 @@
     bc_o[...] = jnp.concatenate([thin[...], jnp.zeros((128 - thin.shape[0], RB), f32)], axis=0).T
 
 
-def post_kernel(nbc, kinds, lens, y, gb, fr, ds, dy, gate, xc, delta, dbc, skip, dtw, *rest):
-    ws, (out_o, y_o, dgate_o, dpre_o, dxc_o, dpp_o, sum_o) = rest[:-7], rest[-7:]
-    blk = pl.program_id(0)
-    position, valid = places(lens, blk)
-    x = xc[...].astype(f32)
+def post_kernel(kinds, lens, y, dy, gate, xc, skip, *rest):
+    ws, (out_o, y_o, dgate_o) = rest[:-3], rest[-3:]
+    position, valid = places(lens, pl.program_id(0))
     z = gate[...]
-    scanned = y[...] + skip[...] * x
+    scanned = y[...] + skip[...] * xc[...].astype(f32)
     yo = (scanned * silu(z) * valid).astype(bf16)
     y_o[...] = yo
     dgate_o[...] = (dy[...] * scanned * valid * dsilu(z)).astype(bf16)
+    for at, w in cut(ws, 2):
+        out_o[:, at] = dot(yo, w[0]).astype(bf16)
+
+
+def step_kernel(nbc, kinds, lens, gb, fr, ds, xc, delta, dbc, dbc2, skip, dtw, dpre_o, dxc_o, dpp_o, sum_o):
+    x = xc[...].astype(f32)
     dl = delta[...]
     g = gb[...]
     dpre = ((x * g + fr[...]) * (1.0 - jnp.exp(-dl))).astype(bf16)
     dpre_o[...] = dpre
     dlow = dot_nt(dtw[0], dpre)
-    dpp_o[...] = jnp.concatenate([dlow, dbc[...].T[:nbc, :]], axis=0).astype(bf16)
+    both = (dbc[...] + dbc2[...]).T
+    dpp_o[...] = jnp.concatenate([dlow, both[:nbc, :]], axis=0).astype(bf16)
     d = ds[...]
     dxc_o[...] = d * skip[...] + dl * g
-    P4 = ws[0].shape[2]
-    for j, w in enumerate(ws):
-        out_o[:, P4 * j : P4 * j + P4] = dot(yo, w[0]).astype(bf16)
-
-    @pl.when(blk == 0)
+
+    @pl.when(pl.program_id(0) == 0)
     def _():
         sum_o[...] = jnp.zeros_like(sum_o)
 
@@ -460,10 +528,8 @@
     sum_o[taps : taps + 1, :] += jnp.sum(dconv, axis=0, keepdims=True)
     din_o[...] = din.astype(bf16)
     dmix = jnp.concatenate([din.astype(bf16), dgate[...]], axis=1)
-    P4 = ws[0].shape[1]
-    for j, w in enumerate(ws):
+    for at, w in cut(ws, 1):
         part = dot_nt(dmix, w[0])
-        at = slice(P4 * j, P4 * j + P4)
         dn_o[:, at] = part.astype(bf16)
         gain_o[0:1, at] += jnp.sum(part * g[:, at].astype(f32), axis=0, keepdims=True)
 
@@ -514,19 +580,20 @@
     return lax.ppermute(v, axis, [(i, i ^ bits) for i in range(n)])
 
 
-def square_gather_near(own):
-    n = lax.axis_size("seq")
-    return [own] + [swap(own, j) for j in range(1, 3 if n == 4 else n)]
-
-
-def square_gather_far(blocks):
+def gather_all(own):
+    return [own] + [swap(own, j) for j in range(1, lax.axis_size("seq"))]
+
+
+def gather_near(own):
+    return [own] + [swap(own, j) for j in range(1, 3)] if lax.axis_size("seq") == 4 else gather_all(own)
+
+
+def gather_far(blocks, dim):
     if lax.axis_size("seq") != 4:
         return blocks
     own, by_x, by_y = blocks
-    half = own.shape[1] // 2
-    first = swap(by_x[:, :half], 2)
-    second = swap(by_y[:, half:], 1)
-    return [own, by_x, by_y, jnp.concatenate([first, second], axis=1)]
+    first, second = jnp.split(by_x, 2, axis=dim)[0], jnp.split(by_y, 2, axis=dim)[1]
+    return [own, by_x, by_y, swap(first, 2), swap(second, 1)]
 
 
 def scatter_far(parts):
@@ -538,7 +605,7 @@
 
 def scatter_near(parts, far):
     if len(parts) != 4:
-        return [parts[0]] + [swap(p, j) for j, p in enumerate(parts) if j]
+        return scatter_all(parts)
     own, for_x, for_y, _ = parts
     a, b = far
     half = a.shape[1]
@@ -551,12 +618,27 @@
     return [own, swap(for_x, 1), swap(for_y, 2)]
 
 
+def scatter_all(parts):
+    return [parts[0]] + [swap(p, j) for j, p in enumerate(parts) if j]
+
+
 def total_of(terms):
     return sum(t.astype(f32) for t in terms)
 
 
 def seq_sum(v):
     return v + sum(swap(v, j) for j in range(1, lax.axis_size("seq")))
+
+
+def chan_gather(v):
+    me = lax.axis_index("chan")
+    bit = 1
+    while bit < lax.axis_size("chan"):
+        other = swap(v, bit, "chan")
+        up = (me & bit) > 0
+        v = jnp.concatenate([jnp.where(up, other, v), jnp.where(up, v, other)], axis=1)
+        bit *= 2
+    return v
 
 
 def chan_scatter(v):
@@ -599,8 +681,8 @@
     w_own, norm_gain = lax.optimization_barrier(
         (in_weight.reshape(MODES, P4, 2 * inner), norm_gain)
     )
-    w_in = square_gather_near(w_own)
-    gain = lax.all_gather(norm_gain, "chan", axis=0, tiled=True)
+    w_in = gather_near(w_own)
+    gain = chan_gather(norm_gain[None, :])[0]
     x_small = jnp.swapaxes(x_weight, 1, 2)
     ncols = x_small.shape[1]
     scales, units, normed, flipped = [], [], [], []
@@ -612,17 +694,18 @@
         flipped.append(square_order(out_grad[i], me))
         scales.append(scale)
         units.append(unit)
-    w_in = square_gather_far(w_in)
     small = jnp.concatenate([x_small, dt_weight], axis=1)
     small = jnp.concatenate([small] + [swap(small, b) for b in range(1, nseq)], axis=2)
     small = square_order(small, me)
     x_full = jnp.concatenate(jnp.split(small[:, :ncols], nseq, axis=2), axis=1)
     dt_full = jnp.concatenate(jnp.split(small[:, ncols:], nseq, axis=2), axis=1)
     rank = dt_full.shape[1]
+    w_in[1], w_in[2], x_full, dt_full = lax.optimization_barrier((w_in[1], w_in[2], x_full, dt_full))
+    w_in = gather_far(w_in, 1)
     later, w_in[-1] = lax.optimization_barrier((out_weight, w_in[-1]))
-    w_out = square_gather_near(later)
-    gathered = [lax.all_gather(normed[i], "chan", axis=0, tiled=True) for i in range(micro)]
-    ups = [lax.all_gather(flipped[i], "chan", axis=0, tiled=True) for i in range(micro)]
+    w_out = gather_near(later)
+    gathered = [lax.all_gather(normed[0], "chan", axis=0, tiled=True)]
+    ups = [lax.all_gather(flipped[0], "chan", axis=0, tiled=True)]
     win = {f"w{j}": w for j, w in enumerate(w_in)}
     ws = list(win)
     vec = dict(cw=conv_weight, cb=conv_bias[None, :])
@@ -643,7 +726,7 @@
             across=dict(dproj=d_proj),
         )
         d_ins.append(d_in)
-        t_xw.extend(by_tile([d_proj], [c["xc"]], 1))
+        t_xw.extend(by_tile([d_proj], [c["xc"]], 1, f32))
         sums.append((c["sum_a"], sum_b, c["s_rate"] * rate, sum_g[:1]))
         return dn_part
 
@@ -661,11 +744,17 @@
             out_across=((rank, bf16), (2 * nstate, f32)),
         )
         if carried is None:
-            *w_out, bc_part = lax.optimization_barrier((*w_out, bc_part))
-            wout = {f"w{j}": w for j, w in enumerate(square_gather_far(w_out))}
             low, thin = chan_sum([low_part, bc_part], 0)
+            low, normed, flipped, w_out = lax.optimization_barrier((low, normed, flipped, w_out))
+            wout = {f"w{j}": w for j, w in enumerate(gather_far(w_out, 2))}
+            wo = list(wout)
+            for j in range(1, micro):
+                gathered.append(lax.all_gather(normed[j], "chan", axis=0, tiled=True))
+                ups.append(lax.all_gather(flipped[j], "chan", axis=0, tiled=True))
         else:
             low, thin, d_proj = chan_sum([low_part, bc_part, d_part], 1)
+            low, out_part = lax.optimization_barrier((low, out_part))
+            branches.append(lax.psum_scatter(out_part, "chan", scatter_dimension=0, tiled=True))
             dn_part = finish(carried, d_proj)
             thin, dn_part = lax.optimization_barrier((thin, dn_part))
             dn_parts.append(lax.psum_scatter(dn_part, "chan", scatter_dimension=0, tiled=True))
@@ -673,37 +762,64 @@
             mid_kernel, "mid_stage", T,
             dict(u=ups[i], gate=gate, xc=xc), dict(**wout, dtw=dt_full), dict(dtb=dtb),
             [(inner, f32)] * 5 + [(128, f32)], [], [], kinds, lens, 19.0,
-            order=["u", "gate", "xc", "low", "thin", "dtw", "dtb", *ws], across=dict(low=low, thin=thin),
+            order=["u", "gate", "xc", "low", "thin", "dtw", "dtb", *wo], across=dict(low=low, thin=thin),
         )
-        y, gb, fr, dbc, s_rate = scan_both(ddec, dx, ds, bc, rate)
+        whole = i < micro - 1
+        if whole:
+            y, gb, fr, s_rate, dbc = scan(0, ddec, dx, ds, bc, rate)
+            dbc2 = jnp.zeros_like(dbc)
+        else:
+            y, dbc, kept = scan(1, ddec, dx, ds, bc, rate)
         if dn_parts:
-            dbc, branches, dn_parts = lax.optimization_barrier((dbc, branches, dn_parts))
-        out_part, y_out, d_gate, d_pre, dxc, d_part, sum_a = stage(
-            functools.partial(post_kernel, 2 * nstate), "post_stage", T,
-            dict(y=y, gb=gb, fr=fr, ds=ds, dy=dy, gate=gate, xc=xc, delta=delta, dbc=dbc),
-            dict(**wout, dtw=dt_full), dict(skip=skip),
-            [(width, bf16), (inner, bf16), (inner, bf16), (inner, bf16), (inner, f32)],
-            [(8, inner)], [], kinds, lens, 23.0,
-            order=["y", "gb", "fr", "ds", "dy", "gate", "xc", "delta", "dbc", "skip", "dtw", *ws],
+            y, branches = lax.optimization_barrier((y, branches))
+        out_part, y_out, d_gate = stage(
+            post_kernel, "post_stage", T,
+            dict(y=y, dy=dy, gate=gate, xc=xc), dict(**wout), dict(skip=skip),
+            [(width, bf16), (inner, bf16), (inner, bf16)], [], [], kinds, lens, 14.0,
+            order=["y", "dy", "gate", "xc", "skip", *wo],
+        )
+        if not whole:
+            branches.append(lax.psum_scatter(out_part, "chan", scatter_dimension=0, tiled=True))
+        t_out += by_tile([y_out], [ups[i]], 0)
+        t_gate += by_tile([gathered[i]], [d_gate], 0)
+        if not whole:
+            g_out = by_modality_blocks(flat, t_out, 1, nseq)
+            g_gate = by_modality_blocks(flat, t_gate, 0, nseq)
+            far = scatter_far(g_out)
+            t_x = by_tile(gathered[:-1], d_ins, 0)
+            bc, far, g_gate[-1], dn_parts, t_x = lax.optimization_barrier(
+                (bc, far, g_gate[-1], dn_parts, t_x)
+            )
+            g_out = scatter_near(g_out, far)
+            gb, fr, s_rate, dbc2 = scan(2, ddec, dx, ds, bc, rate, kept)
+            far = scatter_far(g_gate)
+            dbc2, far, g_out = lax.optimization_barrier((dbc2, far, g_out))
+            g_gate = scatter_near(g_gate, far)
+        d_pre, dxc, d_part, sum_a = stage(
+            functools.partial(step_kernel, 2 * nstate), "step_stage", T,
+            dict(gb=gb, fr=fr, ds=ds, xc=xc, delta=delta, dbc=dbc, dbc2=dbc2), dict(dtw=dt_full), dict(skip=skip),
+            [(inner, bf16), (inner, f32)], [(8, inner)], [], kinds, lens, 12.0,
+            order=["gb", "fr", "ds", "xc", "delta", "dbc", "dbc2", "skip", "dtw"],
             out_across=((x_full.shape[1], bf16),),
         )
-        branches.append(lax.psum_scatter(out_part, "chan", scatter_dimension=0, tiled=True))
-        t_out += by_tile([y_out], [ups[i]], 0)
-        t_gate += by_tile([gathered[i]], [d_gate], 0)
-        t_dt += by_tile([low], [d_pre], 1)
+        t_dt += by_tile([low], [d_pre], 1, f32)
         carried = dict(i=i, dxc=dxc, x=x_in, dgate=d_gate, xc=xc, sum_a=sum_a, s_rate=s_rate)
-    g_out = by_modality_blocks(flat, t_out, 1, nseq)
-    g_gate = by_modality_blocks(flat, t_gate, 0, nseq)
-    far = scatter_far(g_out)
-    d_part, far, g_gate[-1] = lax.optimization_barrier((d_part, far, g_gate[-1]))
-    g_out = scatter_near(g_out, far)
     (d_proj,) = chan_sum([d_part], 2)
-    far = scatter_far(g_gate)
-    d_proj, far, g_out = lax.optimization_barrier((d_proj, far, g_out))
-    g_gate = scatter_near(g_gate, far)
+    d_proj, g_gate = lax.optimization_barrier((d_proj, g_gate))
     dn_part = finish(carried, d_proj)
     dn_part, branches[-1] = lax.optimization_barrier((dn_part, branches[-1]))
     dn_parts.append(lax.psum_scatter(dn_part, "chan", scatter_dimension=0, tiled=True))
+    t_x += by_tile(gathered[-1:], d_ins[-1:], 0)
+    g_x = by_modality_blocks(flat, t_x, 0, nseq)
+    far = scatter_far(g_x)
+    totals = [sum(s[j] for s in sums) for j in range(4)]
+    far, t_dt, t_xw, g_out, g_gate, totals = lax.optimization_barrier(
+        (far, t_dt, t_xw, g_out, g_gate, totals)
+    )
+    g_x = scatter_near(g_x, far)
+    gain_rows = square_order(totals[3], me).reshape(-1, inner)
+    vectors = seq_sum(jnp.concatenate([*totals[:3], gain_rows], axis=0))
+    gain_total = chan_scatter(vectors[-gain_rows.shape[0] :].reshape(1, width))[0] / norm_gain
     g_dt = by_modality(flat, t_dt)
     g_xw = by_modality(flat, t_xw)
     ndt = dt_weight.shape[1]
@@ -714,17 +830,7 @@
         b = lax.dynamic_slice_in_dim(g_dt, seat * ndt, ndt, 1)
         return jnp.concatenate([a, b], axis=1)
 
-    g_small = [seat_rows(0)] + [swap(seat_rows(b), b) for b in range(1, nseq)]
-    totals = [sum(s[j] for s in sums) for j in range(4)]
-    gain_rows = square_order(totals[3], me).reshape(-1, inner)
-    vectors = seq_sum(jnp.concatenate([*totals[:3], gain_rows], axis=0))
-    gain_total = chan_scatter(vectors[-gain_rows.shape[0] :].reshape(1, width))[0] / norm_gain
-    last_in, g_gate, vectors, g_small = lax.optimization_barrier((d_ins[-1], g_gate, vectors, g_small))
-    for i in range(micro):
-        t_x += by_tile([gathered[i]], [last_in if i == micro - 1 else d_ins[i]], 0)
-    g_x = by_modality_blocks(flat, t_x, 0, nseq)
-    g_x = scatter_near(g_x, scatter_far(g_x))
-    g_out, g_gate, g_x = total_of(g_out), total_of(g_gate), total_of(g_x)
+    g_small = scatter_all([seat_rows(b) for b in range(nseq)])
     outputs, input_grads = [], []
     for i in range(micro):
         branch = square_order(branches[i].astype(f32), me)
@@ -734,11 +840,18 @@
             scales[i] * (d_unit - units[i] * jnp.mean(d_unit * units[i], axis=1, keepdims=True))
             + out_grad[i].astype(f32)
         )
-    g_small = total_of(g_small)
+    outputs, input_grads = jnp.stack(outputs, axis=0), jnp.stack(input_grads, axis=0)
+    g_out, g_gate, g_small = total_of(g_out), total_of(g_gate), total_of(g_small)
+    g_x, outputs, input_grads, g_out, g_gate = lax.optimization_barrier(
+        (g_x, outputs, input_grads, g_out, g_gate)
+    )
+    g_x = total_of(g_x)
+    is_x = lax.broadcasted_iota(jnp.int32, (1, 1, 2, 1), 2) == 0
+    g_in = jnp.where(is_x, g_x[:, :, None, :], g_gate[:, :, None, :])
     return (
-        jnp.stack(outputs, axis=0),
-        jnp.stack(input_grads, axis=0),
-        jnp.stack([g_x, g_gate], axis=2),
+        outputs,
+        input_grads,
+        g_in,
         jnp.swapaxes(g_small[:, :ncols], 1, 2),
         g_small[:, ncols:],
         g_out,

time: 984 us -> 934 us (0.949); the launches traced: 971 us -> 932 us
  waiting for transfers between devices: 195 us -> 153 us
  other arithmetic: 58.9 us -> 82.1 us
  blocking collectives: 13.4 us -> 0 us
    ppermute x32 -> x35, waiting for transfers between devices: 194 us -> 142 us  [swap(): return lax.ppermute(v, axis, [(i, i ^ bits) for i in range(n)])]
    pallas_call x3, Pallas kernels: 139 us -> 92.7 us  [chan_sum(): pl.pallas_call(functools.partial(sum_kernel, pairs, n), in_specs=[VMEM] *...]
    pallas_call x8 -> x10, Pallas kernels: 168 us -> 188 us  [stage(): pl.pallas_call(kernel, grid_spec=pltpu.PrefetchScalarGridSpec(num_scalar_...]
    pallas_call x2 -> x3, Pallas kernels: 227 us -> 246 us  [scan(): pl.pallas_call(functools.partial(scan_kernel, S, NG, mode), in_specs=[HBM...]
    all_gather x1 -> x0, blocking collectives: 13.4 us -> none  [shards(): gain = lax.all_gather(norm_gain, 'chan', axis=0, tiled=True)]
    unnamed x212 -> x199, local copies, waits for them, and re-layouts: 35.7 us -> 25.1 us
    reduce_scatter x2, waiting for transfers between devices: 0.02 us -> 10.3 us  [shards(): lax.psum_scatter(dn_part, 'chan', scatter_dimension=0, tiled=True)]
    another operation x31 -> x34, other arithmetic: 18.8 us -> 25 us  [by_modality(): return jnp.stack(out)]
  transfers between devices with their start and end apart: 40 -> 43, of which waited for: 14 -> 15; matrix products, arithmetic and copies ran while one was open for 12% -> 15% of each run, Pallas kernels for 53% -> 57%
where the time goes in v2:
time: 934 us; the launch traced here: 932 us
  Pallas kernels  527 us (56%)
  waiting for transfers between devices  153 us (16%)
  other arithmetic  82.1 us (9%)
  matrix products  50.3 us (5%)
  starting transfers between devices  48.1 us (5%)
  local copies, waits for them, and re-layouts  48 us (5%)
  between operations  23.9 us (3%)
    pallas_call x3, Pallas kernels, scan(): pl.pallas_call(functools.partial(scan_kernel, S, NG, mode), in_specs=[HBM...  246 us
    pallas_call x10, Pallas kernels, stage(): pl.pallas_call(kernel, grid_spec=pltpu.PrefetchScalarGridSpec(num_scalar_...  188 us
    ppermute x35, waiting for transfers between devices, swap(): return lax.ppermute(v, axis, [(i, i ^ bits) for i in range(n)])  142 us
    pallas_call x3, Pallas kernels, chan_sum(): pl.pallas_call(functools.partial(sum_kernel, pairs, n), in_specs=[VMEM] *...  92.7 us
    dot_general x20, matrix products, by_tile(): lax.dot_general(a, b, dims, preferred_element_type=f32).astype(dtype)  50.3 us
    ppermute x35, starting transfers between devices, swap(): return lax.ppermute(v, axis, [(i, i ^ bits) for i in range(n)])  47.1 us
    unnamed x199, local copies, waits for them, and re-layouts  25.1 us
    another operation x34, other arithmetic, by_modality(): return jnp.stack(out)  25 us
  transfers between devices with their start and end apart: 43, of which 15 were waited for; matrix products, arithmetic and copies ran while one was open for 15% of the time, Pallas kernels for 57%

profile of v2, /device:TPU:0, one launch (start us, length us, event | category | flops | bytes accessed | tf_op | source)
XLA Modules:
  0.0 932.1 jit_solution(7770543460202620926)
XLA Ops:
  7.2 4.7 reshape.304.rest_0_
  13.3 3.0 collective-permute-start.1
  18.3 2.7 collective-permute-start.2
  22.9 2.9 fusion.70
  27.1 2.7 slice_bitcast_fusion
  35.4 2.4 collective-permute-start.5
  37.8 70.5 %collective-permute-done.7 = bf16[3,72,512]{2,1,0:T(8,128)(2,1)S(1)} collective-permute-done((bf16[3,72,512]{2,1,0:T(8,128)(2,1)S(1)}, bf16[3,72,512]{2,1,0:T(8,128)(2,1)S(1)}, u32[]{:S(2)}, u32[]{:S(2)}) %collective-permute-start.7) | collective-permute-done | bytes 221216 | tf_op jit(solution)/shard_map/ppermute | solution.py:580
  119.9 27.0 %collective-permute-done.9.rest_4_ = bf16[3,256,1024]{2,1,0:T(8,128)(2,1)} collective-permute-done((bf16[3,256,1024]{2,1,0:T(8,128)(2,1)S(1)}, bf16[3,256,1024]{2,1,0:T(8,128)(2,1)}, u32[]{:S(2)}, u32[]{:S(2)}) %collective-permute-start.9) | collective-permute-done | bytes 1572896 | tf_op jit(solution)/shard_map/ppermute | solution.py:580
  153.5 19.6 %in_stage.2 = (f32[2048,512]{1,0:T(8,128)}, f32[2048,512]{1,0:T(8,128)}, bf16[2048,512]{1,0:T(8,128)(2,1)}, bf16[128,2048]{1,0:T(8,128)(2,1)}, f32[32,2048]{1,0:T(8,128)}) custom-call(s32[2]{0:T(128)} %get-tuple-element.394.kinds, s32[5]{0:T(128)} %get-tuple-element.392.lens, bf16[2048,2048]{1,0:T(8,128)(2,1)} %all-gather.5.cloned.1.call-done.g, ...), custom_call_target="tpu_custom_call" | custom-call | flops 4620000256 | bytes 4194304 | tf_op jit(solution)/shard_map/in_stage/pallas_call | solution.py:562
  175.1 33.9 %chan_sum.3 = (bf16[128,2048]{1,0:T(8,128)(2,1)S(1)}, f32[32,2048]{1,0:T(8,128)S(1)}) custom-call(bf16[128,2048]{1,0:T(8,128)(2,1)S(1)} %copy-done.13, f32[32,2048]{1,0:T(8,128)S(1)} %copy-done.15), custom_call_target="tpu_custom_call" | custom-call | flops 5720000000 | bytes 1638 | tf_op jit(solution)/shard_map/chan_sum/pallas_call | solution.py:364
  217.0 16.5 %collective-permute-done.13.rest_4_ = bf16[3,512,256]{2,1,0:T(8,128)(2,1)} collective-permute-done((bf16[3,512,256]{2,1,0:T(8,128)(2,1)}, bf16[3,512,256]{2,1,0:T(8,128)(2,1)}, u32[]{:S(2)}, u32[]{:S(2)}) %collective-permute-start.13) | collective-permute-done | bytes 786464 | tf_op jit(solution)/shard_map/ppermute | solution.py:580
  235.5 17.3 %mid_stage.2 = (f32[2048,512]{1,0:T(8,128)}, f32[2048,512]{1,0:T(8,128)}, f32[2048,512]{1,0:T(8,128)}, f32[2048,512]{1,0:T(8,128)}, f32[2048,512]{1,0:T(8,128)}, /*index=5*/f32[2048,128]{1,0:T(8,128)}) custom-call(s32[2]{0:T(128)} %get-tuple-element.394.kinds, s32[5]{0:T(128)} %get-tuple-element.392.lens, ...), custom_call_target="tpu_custom_call" | custom-call | flops 4180000000 | bytes 7340032 | tf_op jit(solution)/shard_map/mid_stage/pallas_call | solution.py:562
  252.8 113.5 %scan_both.1 = (f32[2048,512]{1,0:T(8,128)}, f32[2048,512]{1,0:T(8,128)}, f32[2048,512]{1,0:T(8,128)}, f32[16,512]{1,0:T(8,128)}, f32[2048,128]{1,0:T(8,128)}) custom-call(f32[2048,512]{1,0:T(8,128)} %get-tuple-element.161.refs_0_, f32[2048,512]{1,0:T(8,128)} %get-tuple-element.162.refs_1_, f32[2048,512]{1,0:T(8,128)} %get-tuple-element.163.refs_2_.ds, ...), custom_call_target="tpu_custom_call" | custom-call | flops 25080000512 | bytes 5033164 | tf_op jit(solution)/shard_map/scan_both/pallas_call | solution.py:281
  367.4 11.6 %step_stage.2 = (bf16[2048,512]{1,0:T(8,128)(2,1)}, f32[2048,512]{1,0:T(8,128)}, bf16[160,2048]{1,0:T(8,128)(2,1)}, f32[8,512]{1,0:T(8,128)}) custom-call(s32[2]{0:T(128)} %get-tuple-element.394.kinds, s32[5]{0:T(128)} %get-tuple-element.392.lens, f32[2048,512]{1,0:T(8,128)} %get-tuple-element.165.gb, f32[2048,512]{1,0:T(8,128)} %get-tuple-element.166.fr, ...), custom_call_target="tpu_custom_call" | custom-call | flops 2640000000 | bytes 5872025 | tf_op jit(solution)/shard_map/step_stage/pallas_call | solution.py:562
  379.0 14.5 %post_stage.2 = (bf16[2048,2048]{1,0:T(8,128)(2,1)}, bf16[2048,512]{1,0:T(8,128)(2,1)}, bf16[2048,512]{1,0:T(8,128)(2,1)}) custom-call(s32[2]{0:T(128)} %get-tuple-element.394.kinds, s32[5]{0:T(128)} %get-tuple-element.392.lens, f32[2048,512]{1,0:T(8,128)} %get-tuple-element.177.y, f32[2048,512]{1,0:T(8,128)} %get-tuple-element.178.dy, ...), custom_call_target="tpu_custom_call" | custom-call | flops 3080000000 | bytes 7969177 | tf_op jit(solution)/shard_map/post_stage/pallas_call | solution.py:562
  393.6 31.7 %in_stage.3 = (f32[2048,512]{1,0:T(8,128)}, f32[2048,512]{1,0:T(8,128)}, bf16[2048,512]{1,0:T(8,128)(2,1)}, bf16[128,2048]{1,0:T(8,128)(2,1)}, f32[32,2048]{1,0:T(8,128)}) custom-call(s32[2]{0:T(128)} %get-tuple-element.393.kinds, s32[5]{0:T(128)} %get-tuple-element.391.lens, bf16[2048,2048]{1,0:T(8,128)(2,1)} %all-gather.9.cloned.1.call-done.g, ...), custom_call_target="tpu_custom_call" | custom-call | flops 4620000256 | bytes 4194304 | tf_op jit(solution)/shard_map/in_stage/pallas_call | solution.py:562
  427.3 38.6 %chan_sum.4 = (bf16[128,2048]{1,0:T(8,128)(2,1)S(1)}, f32[32,2048]{1,0:T(8,128)S(1)}, bf16[160,2048]{1,0:T(8,128)(2,1)S(1)}) custom-call(bf16[128,2048]{1,0:T(8,128)(2,1)S(1)} %copy-done.12, f32[32,2048]{1,0:T(8,128)S(1)} %copy-done.14, bf16[160,2048]{1,0:T(8,128)(2,1)S(1)} %copy-done.10), custom_call_target="tpu_custom_call" | custom-call | flops 5720000000 | bytes 1638 | tf_op jit(solution)/shard_map/chan_sum/pallas_call | solution.py:364
  468.3 25.4 %back_stage.2 = (bf16[2048,512]{1,0:T(8,128)(2,1)}, bf16[2048,2048]{1,0:T(8,128)(2,1)}, f32[8,512]{1,0:T(8,128)}, f32[8,2048]{1,0:T(8,128)}) custom-call(s32[2]{0:T(128)} %get-tuple-element.394.kinds, s32[5]{0:T(128)} %get-tuple-element.392.lens, bf16[160,2048]{1,0:T(8,128)(2,1)} %copy-done, bf16[3,160,512]{2,1,0:T(8,128)(2,1)} %pad_maximum_fusion.24.xw, ...), custom_call_target="tpu_custom_call" | custom-call | flops 5720000000 | bytes 7969177 | tf_op jit(solution)/shard_map/back_stage/pallas_call | solution.py:562
  502.3 5.0 fusion.51
  507.3 16.3 %mid_stage.3 = (f32[2048,512]{1,0:T(8,128)}, f32[2048,512]{1,0:T(8,128)}, f32[2048,512]{1,0:T(8,128)}, f32[2048,512]{1,0:T(8,128)}, f32[2048,512]{1,0:T(8,128)}, /*index=5*/f32[2048,128]{1,0:T(8,128)}) custom-call(s32[2]{0:T(128)} %get-tuple-element.393.kinds, s32[5]{0:T(128)} %get-tuple-element.391.lens, bf16[2048,2048]{1,0:T(8,128)(2,1)} %all-gather.7.cloned.1.call-done.u, ...), custom_call_target="tpu_custom_call" | custom-call | flops 4180000000 | bytes 7340032 | tf_op jit(solution)/shard_map/mid_stage/pallas_call | solution.py:562
  523.6 59.4 %scan_ahead.1 = (f32[2048,512]{1,0:T(8,128)}, f32[2048,128]{1,0:T(8,128)}, f32[4,256,4,8,512]{4,3,2,1,0:T(8,128)}) custom-call(f32[2048,512]{1,0:T(8,128)} %get-tuple-element.190.refs_0_, f32[2048,512]{1,0:T(8,128)} %get-tuple-element.191.refs_1_, f32[2048,512]{1,0:T(8,128)} %get-tuple-element.192.refs_2_.ds, f32[2048,128]{1,0:T(8,128)} %get-tuple-element.203.refs_3_, ...), custom_call_target="tpu_custom_call" | custom-call | flops 13639999488 | bytes 5033164 | tf_op jit(solution)/shard_map/scan_ahead/pallas_call | solution.py:281
  583.1 14.1 %post_stage.3 = (bf16[2048,2048]{1,0:T(8,128)(2,1)}, bf16[2048,512]{1,0:T(8,128)(2,1)}, bf16[2048,512]{1,0:T(8,128)(2,1)}) custom-call(s32[2]{0:T(128)} %get-tuple-element.393.kinds, s32[5]{0:T(128)} %get-tuple-element.391.lens, f32[2048,512]{1,0:T(8,128)} %get-tuple-element.195.y, f32[2048,512]{1,0:T(8,128)} %get-tuple-element.196.dy, ...), custom_call_target="tpu_custom_call" | custom-call | flops 3080000000 | bytes 7969177 | tf_op jit(solution)/shard_map/post_stage/pallas_call | solution.py:562
  597.7 5.1 fusion.48
  602.8 4.7 fusion.42
  607.6 2.4 fusion.36
  610.0 3.7 fusion.45
  613.7 3.7 fusion.39
  617.4 2.6 fusion.57
  620.0 2.4 fusion.54
  631.4 3.1 collective-permute-start.15
  634.6 2.4 fusion.30
  637.0 2.6 fusion.24
  665.3 73.3 %scan_back.1 = (f32[2048,512]{1,0:T(8,128)}, f32[2048,512]{1,0:T(8,128)}, f32[16,512]{1,0:T(8,128)}, f32[2048,128]{1,0:T(8,128)}) custom-call(f32[2048,512]{1,0:T(8,128)} %get-tuple-element.190.refs_0_, f32[2048,512]{1,0:T(8,128)} %get-tuple-element.191.refs_1_, f32[2048,512]{1,0:T(8,128)} %get-tuple-element.192.refs_2_.ds, ...), custom_call_target="tpu_custom_call" | custom-call | flops 14960000000 | bytes 5033164 | tf_op jit(solution)/shard_map/scan_back/pallas_call | solution.py:281
  745.0 11.4 %step_stage.3 = (bf16[2048,512]{1,0:T(8,128)(2,1)}, f32[2048,512]{1,0:T(8,128)}, bf16[160,2048]{1,0:T(8,128)(2,1)}, f32[8,512]{1,0:T(8,128)}) custom-call(s32[2]{0:T(128)} %get-tuple-element.393.kinds, s32[5]{0:T(128)} %get-tuple-element.391.lens, f32[2048,512]{1,0:T(8,128)} %get-tuple-element.205.gb, f32[2048,512]{1,0:T(8,128)} %get-tuple-element.206.fr, ...), custom_call_target="tpu_custom_call" | custom-call | flops 2640000000 | bytes 5872025 | tf_op jit(solution)/shard_map/step_stage/pallas_call | solution.py:562
  757.6 20.2 %chan_sum.5.dproj = bf16[160,2048]{1,0:T(8,128)(2,1)S(1)} custom-call(bf16[160,2048]{1,0:T(8,128)(2,1)S(1)} %copy-done.11), custom_call_target="tpu_custom_call" | custom-call | flops 5720000000 | bytes 1638 | tf_op jit(solution)/shard_map/chan_sum/pallas_call | solution.py:364
  781.1 25.7 %back_stage.3 = (bf16[2048,512]{1,0:T(8,128)(2,1)}, bf16[2048,2048]{1,0:T(8,128)(2,1)}, f32[8,512]{1,0:T(8,128)}, f32[8,2048]{1,0:T(8,128)}) custom-call(s32[2]{0:T(128)} %get-tuple-element.393.kinds, s32[5]{0:T(128)} %get-tuple-element.391.lens, bf16[160,2048]{1,0:T(8,128)(2,1)} %copy-done.2, bf16[3,160,512]{2,1,0:T(8,128)(2,1)} %pad_maximum_fusion.24.xw, ...), custom_call_target="tpu_custom_call" | custom-call | flops 5720000000 | bytes 7969177 | tf_op jit(solution)/shard_map/back_stage/pallas_call | solution.py:562
  810.1 2.3 fusion.242
  822.5 2.4 fusion.33
  824.9 2.4 fusion.27
  842.3 6.7 collective-permute-done.23
  862.2 4.3 convert_add_fusion.4
  869.2 3.1 collective-permute-start.32
  872.3 2.3 convert_add_fusion.3
  874.7 2.3 collective-permute-start.33
  888.2 10.3 %reduce-scatter.11.cloned.1.call-done = bf16[256,2048]{1,0:T(8,128)(2,1)} async-done(((bf16[2048,2048]{1,0:T(8,128)(2,1)}), bf16[256,2048]{1,0:T(8,128)(2,1)}) %reduce-scatter.11.cloned.1.call-update) | async-done | bytes 1048592 | tf_op jit(solution)/shard_map/reduce_scatter | solution.py:811
  906.8 10.4 %collective-permute-done.24 = bf16[3,512,512]{2,1,0:T(8,128)(2,1)} collective-permute-done((bf16[3,512,512]{2,1,0:T(8,128)(2,1)}, bf16[3,512,512]{2,1,0:T(8,128)(2,1)}, u32[]{:S(2)}, u32[]{:S(2)}) %collective-permute-start.24) | collective-permute-done | bytes 1572896 | tf_op jit(solution)/shard_map/ppermute | solution.py:580
  917.2 2.5 convert_add_fusion.2
  919.7 5.3 broadcast_select_fusion
  (431 shorter events, 157.0 us)
Async XLA Ops:
  7.2 146.3 %all-gather.5.cloned.1.call-start = ((), (), s32[]{:S(2)}) async-start(), calls=%async_computation.4 | async-start | bytes 9437184 | tf_op jit(solution)/shard_map/all_gather | solution.py:707
  11.9 20.8 %copy-start.16 = (bf16[3,512,1024]{2,1,0:T(8,128)(2,1)}, bf16[3,512,1024]{2,1,0:T(8,128)(2,1)S(1)}, u32[]{:S(2)}) copy-start(bf16[3,512,1024]{2,1,0:T(8,128)(2,1)S(1)} %reshape.304.rest_0_) | copy-start | bytes 9437188
  11.9 1.3 collective-permute-start
  13.3 5.0 collective-permute-start.1
  18.3 4.6 collective-permute-start.2
  27.1 189.9 %all-gather.11.cloned.1.call-start = ((), (), s32[]{:S(2)}) async-start(), calls=%async_computation.7 | async-start | bytes 9437184 | tf_op jit(solution)/shard_map/all_gather | solution.py:708
  31.1 362.5 %all-gather.9.cloned.1.call-start = ((), (), s32[]{:S(2)}) async-start(), calls=%async_computation.6 | async-start | bytes 9437184 | tf_op jit(solution)/shard_map/all_gather | solution.py:752
  31.1 81.4 %collective-permute-start.4 = (bf16[3,512,1024]{2,1,0:T(8,128)(2,1)S(1)}, bf16[3,512,1024]{2,1,0:T(8,128)(2,1)S(1)}, u32[]{:S(2)}, u32[]{:S(2)}) collective-permute-start(bf16[3,512,1024]{2,1,0:T(8,128)(2,1)S(1)} %reshape.304.rest_0_), channel_id=1, source_target_pairs={{0,16},{8,24},{16,0},{24,8},{1,17},{9,25},{17,1},{25,9},{2,18},{10... | collective-permute-start | bytes 9437192 | tf_op jit(solution)/shard_map/ppermute | solution.py:580
  32.7 79.9 %collective-permute-start.3 = (bf16[3,512,1024]{2,1,0:T(8,128)(2,1)S(1)}, bf16[3,512,1024]{2,1,0:T(8,128)(2,1)S(1)}, u32[]{:S(2)}, u32[]{:S(2)}) collective-permute-start(bf16[3,512,1024]{2,1,0:T(8,128)(2,1)S(1)} %reshape.304.rest_0_), channel_id=1, source_target_pairs={{0,8},{8,0},{16,24},{24,16},{1,9},{9,1},{17,25},{25,17},{2,10},{10... | collective-permute-start | bytes 9437192 | tf_op jit(solution)/shard_map/ppermute | solution.py:580
  34.2 74.1 %collective-permute-start.7 = (bf16[3,72,512]{2,1,0:T(8,128)(2,1)S(1)}, bf16[3,72,512]{2,1,0:T(8,128)(2,1)S(1)}, u32[]{:S(2)}, u32[]{:S(2)}) collective-permute-start(bf16[3,72,512]{2,1,0:T(8,128)(2,1)S(1)} %pad_maximum_fusion.28), channel_id=1, source_target_pairs={{0,8},{8,0},{16,24},{24,16},{1,9},{9,1},{17,25},{25,17},{2,10},{10... | collective-permute-start | bytes 663560 | tf_op jit(solution)/shard_map/ppermute | solution.py:580
  34.9 73.5 %collective-permute-start.6 = (bf16[3,72,512]{2,1,0:T(8,128)(2,1)S(1)}, bf16[3,72,512]{2,1,0:T(8,128)(2,1)S(1)}, u32[]{:S(2)}, u32[]{:S(2)}) collective-permute-start(bf16[3,72,512]{2,1,0:T(8,128)(2,1)S(1)} %pad_maximum_fusion.28), channel_id=1, source_target_pairs={{0,16},{8,24},{16,0},{24,8},{1,17},{9,25},{17,1},{25,9},{2,18},{10... | collective-permute-start | bytes 663560 | tf_op jit(solution)/shard_map/ppermute | solution.py:580
  35.4 75.3 %collective-permute-start.5 = (bf16[3,72,512]{2,1,0:T(8,128)(2,1)S(1)}, bf16[3,72,512]{2,1,0:T(8,128)(2,1)S(1)}, u32[]{:S(2)}, u32[]{:S(2)}) collective-permute-start(bf16[3,72,512]{2,1,0:T(8,128)(2,1)S(1)} %pad_maximum_fusion.28), channel_id=1, source_target_pairs={{0,24},{8,16},{16,8},{24,0},{1,25},{9,17},{17,9},{25,1},{2,26},{10... | collective-permute-start | bytes 663560 | tf_op jit(solution)/shard_map/ppermute | solution.py:580
  112.8 34.1 %collective-permute-start.9 = (bf16[3,256,1024]{2,1,0:T(8,128)(2,1)S(1)}, bf16[3,256,1024]{2,1,0:T(8,128)(2,1)}, u32[]{:S(2)}, u32[]{:S(2)}) collective-permute-start(bf16[3,256,1024]{2,1,0:T(8,128)(2,1)S(1)} %split.319), channel_id=1, source_target_pairs={{0,8},{8,0},{16,24},{24,16},{1,9},{9,1},{17,25},{25,17},{2,10},{10... | collective-permute-start | bytes 4718600 | tf_op jit(solution)/shard_map/ppermute | solution.py:580
  115.8 37.6 %collective-permute-start.8 = (bf16[3,256,1024]{2,1,0:T(8,128)(2,1)}, bf16[3,256,1024]{2,1,0:T(8,128)(2,1)}, u32[]{:S(2)}, u32[]{:S(2)}) collective-permute-start(bf16[3,256,1024]{2,1,0:T(8,128)(2,1)} %split.318), channel_id=1, source_target_pairs={{0,16},{8,24},{16,0},{24,8},{1,17},{9,25},{17,1},{25,9},{2,18},{10... | collective-permute-start | bytes 4718600 | tf_op jit(solution)/shard_map/ppermute | solution.py:580
  118.7 31.3 %copy-start.83 = (s32[2,1,5]{2,1,0:T(1,128)S(1)}, s32[2,1,5]{2,1,0:T(1,128)}, u32[]{:S(2)}) copy-start(s32[2,1,5]{2,1,0:T(1,128)} %param.17) | copy-start | bytes 124
  146.9 63.6 %collective-permute-start.11 = (bf16[3,512,512]{2,1,0:T(8,128)(2,1)}, bf16[3,512,512]{2,1,0:T(8,128)(2,1)S(1)}, u32[]{:S(2)}, u32[]{:S(2)}) collective-permute-start(bf16[3,512,512]{2,1,0:T(8,128)(2,1)} %rest_0_.3), channel_id=1, source_target_pairs={{0,16},{8,24},{16,0},{24,8},{1,17},{9,25},{17,1},{25,9},{2,18},{10... | collective-permute-start | bytes 4718600 | tf_op jit(solution)/shard_map/ppermute | solution.py:580
  148.5 62.1 %collective-permute-start.10 = (bf16[3,512,512]{2,1,0:T(8,128)(2,1)}, bf16[3,512,512]{2,1,0:T(8,128)(2,1)S(1)}, u32[]{:S(2)}, u32[]{:S(2)}) collective-permute-start(bf16[3,512,512]{2,1,0:T(8,128)(2,1)} %rest_0_.3), channel_id=1, source_target_pairs={{0,8},{8,0},{16,24},{24,16},{1,9},{9,1},{17,25},{25,17},{2,10},{10... | collective-permute-start | bytes 4718600 | tf_op jit(solution)/shard_map/ppermute | solution.py:580
  210.6 296.7 %all-gather.7.cloned.1.call-start = ((), (), s32[]{:S(2)}) async-start(), calls=%async_computation.5 | async-start | bytes 9437184 | tf_op jit(solution)/shard_map/all_gather | solution.py:753
  211.2 371.9 %reduce-scatter.5.cloned.1.call-start = ((), (), s32[]{:S(2)}) async-start(), calls=%async_computation.8 | async-start | bytes 9437184 | tf_op jit(solution)/shard_map/reduce_scatter | solution.py:757
  213.4 20.1 %collective-permute-start.13 = (bf16[3,512,256]{2,1,0:T(8,128)(2,1)}, bf16[3,512,256]{2,1,0:T(8,128)(2,1)}, u32[]{:S(2)}, u32[]{:S(2)}) collective-permute-start(bf16[3,512,256]{2,1,0:T(8,128)(2,1)} %split.333), channel_id=1, source_target_pairs={{0,8},{8,0},{16,24},{24,16},{1,9},{9,1},{17,25},{25,17},{2,10},{10... | collective-permute-start | bytes 2359304 | tf_op jit(solution)/shard_map/ppermute | solution.py:580
  214.9 19.7 %collective-permute-start.12 = (bf16[3,512,256]{2,1,0:T(8,128)(2,1)}, bf16[3,512,256]{2,1,0:T(8,128)(2,1)S(1)}, u32[]{:S(2)}, u32[]{:S(2)}) collective-permute-start(bf16[3,512,256]{2,1,0:T(8,128)(2,1)} %split.332), channel_id=1, source_target_pairs={{0,16},{8,24},{16,0},{24,8},{1,17},{9,25},{17,1},{25,9},{2,18},{10... | collective-permute-start | bytes 2359304 | tf_op jit(solution)/shard_map/ppermute | solution.py:580
  393.6 31.7 %copy-start.10 = (bf16[160,2048]{1,0:T(8,128)(2,1)S(1)}, bf16[160,2048]{1,0:T(8,128)(2,1)}, u32[]{:S(2)}) copy-start(bf16[160,2048]{1,0:T(8,128)(2,1)} %get-tuple-element.175.refs_2_) | copy-start | bytes 1966084
  468.3 183.3 %reduce-scatter.7.cloned.1.call-start = ((), (), s32[]{:S(2)}) async-start(), calls=%async_computation.9 | async-start | bytes 9437184 | tf_op jit(solution)/shard_map/reduce_scatter | solution.py:760
  493.8 313.0 %reduce-scatter.9.cloned.1.call-start = ((), (), s32[]{:S(2)}) async-start(), calls=%async_computation.10 | async-start | bytes 9437184 | tf_op jit(solution)/shard_map/reduce_scatter | solution.py:782
  597.2 301.2 %reduce-scatter.11.cloned.1.call-start = ((), (), s32[]{:S(2)}) async-start(), calls=%async_computation.11 | async-start | bytes 9437184 | tf_op jit(solution)/shard_map/reduce_scatter | solution.py:811
  631.4 21.2 %collective-permute-start.15 = (bf16[3,256,512]{2,1,0:T(8,128)(2,1)}, bf16[3,256,512]{2,1,0:T(8,128)(2,1)}, u32[]{:S(2)}, u32[]{:S(2)}) collective-permute-start(bf16[3,256,512]{2,1,0:T(8,128)(2,1)} %get-tuple-element.338), channel_id=1, source_target_pairs={{0,16},{8,24},{16,0},{24,8},{1,17},{9,25},{17,1},{25,9},{2,18},{10... | collective-permute-start | bytes 2359304 | tf_op jit(solution)/shard_map/ppermute | solution.py:580
  634.6 19.6 %collective-permute-start.14 = (bf16[3,256,512]{2,1,0:T(8,128)(2,1)}, bf16[3,256,512]{2,1,0:T(8,128)(2,1)}, u32[]{:S(2)}, u32[]{:S(2)}) collective-permute-start(bf16[3,256,512]{2,1,0:T(8,128)(2,1)} %get-tuple-element.339), channel_id=1, source_target_pairs={{0,8},{8,0},{16,24},{24,16},{1,9},{9,1},{17,25},{25,17},{2,10},{10... | collective-permute-start | bytes 2359304 | tf_op jit(solution)/shard_map/ppermute | solution.py:580
  657.2 81.5 %collective-permute-start.18 = (bf16[3,512,512]{2,1,0:T(8,128)(2,1)}, bf16[3,512,512]{2,1,0:T(8,128)(2,1)}, u32[]{:S(2)}, u32[]{:S(2)}) collective-permute-start(bf16[3,512,512]{2,1,0:T(8,128)(2,1)} %pad_maximum_fusion.6), channel_id=1, source_target_pairs={{0,8},{8,0},{16,24},{24,16},{1,9},{9,1},{17,25},{25,17},{2,10},{10... | collective-permute-start | bytes 4718600 | tf_op jit(solution)/shard_map/ppermute | solution.py:580
  660.6 78.1 %collective-permute-start.19 = (bf16[3,512,512]{2,1,0:T(8,128)(2,1)}, bf16[3,512,512]{2,1,0:T(8,128)(2,1)}, u32[]{:S(2)}, u32[]{:S(2)}) collective-permute-start(bf16[3,512,512]{2,1,0:T(8,128)(2,1)} %pad_maximum_fusion.8), channel_id=1, source_target_pairs={{0,16},{8,24},{16,0},{24,8},{1,17},{9,25},{17,1},{25,9},{2,18},{10... | collective-permute-start | bytes 4718600 | tf_op jit(solution)/shard_map/ppermute | solution.py:580
  662.6 76.0 %collective-permute-start.17 = (bf16[3,256,512]{2,1,0:T(8,128)(2,1)}, bf16[3,256,512]{2,1,0:T(8,128)(2,1)}, u32[]{:S(2)}, u32[]{:S(2)}) collective-permute-start(bf16[3,256,512]{2,1,0:T(8,128)(2,1)} %get-tuple-element.336), channel_id=1, source_target_pairs={{0,16},{8,24},{16,0},{24,8},{1,17},{9,25},{17,1},{25,9},{2,18},{10... | collective-permute-start | bytes 2359304 | tf_op jit(solution)/shard_map/ppermute | solution.py:580
  664.0 74.7 %collective-permute-start.16 = (bf16[3,256,512]{2,1,0:T(8,128)(2,1)}, bf16[3,256,512]{2,1,0:T(8,128)(2,1)}, u32[]{:S(2)}, u32[]{:S(2)}) collective-permute-start(bf16[3,256,512]{2,1,0:T(8,128)(2,1)} %get-tuple-element.337), channel_id=1, source_target_pairs={{0,8},{8,0},{16,24},{24,16},{1,9},{9,1},{17,25},{25,17},{2,10},{10... | collective-permute-start | bytes 2359304 | tf_op jit(solution)/shard_map/ppermute | solution.py:580
  740.2 38.4 %collective-permute-start.20 = (bf16[3,512,512]{2,1,0:T(8,128)(2,1)S(1)}, bf16[3,512,512]{2,1,0:T(8,128)(2,1)S(1)}, u32[]{:S(2)}, u32[]{:S(2)}) collective-permute-start(bf16[3,512,512]{2,1,0:T(8,128)(2,1)S(1)} %pad_maximum_fusion.11), channel_id=1, source_target_pairs={{0,8},{8,0},{16,24},{24,16},{1,9},{9,1},{17,25},{25,17},{2,10},{10... | collective-permute-start | bytes 4718600 | tf_op jit(solution)/shard_map/ppermute | solution.py:580
  742.5 36.2 %collective-permute-start.21 = (bf16[3,512,512]{2,1,0:T(8,128)(2,1)S(1)}, bf16[3,512,512]{2,1,0:T(8,128)(2,1)S(1)}, u32[]{:S(2)}, u32[]{:S(2)}) collective-permute-start(bf16[3,512,512]{2,1,0:T(8,128)(2,1)S(1)} %pad_maximum_fusion.13), channel_id=1, source_target_pairs={{0,16},{8,24},{16,0},{24,8},{1,17},{9,25},{17,1},{25,9},{2,18},{10... | collective-permute-start | bytes 4718600 | tf_op jit(solution)/shard_map/ppermute | solution.py:580
  829.1 19.9 %collective-permute-start.23 = (bf16[3,256,512]{2,1,0:T(8,128)(2,1)S(1)}, bf16[3,256,512]{2,1,0:T(8,128)(2,1)}, u32[]{:S(2)}, u32[]{:S(2)}) collective-permute-start(bf16[3,256,512]{2,1,0:T(8,128)(2,1)S(1)} %get-tuple-element.334), channel_id=1, source_target_pairs={{0,16},{8,24},{16,0},{24,8},{1,17},{9,25},{17,1},{25,9},{2,18},{10... | collective-permute-start | bytes 2359304 | tf_op jit(solution)/shard_map/ppermute | solution.py:580
  830.2 19.7 %collective-permute-start.22 = (bf16[3,256,512]{2,1,0:T(8,128)(2,1)S(1)}, bf16[3,256,512]{2,1,0:T(8,128)(2,1)}, u32[]{:S(2)}, u32[]{:S(2)}) collective-permute-start(bf16[3,256,512]{2,1,0:T(8,128)(2,1)S(1)} %get-tuple-element.335), channel_id=1, source_target_pairs={{0,8},{8,0},{16,24},{24,16},{1,9},{9,1},{17,25},{25,17},{2,10},{10... | collective-permute-start | bytes 2359304 | tf_op jit(solution)/shard_map/ppermute | solution.py:580
  836.7 24.0 %copy-start.29 = (bf16[3,512,512]{2,1,0:T(8,128)(2,1)}, bf16[3,512,512]{2,1,0:T(8,128)(2,1)S(1)}, u32[]{:S(2)}) copy-start(bf16[3,512,512]{2,1,0:T(8,128)(2,1)S(1)} %pad_maximum_fusion.15) | copy-start | bytes 4718596
  841.3 13.7 %copy-start.63 = (f32[160,512]{1,0:T(8,128)S(1)}, f32[160,512]{1,0:T(8,128)}, u32[]{:S(2)}) copy-start(f32[160,512]{1,0:T(8,128)} %fusion.232) | copy-start | bytes 983044
  850.0 16.5 %collective-permute-start.31 = (f32[36,512]{1,0:T(8,128)S(1)}, f32[36,512]{1,0:T(8,128)S(1)}, u32[]{:S(2)}, u32[]{:S(2)}) collective-permute-start(f32[36,512]{1,0:T(8,128)S(1)} %constant_dynamic-update-slice_fusion), channel_id=1, source_target_pairs={{0,24},{8,16},{16,8},{24,0},{1,25},{9,17},{17,9},{25,1},{2,26},{10... | collective-permute-start | bytes 221192 | tf_op jit(solution)/shard_map/ppermute | solution.py:580
  851.9 15.8 %collective-permute-start.30 = (f32[36,512]{1,0:T(8,128)S(1)}, f32[36,512]{1,0:T(8,128)S(1)}, u32[]{:S(2)}, u32[]{:S(2)}) collective-permute-start(f32[36,512]{1,0:T(8,128)S(1)} %constant_dynamic-update-slice_fusion), channel_id=1, source_target_pairs={{0,16},{8,24},{16,0},{24,8},{1,17},{9,25},{17,1},{25,9},{2,18},{10... | collective-permute-start | bytes 221192 | tf_op jit(solution)/shard_map/ppermute | solution.py:580
  852.9 15.7 %collective-permute-start.29 = (f32[36,512]{1,0:T(8,128)S(1)}, f32[36,512]{1,0:T(8,128)S(1)}, u32[]{:S(2)}, u32[]{:S(2)}) collective-permute-start(f32[36,512]{1,0:T(8,128)S(1)} %constant_dynamic-update-slice_fusion), channel_id=1, source_target_pairs={{0,8},{8,0},{16,24},{24,16},{1,9},{9,1},{17,25},{25,17},{2,10},{10... | collective-permute-start | bytes 221192 | tf_op jit(solution)/shard_map/ppermute | solution.py:580
  855.5 26.5 %collective-permute-start.26 = (bf16[3,72,512]{2,1,0:T(8,128)(2,1)S(1)}, bf16[3,72,512]{2,1,0:T(8,128)(2,1)S(1)}, u32[]{:S(2)}, u32[]{:S(2)}) collective-permute-start(bf16[3,72,512]{2,1,0:T(8,128)(2,1)S(1)} %pad_maximum_fusion.29), channel_id=1, source_target_pairs={{0,8},{8,0},{16,24},{24,16},{1,9},{9,1},{17,25},{25,17},{2,10},{10... | collective-permute-start | bytes 663560 | tf_op jit(solution)/shard_map/ppermute | solution.py:580
  856.9 25.1 %collective-permute-start.27 = (bf16[3,72,512]{2,1,0:T(8,128)(2,1)S(1)}, bf16[3,72,512]{2,1,0:T(8,128)(2,1)S(1)}, u32[]{:S(2)}, u32[]{:S(2)}) collective-permute-start(bf16[3,72,512]{2,1,0:T(8,128)(2,1)S(1)} %pad_maximum_fusion.30), channel_id=1, source_target_pairs={{0,16},{8,24},{16,0},{24,8},{1,17},{9,25},{17,1},{25,9},{2,18},{10... | collective-permute-start | bytes 663560 | tf_op jit(solution)/shard_map/ppermute | solution.py:580
  866.5 15.6 %collective-permute-start.28 = (bf16[3,72,512]{2,1,0:T(8,128)(2,1)S(1)}, bf16[3,72,512]{2,1,0:T(8,128)(2,1)S(1)}, u32[]{:S(2)}, u32[]{:S(2)}) collective-permute-start(bf16[3,72,512]{2,1,0:T(8,128)(2,1)S(1)} %pad_maximum_fusion.31), channel_id=1, source_target_pairs={{0,24},{8,16},{16,8},{24,0},{1,25},{9,17},{17,9},{25,1},{2,26},{10... | collective-permute-start | bytes 663560 | tf_op jit(solution)/shard_map/ppermute | solution.py:580
  867.7 39.2 %collective-permute-start.25 = (bf16[3,512,512]{2,1,0:T(8,128)(2,1)}, bf16[3,512,512]{2,1,0:T(8,128)(2,1)}, u32[]{:S(2)}, u32[]{:S(2)}) collective-permute-start(bf16[3,512,512]{2,1,0:T(8,128)(2,1)} %pad_maximum_fusion.19), channel_id=1, source_target_pairs={{0,16},{8,24},{16,0},{24,8},{1,17},{9,25},{17,1},{25,9},{2,18},{10... | collective-permute-start | bytes 4718600 | tf_op jit(solution)/shard_map/ppermute | solution.py:580
  869.2 5.4 collective-permute-start.32
  874.7 4.1 collective-permute-start.33
  878.8 1.3 collective-permute-start.34
  880.1 37.1 %collective-permute-start.24 = (bf16[3,512,512]{2,1,0:T(8,128)(2,1)}, bf16[3,512,512]{2,1,0:T(8,128)(2,1)}, u32[]{:S(2)}, u32[]{:S(2)}) collective-permute-start(bf16[3,512,512]{2,1,0:T(8,128)(2,1)} %pad_maximum_fusion.17), channel_id=1, source_target_pairs={{0,8},{8,0},{16,24},{24,16},{1,9},{9,1},{17,25},{25,17},{2,10},{10... | collective-permute-start | bytes 4718600 | tf_op jit(solution)/shard_map/ppermute | solution.py:580
  (95 other events, 333.3 us)
Sparse Core Ops, SparseCore 0:
  27.2 83.2 all-gather.4
  112.1 89.5 all-gather.10
  210.7 80.9 all-gather.8
  293.2 80.5 all-gather.6
  468.4 88.9 reduce-scatter.4
  559.6 87.9 reduce-scatter.6
  649.9 87.9 reduce-scatter.8
  807.0 91.4 reduce-scatter.10

commit v3 on v2

--- a/solution.py
+++ b/solution.py
@@ -322,33 +322,33 @@
         return c
 
     first = [send(a, parts[a].at[:, cols(1 - core, H)], near[a], 0, mate) for a in range(n)]
+    sends = []
     for a in range(n):
         first[a].wait()
         half[a][...] = (
             parts[a][:, cols(core, H)].astype(f32) + near[a][...].astype(f32)
         ).astype(half[a].dtype)
-    sends = [
-        [send(a, half[a].at[:, cols(p, Q)], far[a].at[k], 1 + k, 2 * p + core) for a in range(n)]
-        for k, p in enumerate(peers)
-    ]
-    totals = [half[a][:, cols(z, Q)].astype(f32) for a in range(n)]
-    for k in range(pairs - 1):
-        for a in range(n):
-            sends[k][a].wait()
-            totals[a] = totals[a] + far[a][k].astype(f32)
+        sends.append(
+            [send(a, half[a].at[:, cols(p, Q)], far[a].at[k], 1 + k, 2 * p + core) for k, p in enumerate(peers)]
+        )
     at = pl.ds(pl.multiple_of(core * H + z * Q, Q), Q)
-    sends = []
+    back = []
     for a in range(n):
-        mine[a][...] = totals[a].astype(mine[a].dtype)
-        for k, p in enumerate(peers):
-            sends.append(send(a, mine[a], outs[a].at[:, at], pairs + k, 2 * p + core))
+        total = half[a][:, cols(z, Q)].astype(f32)
+        for k in range(pairs - 1):
+            sends[a][k].wait()
+            total = total + far[a][k].astype(f32)
+        mine[a][...] = total.astype(mine[a].dtype)
+        back.append(
+            [send(a, mine[a], outs[a].at[:, at], pairs + k, 2 * p + core) for k, p in enumerate(peers)]
+        )
         outs[a][:, at] = mine[a][...]
-    for c in sends:
-        c.wait()
-    last = [
-        send(a, outs[a].at[:, cols(core, H)], outs[a].at[:, cols(core, H)], 2 * pairs - 1, mate)
-        for a in range(n)
-    ]
+    last = []
+    for a in range(n):
+        for c in back[a]:
+            c.wait()
+        done = outs[a].at[:, cols(core, H)]
+        last.append(send(a, done, done, 2 * pairs - 1, mate))
     for c in last:
         c.wait()
 
@@ -596,6 +596,10 @@
     return [own, by_x, by_y, swap(first, 2), swap(second, 1)]
 
 
+def scatter_all(parts):
+    return [parts[0]] + [swap(p, j) for j, p in enumerate(parts) if j]
+
+
 def scatter_far(parts):
     if len(parts) != 4:
         return []
@@ -603,9 +607,9 @@
     return [swap(parts[3][:, :half], 1), swap(parts[3][:, half:], 2)]
 
 
-def scatter_near(parts, far):
+def with_far(parts, far):
     if len(parts) != 4:
-        return scatter_all(parts)
+        return parts
     own, for_x, for_y, _ = parts
     a, b = far
     half = a.shape[1]
@@ -615,11 +619,11 @@
     for_x = jnp.concatenate(
         [for_x[:, :half], (for_x[:, half:].astype(f32) + b.astype(f32)).astype(bf16)], axis=1
     )
-    return [own, swap(for_x, 1), swap(for_y, 2)]
-
-
-def scatter_all(parts):
-    return [parts[0]] + [swap(p, j) for j, p in enumerate(parts) if j]
+    return [own, for_x, for_y]
+
+
+def scatter_near(parts, far):
+    return scatter_all(with_far(parts, far))
 
 
 def total_of(terms):
@@ -809,17 +813,17 @@
     dn_part = finish(carried, d_proj)
     dn_part, branches[-1] = lax.optimization_barrier((dn_part, branches[-1]))
     dn_parts.append(lax.psum_scatter(dn_part, "chan", scatter_dimension=0, tiled=True))
-    t_x += by_tile(gathered[-1:], d_ins[-1:], 0)
-    g_x = by_modality_blocks(flat, t_x, 0, nseq)
-    far = scatter_far(g_x)
     totals = [sum(s[j] for s in sums) for j in range(4)]
-    far, t_dt, t_xw, g_out, g_gate, totals = lax.optimization_barrier(
-        (far, t_dt, t_xw, g_out, g_gate, totals)
-    )
-    g_x = scatter_near(g_x, far)
     gain_rows = square_order(totals[3], me).reshape(-1, inner)
     vectors = seq_sum(jnp.concatenate([*totals[:3], gain_rows], axis=0))
     gain_total = chan_scatter(vectors[-gain_rows.shape[0] :].reshape(1, width))[0] / norm_gain
+    t_x += by_tile(gathered[-1:], d_ins[-1:], 0)
+    g_x = by_modality_blocks(flat, t_x, 0, nseq)
+    g_x[-1], vectors, gain_total = lax.optimization_barrier((g_x[-1], vectors, gain_total))
+    far = scatter_far(g_x)
+    g_x = with_far(g_x, far)
+    g_x, t_dt, t_xw, g_out, g_gate = lax.optimization_barrier((g_x, t_dt, t_xw, g_out, g_gate))
+    g_x = scatter_all(g_x)
     g_dt = by_modality(flat, t_dt)
     g_xw = by_modality(flat, t_xw)
     ndt = dt_weight.shape[1]

time: 934 us -> 934 us (level)
    ppermute x35, waiting for transfers between devices: 142 us -> 156 us  [swap(): return lax.ppermute(v, axis, [(i, i ^ bits) for i in range(n)])]
    unnamed x199 -> x178, local copies, waits for them, and re-layouts: 25.1 us -> 22.7 us
  transfers between devices with their start and end apart: 43 -> 43, of which waited for: 15 -> 19; matrix products, arithmetic and copies ran while one was open for 15% -> 14% of each run, Pallas kernels for 57% -> 56%
where the time goes in v3:
time: 934 us; the launch traced here: 933 us
  Pallas kernels  526 us (56%)
  waiting for transfers between devices  161 us (17%)
  other arithmetic  77.6 us (8%)
  matrix products  50.8 us (5%)
  starting transfers between devices  47.4 us (5%)
  local copies, waits for them, and re-layouts  45.4 us (5%)
  between operations  23.9 us (3%)
    pallas_call x3, Pallas kernels, scan(): pl.pallas_call(functools.partial(scan_kernel, S, NG, mode), in_specs=[HBM...  246 us
    pallas_call x10, Pallas kernels, stage(): pl.pallas_call(kernel, grid_spec=pltpu.PrefetchScalarGridSpec(num_scalar_...  190 us
    ppermute x35, waiting for transfers between devices, swap(): return lax.ppermute(v, axis, [(i, i ^ bits) for i in range(n)])  156 us
    pallas_call x3, Pallas kernels, chan_sum(): pl.pallas_call(functools.partial(sum_kernel, pairs, n), in_specs=[VMEM] *...  90.3 us
    dot_general x20, matrix products, by_tile(): lax.dot_general(a, b, dims, preferred_element_type=f32).astype(dtype)  50.8 us
    ppermute x35, starting transfers between devices, swap(): return lax.ppermute(v, axis, [(i, i ^ bits) for i in range(n)])  46.4 us
    another operation x34, other arithmetic, by_modality(): return jnp.stack(out)  23.8 us
    unnamed x178, local copies, waits for them, and re-layouts  22.7 us
  transfers between devices with their start and end apart: 43, of which 19 were waited for; matrix products, arithmetic and copies ran while one was open for 14% of the time, Pallas kernels for 56%

profile of v3, /device:TPU:0, one launch (start us, length us, event | category | flops | bytes accessed | tf_op | source)
XLA Modules:
  0.0 932.7 jit_solution(13617893635055166353)
XLA Ops:
  7.2 4.7 reshape.304.rest_0_
  13.3 3.0 collective-permute-start.1
  18.3 2.7 collective-permute-start.2
  22.9 2.9 fusion.70
  27.2 2.7 slice_bitcast_fusion
  35.4 2.4 collective-permute-start.5
  37.9 70.5 %collective-permute-done.7 = bf16[3,72,512]{2,1,0:T(8,128)(2,1)S(1)} collective-permute-done((bf16[3,72,512]{2,1,0:T(8,128)(2,1)S(1)}, bf16[3,72,512]{2,1,0:T(8,128)(2,1)S(1)}, u32[]{:S(2)}, u32[]{:S(2)}) %collective-permute-start.7) | collective-permute-done | bytes 221216 | tf_op jit(solution)/shard_map/ppermute | solution.py:580
  108.4 2.3 collective-permute-done.5
  119.9 27.0 %collective-permute-done.9.rest_4_ = bf16[3,256,1024]{2,1,0:T(8,128)(2,1)} collective-permute-done((bf16[3,256,1024]{2,1,0:T(8,128)(2,1)S(1)}, bf16[3,256,1024]{2,1,0:T(8,128)(2,1)}, u32[]{:S(2)}, u32[]{:S(2)}) %collective-permute-start.9) | collective-permute-done | bytes 1572896 | tf_op jit(solution)/shard_map/ppermute | solution.py:580
  153.5 19.6 %in_stage.2 = (f32[2048,512]{1,0:T(8,128)}, f32[2048,512]{1,0:T(8,128)}, bf16[2048,512]{1,0:T(8,128)(2,1)}, bf16[128,2048]{1,0:T(8,128)(2,1)}, f32[32,2048]{1,0:T(8,128)}) custom-call(s32[2]{0:T(128)} %get-tuple-element.392.kinds, s32[5]{0:T(128)} %get-tuple-element.390.lens, bf16[2048,2048]{1,0:T(8,128)(2,1)} %all-gather.5.cloned.1.call-done.g, ...), custom_call_target="tpu_custom_call" | custom-call | flops 4620000256 | bytes 4194304 | tf_op jit(solution)/shard_map/in_stage/pallas_call | solution.py:562
  175.2 33.3 %chan_sum.3 = (bf16[128,2048]{1,0:T(8,128)(2,1)S(1)}, f32[32,2048]{1,0:T(8,128)S(1)}) custom-call(bf16[128,2048]{1,0:T(8,128)(2,1)S(1)} %copy-done.13, f32[32,2048]{1,0:T(8,128)S(1)} %copy-done.15), custom_call_target="tpu_custom_call" | custom-call | flops 5720000000 | bytes 1638 | tf_op jit(solution)/shard_map/chan_sum/pallas_call | solution.py:364
  216.5 16.5 %collective-permute-done.13.rest_4_ = bf16[3,512,256]{2,1,0:T(8,128)(2,1)} collective-permute-done((bf16[3,512,256]{2,1,0:T(8,128)(2,1)}, bf16[3,512,256]{2,1,0:T(8,128)(2,1)}, u32[]{:S(2)}, u32[]{:S(2)}) %collective-permute-start.13) | collective-permute-done | bytes 786464 | tf_op jit(solution)/shard_map/ppermute | solution.py:580
  235.0 17.4 %mid_stage.2 = (f32[2048,512]{1,0:T(8,128)}, f32[2048,512]{1,0:T(8,128)}, f32[2048,512]{1,0:T(8,128)}, f32[2048,512]{1,0:T(8,128)}, f32[2048,512]{1,0:T(8,128)}, /*index=5*/f32[2048,128]{1,0:T(8,128)}) custom-call(s32[2]{0:T(128)} %get-tuple-element.392.kinds, s32[5]{0:T(128)} %get-tuple-element.390.lens, ...), custom_call_target="tpu_custom_call" | custom-call | flops 4180000000 | bytes 7340032 | tf_op jit(solution)/shard_map/mid_stage/pallas_call | solution.py:562
  252.4 113.6 %scan_both.1 = (f32[2048,512]{1,0:T(8,128)}, f32[2048,512]{1,0:T(8,128)}, f32[2048,512]{1,0:T(8,128)}, f32[16,512]{1,0:T(8,128)}, f32[2048,128]{1,0:T(8,128)}) custom-call(f32[2048,512]{1,0:T(8,128)} %get-tuple-element.161.refs_0_, f32[2048,512]{1,0:T(8,128)} %get-tuple-element.162.refs_1_, f32[2048,512]{1,0:T(8,128)} %get-tuple-element.163.refs_2_.ds, ...), custom_call_target="tpu_custom_call" | custom-call | flops 25080000512 | bytes 5033164 | tf_op jit(solution)/shard_map/scan_both/pallas_call | solution.py:281
  367.1 11.6 %step_stage.2 = (bf16[2048,512]{1,0:T(8,128)(2,1)}, f32[2048,512]{1,0:T(8,128)}, bf16[160,2048]{1,0:T(8,128)(2,1)}, f32[8,512]{1,0:T(8,128)}) custom-call(s32[2]{0:T(128)} %get-tuple-element.392.kinds, s32[5]{0:T(128)} %get-tuple-element.390.lens, f32[2048,512]{1,0:T(8,128)} %get-tuple-element.165.gb, f32[2048,512]{1,0:T(8,128)} %get-tuple-element.166.fr, ...), custom_call_target="tpu_custom_call" | custom-call | flops 2640000000 | bytes 5872025 | tf_op jit(solution)/shard_map/step_stage/pallas_call | solution.py:562
  378.7 14.6 %post_stage.2 = (bf16[2048,2048]{1,0:T(8,128)(2,1)}, bf16[2048,512]{1,0:T(8,128)(2,1)}, bf16[2048,512]{1,0:T(8,128)(2,1)}) custom-call(s32[2]{0:T(128)} %get-tuple-element.392.kinds, s32[5]{0:T(128)} %get-tuple-element.390.lens, f32[2048,512]{1,0:T(8,128)} %get-tuple-element.177.y, f32[2048,512]{1,0:T(8,128)} %get-tuple-element.178.dy, ...), custom_call_target="tpu_custom_call" | custom-call | flops 3080000000 | bytes 7969177 | tf_op jit(solution)/shard_map/post_stage/pallas_call | solution.py:562
  393.3 31.7 %in_stage.3 = (f32[2048,512]{1,0:T(8,128)}, f32[2048,512]{1,0:T(8,128)}, bf16[2048,512]{1,0:T(8,128)(2,1)}, bf16[128,2048]{1,0:T(8,128)(2,1)}, f32[32,2048]{1,0:T(8,128)}) custom-call(s32[2]{0:T(128)} %get-tuple-element.391.kinds, s32[5]{0:T(128)} %get-tuple-element.389.lens, bf16[2048,2048]{1,0:T(8,128)(2,1)} %all-gather.9.cloned.1.call-done.g, ...), custom_call_target="tpu_custom_call" | custom-call | flops 4620000256 | bytes 4194304 | tf_op jit(solution)/shard_map/in_stage/pallas_call | solution.py:562
  427.0 36.6 %chan_sum.4 = (bf16[128,2048]{1,0:T(8,128)(2,1)S(1)}, f32[32,2048]{1,0:T(8,128)S(1)}, bf16[160,2048]{1,0:T(8,128)(2,1)S(1)}) custom-call(bf16[128,2048]{1,0:T(8,128)(2,1)S(1)} %copy-done.12, f32[32,2048]{1,0:T(8,128)S(1)} %copy-done.14, bf16[160,2048]{1,0:T(8,128)(2,1)S(1)} %copy-done.10), custom_call_target="tpu_custom_call" | custom-call | flops 5720000000 | bytes 1638 | tf_op jit(solution)/shard_map/chan_sum/pallas_call | solution.py:364
  466.0 25.5 %back_stage.2 = (bf16[2048,512]{1,0:T(8,128)(2,1)}, bf16[2048,2048]{1,0:T(8,128)(2,1)}, f32[8,512]{1,0:T(8,128)}, f32[8,2048]{1,0:T(8,128)}) custom-call(s32[2]{0:T(128)} %get-tuple-element.392.kinds, s32[5]{0:T(128)} %get-tuple-element.390.lens, bf16[160,2048]{1,0:T(8,128)(2,1)} %copy-done, bf16[3,160,512]{2,1,0:T(8,128)(2,1)} %pad_maximum_fusion.24.xw, ...), custom_call_target="tpu_custom_call" | custom-call | flops 5720000000 | bytes 7969177 | tf_op jit(solution)/shard_map/back_stage/pallas_call | solution.py:562
  500.0 4.9 fusion.51
  504.9 17.3 %mid_stage.3 = (f32[2048,512]{1,0:T(8,128)}, f32[2048,512]{1,0:T(8,128)}, f32[2048,512]{1,0:T(8,128)}, f32[2048,512]{1,0:T(8,128)}, f32[2048,512]{1,0:T(8,128)}, /*index=5*/f32[2048,128]{1,0:T(8,128)}) custom-call(s32[2]{0:T(128)} %get-tuple-element.391.kinds, s32[5]{0:T(128)} %get-tuple-element.389.lens, bf16[2048,2048]{1,0:T(8,128)(2,1)} %all-gather.7.cloned.1.call-done.u, ...), custom_call_target="tpu_custom_call" | custom-call | flops 4180000000 | bytes 7340032 | tf_op jit(solution)/shard_map/mid_stage/pallas_call | solution.py:562
  522.3 59.5 %scan_ahead.1 = (f32[2048,512]{1,0:T(8,128)}, f32[2048,128]{1,0:T(8,128)}, f32[4,256,4,8,512]{4,3,2,1,0:T(8,128)}) custom-call(f32[2048,512]{1,0:T(8,128)} %get-tuple-element.190.refs_0_, f32[2048,512]{1,0:T(8,128)} %get-tuple-element.191.refs_1_, f32[2048,512]{1,0:T(8,128)} %get-tuple-element.192.refs_2_.ds, f32[2048,128]{1,0:T(8,128)} %get-tuple-element.203.refs_3_, ...), custom_call_target="tpu_custom_call" | custom-call | flops 13639999488 | bytes 5033164 | tf_op jit(solution)/shard_map/scan_ahead/pallas_call | solution.py:281
  581.8 14.7 %post_stage.3 = (bf16[2048,2048]{1,0:T(8,128)(2,1)}, bf16[2048,512]{1,0:T(8,128)(2,1)}, bf16[2048,512]{1,0:T(8,128)(2,1)}) custom-call(s32[2]{0:T(128)} %get-tuple-element.391.kinds, s32[5]{0:T(128)} %get-tuple-element.389.lens, f32[2048,512]{1,0:T(8,128)} %get-tuple-element.195.y, f32[2048,512]{1,0:T(8,128)} %get-tuple-element.196.dy, ...), custom_call_target="tpu_custom_call" | custom-call | flops 3080000000 | bytes 7969177 | tf_op jit(solution)/shard_map/post_stage/pallas_call | solution.py:562
  597.0 5.1 fusion.48
  602.1 4.8 fusion.42
  607.0 2.4 fusion.36
  609.4 3.7 fusion.45
  613.1 3.7 fusion.39
  616.8 2.6 fusion.57
  619.4 2.4 fusion.54
  632.8 2.4 fusion.30
  635.2 2.6 fusion.24
  663.2 73.4 %scan_back.1 = (f32[2048,512]{1,0:T(8,128)}, f32[2048,512]{1,0:T(8,128)}, f32[16,512]{1,0:T(8,128)}, f32[2048,128]{1,0:T(8,128)}) custom-call(f32[2048,512]{1,0:T(8,128)} %get-tuple-element.190.refs_0_, f32[2048,512]{1,0:T(8,128)} %get-tuple-element.191.refs_1_, f32[2048,512]{1,0:T(8,128)} %get-tuple-element.192.refs_2_.ds, ...), custom_call_target="tpu_custom_call" | custom-call | flops 14960000000 | bytes 5033164 | tf_op jit(solution)/shard_map/scan_back/pallas_call | solution.py:281
  743.0 11.5 %step_stage.3 = (bf16[2048,512]{1,0:T(8,128)(2,1)}, f32[2048,512]{1,0:T(8,128)}, bf16[160,2048]{1,0:T(8,128)(2,1)}, f32[8,512]{1,0:T(8,128)}) custom-call(s32[2]{0:T(128)} %get-tuple-element.391.kinds, s32[5]{0:T(128)} %get-tuple-element.389.lens, f32[2048,512]{1,0:T(8,128)} %get-tuple-element.205.gb, f32[2048,512]{1,0:T(8,128)} %get-tuple-element.206.fr, ...), custom_call_target="tpu_custom_call" | custom-call | flops 2640000000 | bytes 5872025 | tf_op jit(solution)/shard_map/step_stage/pallas_call | solution.py:562
  755.5 20.4 %chan_sum.5.dproj = bf16[160,2048]{1,0:T(8,128)(2,1)S(1)} custom-call(bf16[160,2048]{1,0:T(8,128)(2,1)S(1)} %copy-done.11), custom_call_target="tpu_custom_call" | custom-call | flops 5720000000 | bytes 1638 | tf_op jit(solution)/shard_map/chan_sum/pallas_call | solution.py:364
  779.2 25.7 %back_stage.3 = (bf16[2048,512]{1,0:T(8,128)(2,1)}, bf16[2048,2048]{1,0:T(8,128)(2,1)}, f32[8,512]{1,0:T(8,128)}, f32[8,2048]{1,0:T(8,128)}) custom-call(s32[2]{0:T(128)} %get-tuple-element.391.kinds, s32[5]{0:T(128)} %get-tuple-element.389.lens, bf16[160,2048]{1,0:T(8,128)(2,1)} %copy-done.2, bf16[3,160,512]{2,1,0:T(8,128)(2,1)} %pad_maximum_fusion.24.xw, ...), custom_call_target="tpu_custom_call" | custom-call | flops 5720000000 | bytes 7969177 | tf_op jit(solution)/shard_map/back_stage/pallas_call | solution.py:562
  821.2 5.0 fusion.33
  826.3 4.7 fusion.27
  835.7 3.3 collective-permute-start.25
  840.9 2.3 collective-permute-start.26
  853.3 13.4 %collective-permute-done.29 = bf16[3,256,512]{2,1,0:T(8,128)(2,1)S(1)} collective-permute-done((bf16[3,256,512]{2,1,0:T(8,128)(2,1)S(1)}, bf16[3,256,512]{2,1,0:T(8,128)(2,1)S(1)}, u32[]{:S(2)}, u32[]{:S(2)}) %collective-permute-start.29) | collective-permute-done | bytes 786464 | tf_op jit(solution)/shard_map/ppermute | solution.py:580
  877.3 4.1 convert_add_fusion.4
  881.4 2.3 convert_add_fusion.3
  891.9 4.8 reduce-scatter.11.cloned.1.call-done
  902.4 2.3 pad_maximum_fusion
  904.7 12.0 %collective-permute-done.30 = bf16[3,512,512]{2,1,0:T(8,128)(2,1)} collective-permute-done((bf16[3,512,512]{2,1,0:T(8,128)(2,1)}, bf16[3,512,512]{2,1,0:T(8,128)(2,1)}, u32[]{:S(2)}, u32[]{:S(2)}) %collective-permute-start.30) | collective-permute-done | bytes 1572896 | tf_op jit(solution)/shard_map/ppermute | solution.py:580
  917.8 2.5 convert_add_fusion.2
  920.3 5.3 broadcast_select_fusion
  (409 shorter events, 151.2 us)
Async XLA Ops:
  7.2 146.3 %all-gather.5.cloned.1.call-start = ((), (), s32[]{:S(2)}) async-start(), calls=%async_computation.4 | async-start | bytes 9437184 | tf_op jit(solution)/shard_map/all_gather | solution.py:711
  11.9 20.9 %copy-start.16 = (bf16[3,512,1024]{2,1,0:T(8,128)(2,1)}, bf16[3,512,1024]{2,1,0:T(8,128)(2,1)S(1)}, u32[]{:S(2)}) copy-start(bf16[3,512,1024]{2,1,0:T(8,128)(2,1)S(1)} %reshape.304.rest_0_) | copy-start | bytes 9437188
  11.9 1.3 collective-permute-start
  13.3 5.0 collective-permute-start.1
  18.3 4.6 collective-permute-start.2
  27.1 189.4 %all-gather.11.cloned.1.call-start = ((), (), s32[]{:S(2)}) async-start(), calls=%async_computation.7 | async-start | bytes 9437184 | tf_op jit(solution)/shard_map/all_gather | solution.py:712
  31.1 362.1 %all-gather.9.cloned.1.call-start = ((), (), s32[]{:S(2)}) async-start(), calls=%async_computation.6 | async-start | bytes 9437184 | tf_op jit(solution)/shard_map/all_gather | solution.py:756
  31.2 81.5 %collective-permute-start.4 = (bf16[3,512,1024]{2,1,0:T(8,128)(2,1)S(1)}, bf16[3,512,1024]{2,1,0:T(8,128)(2,1)S(1)}, u32[]{:S(2)}, u32[]{:S(2)}) collective-permute-start(bf16[3,512,1024]{2,1,0:T(8,128)(2,1)S(1)} %reshape.304.rest_0_), channel_id=1, source_target_pairs={{0,16},{8,24},{16,0},{24,8},{1,17},{9,25},{17,1},{25,9},{2,18},{10... | collective-permute-start | bytes 9437192 | tf_op jit(solution)/shard_map/ppermute | solution.py:580
  32.8 79.9 %collective-permute-start.3 = (bf16[3,512,1024]{2,1,0:T(8,128)(2,1)S(1)}, bf16[3,512,1024]{2,1,0:T(8,128)(2,1)S(1)}, u32[]{:S(2)}, u32[]{:S(2)}) collective-permute-start(bf16[3,512,1024]{2,1,0:T(8,128)(2,1)S(1)} %reshape.304.rest_0_), channel_id=1, source_target_pairs={{0,8},{8,0},{16,24},{24,16},{1,9},{9,1},{17,25},{25,17},{2,10},{10... | collective-permute-start | bytes 9437192 | tf_op jit(solution)/shard_map/ppermute | solution.py:580
  34.3 74.1 %collective-permute-start.7 = (bf16[3,72,512]{2,1,0:T(8,128)(2,1)S(1)}, bf16[3,72,512]{2,1,0:T(8,128)(2,1)S(1)}, u32[]{:S(2)}, u32[]{:S(2)}) collective-permute-start(bf16[3,72,512]{2,1,0:T(8,128)(2,1)S(1)} %pad_maximum_fusion.28), channel_id=1, source_target_pairs={{0,8},{8,0},{16,24},{24,16},{1,9},{9,1},{17,25},{25,17},{2,10},{10... | collective-permute-start | bytes 663560 | tf_op jit(solution)/shard_map/ppermute | solution.py:580
  34.9 73.5 %collective-permute-start.6 = (bf16[3,72,512]{2,1,0:T(8,128)(2,1)S(1)}, bf16[3,72,512]{2,1,0:T(8,128)(2,1)S(1)}, u32[]{:S(2)}, u32[]{:S(2)}) collective-permute-start(bf16[3,72,512]{2,1,0:T(8,128)(2,1)S(1)} %pad_maximum_fusion.28), channel_id=1, source_target_pairs={{0,16},{8,24},{16,0},{24,8},{1,17},{9,25},{17,1},{25,9},{2,18},{10... | collective-permute-start | bytes 663560 | tf_op jit(solution)/shard_map/ppermute | solution.py:580
  35.4 75.3 %collective-permute-start.5 = (bf16[3,72,512]{2,1,0:T(8,128)(2,1)S(1)}, bf16[3,72,512]{2,1,0:T(8,128)(2,1)S(1)}, u32[]{:S(2)}, u32[]{:S(2)}) collective-permute-start(bf16[3,72,512]{2,1,0:T(8,128)(2,1)S(1)} %pad_maximum_fusion.28), channel_id=1, source_target_pairs={{0,24},{8,16},{16,8},{24,0},{1,25},{9,17},{17,9},{25,1},{2,26},{10... | collective-permute-start | bytes 663560 | tf_op jit(solution)/shard_map/ppermute | solution.py:580
  112.8 34.1 %collective-permute-start.9 = (bf16[3,256,1024]{2,1,0:T(8,128)(2,1)S(1)}, bf16[3,256,1024]{2,1,0:T(8,128)(2,1)}, u32[]{:S(2)}, u32[]{:S(2)}) collective-permute-start(bf16[3,256,1024]{2,1,0:T(8,128)(2,1)S(1)} %split.319), channel_id=1, source_target_pairs={{0,8},{8,0},{16,24},{24,16},{1,9},{9,1},{17,25},{25,17},{2,10},{10... | collective-permute-start | bytes 4718600 | tf_op jit(solution)/shard_map/ppermute | solution.py:580
  115.9 37.6 %collective-permute-start.8 = (bf16[3,256,1024]{2,1,0:T(8,128)(2,1)}, bf16[3,256,1024]{2,1,0:T(8,128)(2,1)}, u32[]{:S(2)}, u32[]{:S(2)}) collective-permute-start(bf16[3,256,1024]{2,1,0:T(8,128)(2,1)} %split.318), channel_id=1, source_target_pairs={{0,16},{8,24},{16,0},{24,8},{1,17},{9,25},{17,1},{25,9},{2,18},{10... | collective-permute-start | bytes 4718600 | tf_op jit(solution)/shard_map/ppermute | solution.py:580
  118.7 31.3 %copy-start.77 = (s32[2,1,5]{2,1,0:T(1,128)S(1)}, s32[2,1,5]{2,1,0:T(1,128)}, u32[]{:S(2)}) copy-start(s32[2,1,5]{2,1,0:T(1,128)} %param.17) | copy-start | bytes 124
  147.0 63.1 %collective-permute-start.11 = (bf16[3,512,512]{2,1,0:T(8,128)(2,1)}, bf16[3,512,512]{2,1,0:T(8,128)(2,1)S(1)}, u32[]{:S(2)}, u32[]{:S(2)}) collective-permute-start(bf16[3,512,512]{2,1,0:T(8,128)(2,1)} %rest_0_.3), channel_id=1, source_target_pairs={{0,16},{8,24},{16,0},{24,8},{1,17},{9,25},{17,1},{25,9},{2,18},{10... | collective-permute-start | bytes 4718600 | tf_op jit(solution)/shard_map/ppermute | solution.py:580
  148.5 61.5 %collective-permute-start.10 = (bf16[3,512,512]{2,1,0:T(8,128)(2,1)}, bf16[3,512,512]{2,1,0:T(8,128)(2,1)S(1)}, u32[]{:S(2)}, u32[]{:S(2)}) collective-permute-start(bf16[3,512,512]{2,1,0:T(8,128)(2,1)} %rest_0_.3), channel_id=1, source_target_pairs={{0,8},{8,0},{16,24},{24,16},{1,9},{9,1},{17,25},{25,17},{2,10},{10... | collective-permute-start | bytes 4718600 | tf_op jit(solution)/shard_map/ppermute | solution.py:580
  210.1 294.9 %all-gather.7.cloned.1.call-start = ((), (), s32[]{:S(2)}) async-start(), calls=%async_computation.5 | async-start | bytes 9437184 | tf_op jit(solution)/shard_map/all_gather | solution.py:757
  210.6 371.2 %reduce-scatter.5.cloned.1.call-start = ((), (), s32[]{:S(2)}) async-start(), calls=%async_computation.8 | async-start | bytes 9437184 | tf_op jit(solution)/shard_map/reduce_scatter | solution.py:761
  212.9 20.1 %collective-permute-start.13 = (bf16[3,512,256]{2,1,0:T(8,128)(2,1)}, bf16[3,512,256]{2,1,0:T(8,128)(2,1)}, u32[]{:S(2)}, u32[]{:S(2)}) collective-permute-start(bf16[3,512,256]{2,1,0:T(8,128)(2,1)} %split.333), channel_id=1, source_target_pairs={{0,8},{8,0},{16,24},{24,16},{1,9},{9,1},{17,25},{25,17},{2,10},{10... | collective-permute-start | bytes 2359304 | tf_op jit(solution)/shard_map/ppermute | solution.py:580
  214.4 19.7 %collective-permute-start.12 = (bf16[3,512,256]{2,1,0:T(8,128)(2,1)}, bf16[3,512,256]{2,1,0:T(8,128)(2,1)S(1)}, u32[]{:S(2)}, u32[]{:S(2)}) collective-permute-start(bf16[3,512,256]{2,1,0:T(8,128)(2,1)} %split.332), channel_id=1, source_target_pairs={{0,16},{8,24},{16,0},{24,8},{1,17},{9,25},{17,1},{25,9},{2,18},{10... | collective-permute-start | bytes 2359304 | tf_op jit(solution)/shard_map/ppermute | solution.py:580
  393.3 31.8 %copy-start.10 = (bf16[160,2048]{1,0:T(8,128)(2,1)S(1)}, bf16[160,2048]{1,0:T(8,128)(2,1)}, u32[]{:S(2)}) copy-start(bf16[160,2048]{1,0:T(8,128)(2,1)} %get-tuple-element.175.refs_2_) | copy-start | bytes 1966084
  465.9 183.8 %reduce-scatter.7.cloned.1.call-start = ((), (), s32[]{:S(2)}) async-start(), calls=%async_computation.9 | async-start | bytes 9437184 | tf_op jit(solution)/shard_map/reduce_scatter | solution.py:764
  491.5 313.4 %reduce-scatter.9.cloned.1.call-start = ((), (), s32[]{:S(2)}) async-start(), calls=%async_computation.10 | async-start | bytes 9437184 | tf_op jit(solution)/shard_map/reduce_scatter | solution.py:786
  596.5 300.1 %reduce-scatter.11.cloned.1.call-start = ((), (), s32[]{:S(2)}) async-start(), calls=%async_computation.11 | async-start | bytes 9437184 | tf_op jit(solution)/shard_map/reduce_scatter | solution.py:815
  630.9 19.8 %collective-permute-start.15 = (bf16[3,256,512]{2,1,0:T(8,128)(2,1)}, bf16[3,256,512]{2,1,0:T(8,128)(2,1)}, u32[]{:S(2)}, u32[]{:S(2)}) collective-permute-start(bf16[3,256,512]{2,1,0:T(8,128)(2,1)} %get-tuple-element.338), channel_id=1, source_target_pairs={{0,16},{8,24},{16,0},{24,8},{1,17},{9,25},{17,1},{25,9},{2,18},{10... | collective-permute-start | bytes 2359304 | tf_op jit(solution)/shard_map/ppermute | solution.py:580
  632.4 19.6 %collective-permute-start.14 = (bf16[3,256,512]{2,1,0:T(8,128)(2,1)}, bf16[3,256,512]{2,1,0:T(8,128)(2,1)}, u32[]{:S(2)}, u32[]{:S(2)}) collective-permute-start(bf16[3,256,512]{2,1,0:T(8,128)(2,1)} %get-tuple-element.339), channel_id=1, source_target_pairs={{0,8},{8,0},{16,24},{24,16},{1,9},{9,1},{17,25},{25,17},{2,10},{10... | collective-permute-start | bytes 2359304 | tf_op jit(solution)/shard_map/ppermute | solution.py:580
  655.1 81.5 %collective-permute-start.18 = (bf16[3,512,512]{2,1,0:T(8,128)(2,1)}, bf16[3,512,512]{2,1,0:T(8,128)(2,1)}, u32[]{:S(2)}, u32[]{:S(2)}) collective-permute-start(bf16[3,512,512]{2,1,0:T(8,128)(2,1)} %pad_maximum_fusion.6), channel_id=1, source_target_pairs={{0,8},{8,0},{16,24},{24,16},{1,9},{9,1},{17,25},{25,17},{2,10},{10... | collective-permute-start | bytes 4718600 | tf_op jit(solution)/shard_map/ppermute | solution.py:580
  658.5 78.1 %collective-permute-start.19 = (bf16[3,512,512]{2,1,0:T(8,128)(2,1)}, bf16[3,512,512]{2,1,0:T(8,128)(2,1)}, u32[]{:S(2)}, u32[]{:S(2)}) collective-permute-start(bf16[3,512,512]{2,1,0:T(8,128)(2,1)} %pad_maximum_fusion.8), channel_id=1, source_target_pairs={{0,16},{8,24},{16,0},{24,8},{1,17},{9,25},{17,1},{25,9},{2,18},{10... | collective-permute-start | bytes 4718600 | tf_op jit(solution)/shard_map/ppermute | solution.py:580
  660.5 76.1 %collective-permute-start.17 = (bf16[3,256,512]{2,1,0:T(8,128)(2,1)}, bf16[3,256,512]{2,1,0:T(8,128)(2,1)}, u32[]{:S(2)}, u32[]{:S(2)}) collective-permute-start(bf16[3,256,512]{2,1,0:T(8,128)(2,1)} %get-tuple-element.336), channel_id=1, source_target_pairs={{0,16},{8,24},{16,0},{24,8},{1,17},{9,25},{17,1},{25,9},{2,18},{10... | collective-permute-start | bytes 2359304 | tf_op jit(solution)/shard_map/ppermute | solution.py:580
  661.9 74.7 %collective-permute-start.16 = (bf16[3,256,512]{2,1,0:T(8,128)(2,1)}, bf16[3,256,512]{2,1,0:T(8,128)(2,1)}, u32[]{:S(2)}, u32[]{:S(2)}) collective-permute-start(bf16[3,256,512]{2,1,0:T(8,128)(2,1)} %get-tuple-element.337), channel_id=1, source_target_pairs={{0,8},{8,0},{16,24},{24,16},{1,9},{9,1},{17,25},{25,17},{2,10},{10... | collective-permute-start | bytes 2359304 | tf_op jit(solution)/shard_map/ppermute | solution.py:580
  738.2 38.6 %collective-permute-start.20 = (bf16[3,512,512]{2,1,0:T(8,128)(2,1)S(1)}, bf16[3,512,512]{2,1,0:T(8,128)(2,1)S(1)}, u32[]{:S(2)}, u32[]{:S(2)}) collective-permute-start(bf16[3,512,512]{2,1,0:T(8,128)(2,1)S(1)} %pad_maximum_fusion.11), channel_id=1, source_target_pairs={{0,8},{8,0},{16,24},{24,16},{1,9},{9,1},{17,25},{25,17},{2,10},{10... | collective-permute-start | bytes 4718600 | tf_op jit(solution)/shard_map/ppermute | solution.py:580
  740.4 36.4 %collective-permute-start.21 = (bf16[3,512,512]{2,1,0:T(8,128)(2,1)S(1)}, bf16[3,512,512]{2,1,0:T(8,128)(2,1)S(1)}, u32[]{:S(2)}, u32[]{:S(2)}) collective-permute-start(bf16[3,512,512]{2,1,0:T(8,128)(2,1)S(1)} %pad_maximum_fusion.13), channel_id=1, source_target_pairs={{0,16},{8,24},{16,0},{24,8},{1,17},{9,25},{17,1},{25,9},{2,18},{10... | collective-permute-start | bytes 4718600 | tf_op jit(solution)/shard_map/ppermute | solution.py:580
  817.7 17.9 %collective-permute-start.24 = (f32[36,512]{1,0:T(8,128)S(1)}, f32[36,512]{1,0:T(8,128)S(1)}, u32[]{:S(2)}, u32[]{:S(2)}) collective-permute-start(f32[36,512]{1,0:T(8,128)S(1)} %pad_maximum_fusion.32), channel_id=1, source_target_pairs={{0,24},{8,16},{16,8},{24,0},{1,25},{9,17},{17,9},{25,1},{2,26},{10... | collective-permute-start | bytes 221192 | tf_op jit(solution)/shard_map/ppermute | solution.py:580
  819.6 16.0 %collective-permute-start.23 = (f32[36,512]{1,0:T(8,128)S(1)}, f32[36,512]{1,0:T(8,128)S(1)}, u32[]{:S(2)}, u32[]{:S(2)}) collective-permute-start(f32[36,512]{1,0:T(8,128)S(1)} %pad_maximum_fusion.32), channel_id=1, source_target_pairs={{0,16},{8,24},{16,0},{24,8},{1,17},{9,25},{17,1},{25,9},{2,18},{10... | collective-permute-start | bytes 221192 | tf_op jit(solution)/shard_map/ppermute | solution.py:580
  820.7 14.9 %collective-permute-start.22 = (f32[36,512]{1,0:T(8,128)S(1)}, f32[36,512]{1,0:T(8,128)S(1)}, u32[]{:S(2)}, u32[]{:S(2)}) collective-permute-start(f32[36,512]{1,0:T(8,128)S(1)} %pad_maximum_fusion.32), channel_id=1, source_target_pairs={{0,8},{8,0},{16,24},{24,16},{1,9},{9,1},{17,25},{25,17},{2,10},{10... | collective-permute-start | bytes 221192 | tf_op jit(solution)/shard_map/ppermute | solution.py:580
  835.7 5.1 collective-permute-start.25
  840.9 4.1 collective-permute-start.26
  845.0 1.2 collective-permute-start.27
  847.0 19.7 %collective-permute-start.29 = (bf16[3,256,512]{2,1,0:T(8,128)(2,1)S(1)}, bf16[3,256,512]{2,1,0:T(8,128)(2,1)S(1)}, u32[]{:S(2)}, u32[]{:S(2)}) collective-permute-start(bf16[3,256,512]{2,1,0:T(8,128)(2,1)S(1)} %get-tuple-element.334), channel_id=1, source_target_pairs={{0,8},{8,0},{16,24},{24,16},{1,9},{9,1},{17,25},{25,17},{2,10},{10... | collective-permute-start | bytes 2359304 | tf_op jit(solution)/shard_map/ppermute | solution.py:580
  849.1 19.5 %collective-permute-start.28 = (bf16[3,256,512]{2,1,0:T(8,128)(2,1)S(1)}, bf16[3,256,512]{2,1,0:T(8,128)(2,1)S(1)}, u32[]{:S(2)}, u32[]{:S(2)}) collective-permute-start(bf16[3,256,512]{2,1,0:T(8,128)(2,1)S(1)} %get-tuple-element.335), channel_id=1, source_target_pairs={{0,16},{8,24},{16,0},{24,8},{1,17},{9,25},{17,1},{25,9},{2,18},{10... | collective-permute-start | bytes 2359304 | tf_op jit(solution)/shard_map/ppermute | solution.py:580
  871.5 12.3 %collective-permute-start.32 = (bf16[3,72,512]{2,1,0:T(8,128)(2,1)S(1)}, bf16[3,72,512]{2,1,0:T(8,128)(2,1)S(1)}, u32[]{:S(2)}, u32[]{:S(2)}) collective-permute-start(bf16[3,72,512]{2,1,0:T(8,128)(2,1)S(1)} %pad_maximum_fusion.29), channel_id=1, source_target_pairs={{0,8},{8,0},{16,24},{24,16},{1,9},{9,1},{17,25},{25,17},{2,10},{10... | collective-permute-start | bytes 663560 | tf_op jit(solution)/shard_map/ppermute | solution.py:580
  872.6 13.2 %collective-permute-start.33 = (bf16[3,72,512]{2,1,0:T(8,128)(2,1)S(1)}, bf16[3,72,512]{2,1,0:T(8,128)(2,1)S(1)}, u32[]{:S(2)}, u32[]{:S(2)}) collective-permute-start(bf16[3,72,512]{2,1,0:T(8,128)(2,1)S(1)} %pad_maximum_fusion.30), channel_id=1, source_target_pairs={{0,16},{8,24},{16,0},{24,8},{1,17},{9,25},{17,1},{25,9},{2,18},{10... | collective-permute-start | bytes 663560 | tf_op jit(solution)/shard_map/ppermute | solution.py:580
  873.7 12.1 %collective-permute-start.34 = (bf16[3,72,512]{2,1,0:T(8,128)(2,1)S(1)}, bf16[3,72,512]{2,1,0:T(8,128)(2,1)S(1)}, u32[]{:S(2)}, u32[]{:S(2)}) collective-permute-start(bf16[3,72,512]{2,1,0:T(8,128)(2,1)S(1)} %pad_maximum_fusion.31), channel_id=1, source_target_pairs={{0,24},{8,16},{16,8},{24,0},{1,25},{9,17},{17,9},{25,1},{2,26},{10... | collective-permute-start | bytes 663560 | tf_op jit(solution)/shard_map/ppermute | solution.py:580
  875.2 41.4 %collective-permute-start.30 = (bf16[3,512,512]{2,1,0:T(8,128)(2,1)}, bf16[3,512,512]{2,1,0:T(8,128)(2,1)}, u32[]{:S(2)}, u32[]{:S(2)}) collective-permute-start(bf16[3,512,512]{2,1,0:T(8,128)(2,1)} %pad_maximum_fusion.17), channel_id=1, source_target_pairs={{0,8},{8,0},{16,24},{24,16},{1,9},{9,1},{17,25},{25,17},{2,10},{10... | collective-permute-start | bytes 4718600 | tf_op jit(solution)/shard_map/ppermute | solution.py:580
  876.3 41.5 %collective-permute-start.31 = (bf16[3,512,512]{2,1,0:T(8,128)(2,1)}, bf16[3,512,512]{2,1,0:T(8,128)(2,1)}, u32[]{:S(2)}, u32[]{:S(2)}) collective-permute-start(bf16[3,512,512]{2,1,0:T(8,128)(2,1)} %pad_maximum_fusion.19), channel_id=1, source_target_pairs={{0,16},{8,24},{16,0},{24,8},{1,17},{9,25},{17,1},{25,9},{2,18},{10... | collective-permute-start | bytes 4718600 | tf_op jit(solution)/shard_map/ppermute | solution.py:580
  902.4 15.4 %copy-start.35 = (bf16[3,512,512]{2,1,0:T(8,128)(2,1)S(1)}, bf16[3,512,512]{2,1,0:T(8,128)(2,1)}, u32[]{:S(2)}) copy-start(bf16[3,512,512]{2,1,0:T(8,128)(2,1)} %pad_maximum_fusion.14) | copy-start | bytes 4718596
  904.7 15.6 %copy-start.27 = (f32[3,512,512]{2,1,0:T(8,128)S(1)}, f32[3,512,512]{2,1,0:T(8,128)}, u32[]{:S(2)}) copy-start(f32[3,512,512]{2,1,0:T(8,128)} %convert_add_fusion.3) | copy-start | bytes 9437188
  (85 other events, 234.6 us)
Sparse Core Ops, SparseCore 0:
  27.2 83.2 all-gather.4
  112.1 94.6 all-gather.10
  210.2 81.1 all-gather.8
  292.8 80.5 all-gather.6
  466.1 89.3 reduce-scatter.4
  557.6 87.9 reduce-scatter.6
  647.9 87.9 reduce-scatter.8
  805.1 91.5 reduce-scatter.10
